TPU v7x, 256 devices: a whole 4x4x8 slice. The times are simulated.
256 devices in a mesh: xi: 4 (over x), eta: 2 (over core), zeta: 32 (over z, y).
Axes of the slice: x: 4, y: 4, z: 8, core: 2. Of those that a mesh axis runs over, the one named last changes fastest.
Arguments:
- state: float32 [5, 32, 64, 4096], P(None, 'xi', 'eta', 'zeta'), may hold values from -6 to 6
- radius: float32 [32, 64, 4096], P('xi', 'eta', 'zeta'), may hold values from 0.5 to 4
- iblank: int32 [32, 64, 4096], P('xi', 'eta', 'zeta'), may hold values 0 or 1
- speeds: float32 [3, 5], replicated, may hold values from -1.5 to 1.5
- transforms: float32 [4, 5, 5], replicated, as said below
- inv_xi: float32 [5, 32, 32], P(None, 'xi')
- inv_eta: float32 [5, 64, 64], P(None, 'eta')
- inv_zeta: float32 [5, 4096, 4096], P(None, 'zeta')
Outputs:
- residual: float32 [5, 32, 64, 4096], P(None, 'xi', 'eta', 'zeta')
- advanced: float32 [5, 32, 64, 4096], P(None, 'xi', 'eta', 'zeta')
Inputs may be any that keep to these rules, and one draw needn't show every extreme that they name: transforms and line inverses are of order one with a unit diagonal part.
All inputs are finite; a program needn't handle non-finite values. No bound on the sum of `iblank` on one device may be relied on, other than what follows from the above.
Results may differ from a plain program's by a relative error of at most 0.000082.
Values sent between devices are 32-bit elements; how exact they have to be, the bound alone decides.
No kernel may reach another device: no remote copies, remote signals or barrier semaphores. Data moves between devices by JAX's collectives and lax.ppermute only.
A program may use at most 128 MiB of HBM per device.

v0:
```python
import functools

import jax
import jax.numpy as jnp
from jax import lax
from jax.experimental import pallas as pl
from jax.experimental.pallas import tpu as pltpu
from jax.sharding import PartitionSpec as P

F32 = jnp.float32
BF16 = jnp.bfloat16
SMEM = pl.BlockSpec(memory_space=pltpu.SMEM)
HBM = pl.BlockSpec(memory_space=pltpu.HBM)
VMEM = pl.BlockSpec()
NZC, NYC = 8, 4
PICKED_STEP = (2, 2, 1, 3)
PICKED_FIRST = (0, 3, 0, 0)
PICKED_COUNT = (3, 2, 5, 5)


def position():
    xi, eta, zeta = (lax.axis_index(name) for name in ("xi", "eta", "zeta"))
    return xi, eta, lax.div(zeta, 4), lax.rem(zeta, 4)


def shape(*dims, dtype=F32):
    return jax.ShapeDtypeStruct(dims, dtype)


def split(x):
    high = x.astype(BF16)
    low = (x - high.astype(F32)).astype(BF16)
    return high, low


def dot(a, b, dims):
    return lax.dot_general(a, b, (dims, ((), ())), preferred_element_type=F32)


def dot3(a, b, dims=((1,), (0,))):
    a_high, a_low = a
    b_high, b_low = b
    return dot(a_high, b_high, dims) + dot(a_high, b_low, dims) + dot(a_low, b_high, dims)


def mixed(t_ref, which, fields):
    out = []
    for a in range(5):
        total = t_ref[which, a, 0] * fields[0]
        for b in range(1, 5):
            total = total + t_ref[which, a, b] * fields[b]
        out.append(total)
    return out


def faces_kernel(state, xlo, xhi, yface, zlo, zhi):
    _, eta, _, _ = position()
    xlo[...] = state[:, 0:2]
    xhi[...] = state[:, 6:8]
    start = pl.multiple_of(24 * (1 - eta), 8)
    yface[...] = state[:, :, pl.ds(start, 8), :]
    for c in range(10):
        v, x = divmod(4 * c, 8)
        t = state[v, x : x + 4].reshape(128, 128).T
        zlo[:, 128 * c : 128 * (c + 1)] = t[0:8]
        zhi[:, 128 * c : 128 * (c + 1)] = t[120:128]


def faces(state):
    return pl.pallas_call(
        faces_kernel,
        in_specs=[VMEM],
        out_specs=[VMEM] * 5,
        out_shape=[
            shape(5, 2, 32, 128),
            shape(5, 2, 32, 128),
            shape(5, 8, 8, 128),
            shape(8, 1280),
            shape(8, 1280),
        ],
        name="faces",
    )(state)


def residual_kernel(
    speeds, t_ref, state, radius_hbm, iblank_hbm, inv_xi_hbm, xprev, xnext, yrec, zprev, znext,
    residual, m0, m1, m2, m3, ext, radius, iblank, inv_xi, zface, w0, sems,
):
    xi, eta, _, _ = position()
    copies = [
        pltpu.make_async_copy(state, ext.at[:, pl.ds(2, 8)], sems.at[0]),
        pltpu.make_async_copy(radius_hbm, radius, sems.at[1]),
        pltpu.make_async_copy(iblank_hbm, iblank, sems.at[2]),
        pltpu.make_async_copy(inv_xi_hbm, inv_xi, sems.at[3]),
    ]
    for copy in copies:
        copy.start()
    ext[:, 0:2] = xprev[...]
    ext[:, 10:12] = xnext[...]
    for c in range(10):
        v, x = divmod(4 * c, 8)
        lanes = slice(128 * c, 128 * (c + 1))
        t = jnp.concatenate([znext[:, lanes], jnp.zeros((112, 128), F32), zprev[:, lanes]], axis=0)
        zface[v, x : x + 4] = t.T.reshape(4, 32, 128)
    lane = lax.broadcasted_iota(jnp.int32, (32, 128), 1)
    row = lax.broadcasted_iota(jnp.int32, (32, 128), 0)
    has_low = eta == 1
    for copy in copies:
        copy.wait()

    def body(x, carry):
        rad = 0.04 * radius[x]
        keep = -iblank[x].astype(F32)
        fields = []
        for v in range(5):
            q = ext[v, x + 2]
            xp, xm = ext[v, x + 3], ext[v, x + 1]
            xpp, xmm = ext[v, x + 4], ext[v, x]
            face = yrec[v, x]
            lows = jnp.where(has_low, face, 0.0)
            highs = jnp.where(has_low, 0.0, face)
            l2, l1 = lows[6:7], lows[7:8]
            h1, h2 = highs[0:1], highs[1:2]
            yp = jnp.where(row == 31, h1, pltpu.roll(q, 31, 0))
            ypp = jnp.where(row == 31, h2, jnp.where(row == 30, h1, pltpu.roll(q, 30, 0)))
            ym = jnp.where(row == 0, l1, pltpu.roll(q, 1, 0))
            ymm = jnp.where(row == 0, l2, jnp.where(row == 1, l1, pltpu.roll(q, 2, 0)))
            z = zface[v, x]
            zp = pltpu.roll(jnp.where(lane == 0, z, q), 127, 1)
            zpp = pltpu.roll(jnp.where(lane < 2, z, q), 126, 1)
            zm = pltpu.roll(jnp.where(lane == 127, z, q), 1, 1)
            zmm = pltpu.roll(jnp.where(lane >= 126, z, q), 2, 1)
            flux = (
                (0.5 * speeds[0, v]) * (xp - xm)
                + (0.5 * speeds[1, v]) * (yp - ym)
                + (0.5 * speeds[2, v]) * (zp - zm)
            )
            far = (xpp + xmm) + (ypp + ymm) + (zpp + zmm)
            near = (xp + xm) + (yp + ym) + (zp + zm)
            diss = rad * (far - 4.0 * near + 18.0 * q)
            r = keep * (flux + diss)
            residual[v, x] = r
            fields.append(r)
        for v, value in enumerate(mixed(t_ref, 0, fields)):
            w0[v, x] = value
        return carry

    lax.fori_loop(0, 8, body, 0)
    for s, m in enumerate((m0, m1, m2, m3)):
        start = pl.multiple_of(8 * lax.rem(xi + s, 4), 8)
        m[:, 0:8] = w0[:, :, pl.ds(start, 8), :]
        m[:, 8] = jnp.concatenate([inv_xi[...], jnp.zeros((5, 8, 96), F32)], axis=2)


def residual_step(speeds, transforms, *arrays):
    return pl.pallas_call(
        residual_kernel,
        in_specs=[SMEM] * 2 + [HBM] * 4 + [VMEM] * 5,
        out_specs=[VMEM] * 5,
        out_shape=[shape(5, 8, 32, 128)] + [shape(5, 9, 8, 128)] * 4,
        scratch_shapes=[
            pltpu.VMEM((5, 12, 32, 128), F32),
            pltpu.VMEM((8, 32, 128), F32),
            pltpu.VMEM((8, 32, 128), jnp.int32),
            pltpu.VMEM((5, 8, 32), F32),
            pltpu.VMEM((5, 8, 32, 128), F32),
            pltpu.VMEM((5, 8, 32, 128), F32),
            pltpu.SemaphoreType.DMA((4,)),
        ],
        compiler_params=pltpu.CompilerParams(vmem_limit_bytes=16 << 20),
        name="residual",
    )(speeds, transforms, *arrays)


def xi_kernel(t_ref, r0, r1, r2, r3, b0, b1, b2, b3, field, inverse, work):
    xi, _, _, _ = position()
    for s, r in enumerate((r0, r1, r2, r3)):
        start = pl.multiple_of(8 * lax.rem(xi + 4 - s, 4), 8)
        field[:, pl.ds(start, 8)] = r[:, 0:8]
        inverse[:, pl.ds(start, 8), :] = r[:, 8]
    rows = lax.broadcasted_iota(jnp.int32, (256, 32), 0) // 8
    spread = (rows == lax.broadcasted_iota(jnp.int32, (256, 32), 1)).astype(F32).astype(BF16)
    cols = lax.broadcasted_iota(jnp.int32, (128, 256), 1) // 8
    widen = (cols == lax.broadcasted_iota(jnp.int32, (128, 256), 0)).astype(F32).astype(BF16)
    same = (
        lax.broadcasted_iota(jnp.int32, (256, 256), 0) % 8
        == lax.broadcasted_iota(jnp.int32, (256, 256), 1) % 8
    )
    for v in range(5):
        line = []
        for part in split(inverse[v]):
            wide = dot(part, widen, ((1,), (0,))).astype(BF16)
            full = dot(spread, wide, ((1,), (0,)))
            line.append(jnp.where(same, full, 0.0).astype(BF16))
        value = dot3(line, split(field[v].reshape(256, 128)))
        work[v] = value.reshape(32, 8, 128)

    def body(x, carry):
        for v, value in enumerate(mixed(t_ref, 1, [work[v, x] for v in range(5)])):
            field[v, x] = value
        return carry

    lax.fori_loop(0, 32, body, 0)
    for s, b in enumerate((b0, b1, b2, b3)):
        b[...] = field[:, pl.ds(8 * lax.rem(xi + s, 4), 8)]


def xi_step(transforms, parts):
    return pl.pallas_call(
        xi_kernel,
        in_specs=[SMEM] + [VMEM] * 4,
        out_specs=[VMEM] * 4,
        out_shape=[shape(5, 8, 8, 128)] * 4,
        scratch_shapes=[
            pltpu.VMEM((5, 32, 8, 128), F32),
            pltpu.VMEM((5, 32, 128), F32),
            pltpu.VMEM((5, 32, 8, 128), F32),
        ],
        compiler_params=pltpu.CompilerParams(vmem_limit_bytes=16 << 20),
        name="xi_lines",
    )(transforms, *parts)


def eta_kernel(t_ref, inv_eta, p0, p1, p2, p3, q0, q1, q2, q3, out, field, work):
    xi, eta, _, _ = position()
    for s, (p, q) in enumerate(zip((p0, p1, p2, p3), (q0, q1, q2, q3))):
        rows = 8 * lax.rem(xi + 4 - s, 4)
        field[:, :, pl.ds(pl.multiple_of(32 * eta + rows, 8), 8), :] = p[...]
        field[:, :, pl.ds(pl.multiple_of(32 * (1 - eta) + rows, 8), 8), :] = q[...]
    for v in range(5):
        wide = jnp.concatenate([field[v, x] for x in range(8)], axis=1)
        value = dot3(split(inv_eta[v]), split(wide))
        for x in range(8):
            work[v, x] = value[:, 128 * x : 128 * (x + 1)]


    def body(x, carry):
        for v, value in enumerate(mixed(t_ref, 2, [work[v, x] for v in range(5)])):
            out[v, x] = value
        return carry

    lax.fori_loop(0, 8, body, 0)


def eta_step(transforms, inv_eta, own, other):
    return pl.pallas_call(
        eta_kernel,
        in_specs=[SMEM] + [VMEM] * 9,
        out_specs=VMEM,
        out_shape=shape(5, 8, 32, 128),
        scratch_shapes=[pltpu.VMEM((5, 8, 64, 128), F32), pltpu.VMEM((5, 8, 32, 128), F32)],
        compiler_params=pltpu.CompilerParams(vmem_limit_bytes=16 << 20),
        name="eta_lines",
    )(transforms, inv_eta, *own, *other)


def pick_kernel(inv, *refs):
    _, eta, _, y = position()
    *outs, lines, sems = refs
    rows = pl.ds(pl.multiple_of(64 * eta, 64), 64)
    copies = [
        pltpu.make_async_copy(inv.at[v, rows], lines.at[v], sems.at[v]) for v in range(5)
    ]
    for copy in copies:
        copy.start()
    for v, copy in enumerate(copies):
        copy.wait()
        for s, first, count, g in zip(PICKED_STEP, PICKED_FIRST, PICKED_COUNT, outs):
            if first <= v < first + count:
                for z in range(NZC):
                    lanes = pl.multiple_of(512 * z + 128 * lax.rem(y + s, 4), 128)
                    g[z, v - first] = lines[v, :, pl.ds(lanes, 128)]


def pick(inv_zeta):
    return pl.pallas_call(
        pick_kernel,
        in_specs=[HBM],
        out_specs=[VMEM] * 4,
        out_shape=[shape(NZC, count, 64, 128) for count in PICKED_COUNT],
        scratch_shapes=[pltpu.VMEM((5, 64, 4096), F32), pltpu.SemaphoreType.DMA((5,))],
        compiler_params=pltpu.CompilerParams(vmem_limit_bytes=56 << 20),
        name="pick",
    )(inv_zeta)


def own_kernel(inv, high, low):
    _, _, _, y = position()
    for z in range(NZC):
        block = inv[0, :, pl.ds(pl.multiple_of(512 * z + 128 * y, 128), 128)]
        rows = slice(128 * z, 128 * (z + 1))
        high[0, rows], low[0, rows] = split(block.T)


def prepare_own(inv_zeta):
    return pl.pallas_call(
        own_kernel,
        grid=(5,),
        in_specs=[pl.BlockSpec((1, 128, 4096), lambda v: (v, 0, 0))],
        out_specs=[pl.BlockSpec((1, 1024, 128), lambda v: (v, 0, 0))] * 2,
        out_shape=[shape(5, 1024, 128, dtype=BF16)] * 2,
        compiler_params=pltpu.CompilerParams(vmem_limit_bytes=24 << 20),
        name="prepare_own",
    )(inv_zeta)


def prepare_kernel(*refs):
    _, eta, _, _ = position()
    own_parts, other_parts, (high2, low2, high, low, lines) = refs[:4], refs[4:8], refs[8:]
    v = pl.program_id(0)

    def place(index, own, other):
        for half, part in ((eta, own), (1 - eta, other)):
            rows = pl.ds(pl.multiple_of(64 * half, 64), 64)
            for z in range(NZC):
                lines[PICKED_STEP[index] - 1, rows, 128 * z : 128 * (z + 1)] = part[z, 0]

    for index, (own, other) in enumerate(zip(own_parts, other_parts)):
        first, count = PICKED_FIRST[index], PICKED_COUNT[index]
        if count == 5:
            place(index, own, other)
        else:
            held = jnp.logical_and(v >= first, v < first + count)
            pl.when(held)(functools.partial(place, index, own, other))
    for z in range(NZC):
        rows = slice(128 * z, 128 * (z + 1))
        high2[0, rows], low2[0, rows] = split(lines[1, :, rows].T)
        for c in range(2):
            lanes = slice(128 * c, 128 * (c + 1))
            high[0, rows, lanes], low[0, rows, lanes] = split(lines[2 * c, :, rows].T)


def prepare(own_parts, other_parts):
    widths = (128, 128, 256, 256)

    def part(first, count):
        return pl.BlockSpec(
            (NZC, 1, 64, 128), lambda v: (0, jnp.clip(v - first, 0, count - 1), 0, 0)
        )

    parts = [part(*pair) for pair in zip(PICKED_FIRST, PICKED_COUNT)]
    return pl.pallas_call(
        prepare_kernel,
        grid=(5,),
        in_specs=parts * 2,
        out_specs=[pl.BlockSpec((1, 1024, w), lambda v: (v, 0, 0)) for w in widths],
        out_shape=[shape(5, 1024, w, dtype=BF16) for w in widths],
        scratch_shapes=[pltpu.VMEM((3, 128, 1024), F32)],
        compiler_params=pltpu.CompilerParams(vmem_limit_bytes=24 << 20),
        name="prepare",
    )(*own_parts, *other_parts)


def zeta_kernel(count, b_ref, *refs):
    b = split(jnp.concatenate([b_ref[z, 0].reshape(256, 128) for z in range(NZC)], axis=1))
    outs = list(refs[2 * count :])
    for high, low in zip(refs[0 : 2 * count : 2], refs[1 : 2 * count : 2]):
        value = dot3(b, (high[0], low[0]))
        for place in range(high.shape[2] // 128):
            lanes = slice(128 * place, 128 * (place + 1))
            outs.pop(0)[0] = value[:128, lanes]
            outs.pop(0)[0] = value[128:, lanes]


def zeta_step(gathered, *lines):
    widths = [array.shape[2] for array in lines]
    count = sum(widths) // 128
    return pl.pallas_call(
        functools.partial(zeta_kernel, len(lines) // 2),
        grid=(5,),
        in_specs=[pl.BlockSpec((NZC, 1, 8, 32, 128), lambda v: (0, v, 0, 0, 0))]
        + [pl.BlockSpec((1, 1024, w), lambda v: (v, 0, 0)) for w in widths],
        out_specs=[pl.BlockSpec((1, 128, 128), lambda v: (v, 0, 0))] * count,
        out_shape=[shape(5, 128, 128)] * count,
        compiler_params=pltpu.CompilerParams(vmem_limit_bytes=48 << 20),
        name="zeta_lines",
    )(gathered, *lines)


def final_kernel(t_ref, state, own0, own1, low0, low1, high0, high1, out):
    for half, parts in enumerate(((own0, low0, high0), (own1, low1, high1))):

        def body(x, carry):
            rows = pl.ds(pl.multiple_of(32 * x, 32), 32)
            fields = [sum(part[v, rows] for part in parts) for v in range(5)]
            for v, value in enumerate(mixed(t_ref, 3, fields)):
                out[v, 4 * half + x] = state[v, 4 * half + x] + value
            return carry

        lax.fori_loop(0, 4, body, 0)


def final_step(transforms, state, parts):
    return pl.pallas_call(
        final_kernel,
        in_specs=[SMEM] + [VMEM] * 7,
        out_specs=VMEM,
        out_shape=shape(5, 8, 32, 128),
        compiler_params=pltpu.CompilerParams(vmem_limit_bytes=56 << 20),
        name="final",
    )(transforms, state, *parts)


def over_x(array, s):
    return lax.ppermute(array, "xi", [(i, (i + s) % 4) for i in range(4)])


def over_y(array, s):
    pairs = [(4 * z + y, 4 * z + (y + s) % 4) for z in range(NZC) for y in range(NYC)]
    return lax.ppermute(array, "zeta", pairs)


def over_core(array):
    return lax.ppermute(array, "eta", [(0, 1), (1, 0)])


def shift_line(array, axis, s):
    size = lax.axis_size(axis)
    pairs = [(i, i + s) for i in range(size) if 0 <= i + s < size]
    return lax.ppermute(array, axis, pairs)


def after(array, *first):
    return lax.optimization_barrier((array, *first))[0]


def local(state, radius, iblank, speeds, transforms, inv_xi, inv_eta, inv_zeta):
    xlo, xhi, yface, zlo, zhi = faces(state)
    halos = [
        shift_line(xhi, "xi", 1),
        shift_line(xlo, "xi", -1),
        over_core(yface),
        shift_line(zhi, "zeta", 1),
        shift_line(zlo, "zeta", -1),
    ]
    picked = pick(inv_zeta)
    halos[0] = after(halos[0], picked[0])
    residual, m0, m1, m2, m3 = residual_step(
        speeds, transforms, state, radius, iblank, inv_xi, *halos
    )
    parts = [m0] + [over_x(m, s + 1) for s, m in enumerate((m1, m2, m3))]
    sent = [over_y(after(picked[0], m0), PICKED_STEP[0])]
    b0, b1, b2, b3 = xi_step(transforms, parts)
    own = [b0] + [over_x(b, s + 1) for s, b in enumerate((b1, b2, b3))]
    other = [over_core(p) for p in own]
    own[0] = after(own[0], *sent)
    work = eta_step(transforms, inv_eta, own, other)

    columns = [[4 * z + y for z in range(NZC)] for y in range(NYC)]
    gathered = lax.all_gather(work, "zeta", axis_index_groups=columns)
    sent += [over_y(after(picked[i], work), PICKED_STEP[i]) for i in range(1, 4)]
    own_lines = prepare_own(after(inv_zeta, work))
    swapped = [over_core(after(part, *own_lines)) for part in sent]
    high2, low2, high, low = prepare(sent, swapped)

    far0, far1 = zeta_step(gathered, high2, low2)
    far0, far1 = over_y(far0, 1), over_y(far1, -1)
    down0, down1, up0, up1, own0, own1 = zeta_step(gathered, high, low, *own_lines)
    up1, down0 = over_y(up1, 1), over_y(down0, -1)
    up0, down1 = over_y(up0 + far0, 1), over_y(down1 + far1, -1)
    advanced = final_step(transforms, state, (own0, own1, up0, up1, down0, down1))
    return residual, advanced


def solution(mesh):
    placed = (
        P(None, "xi", "eta", "zeta"),
        P("xi", "eta", "zeta"),
        P("xi", "eta", "zeta"),
        P(),
        P(),
        P(None, "xi", None),
        P(None, "eta", None),
        P(None, "zeta", None),
    )
    return jax.shard_map(
        local,
        mesh=mesh,
        in_specs=placed,
        out_specs=(P(None, "xi", "eta", "zeta"), P(None, "xi", "eta", "zeta")),
        check_vma=False,
    )
```

profile of v0, /device:TPU:24, one launch (start us, length us, event | category | flops | bytes accessed | tf_op | source)
XLA Modules:
  0.0 178.6 jit_solution(13687650661974567712)
XLA Ops:
  7.2 2.0 %faces.1 = (f32[5,2,32,128]{3,2,1,0:T(8,128)}, f32[5,2,32,128]{3,2,1,0:T(8,128)}, f32[5,8,8,128]{3,2,1,0:T(8,128)}, f32[8,1280]{1,0:T(8,128)}, f32[8,1280]{1,0:T(8,128)}) custom-call(f32[5,8,32,128]{3,2,1,0:T(8,128)} %state.5), custom_call_target="tpu_custom_call" | custom-call | tf_op jit(solution)/shard_map/faces/pallas_call | solution.py:70
  9.2 3.4 %collective-permute-start = (f32[5,2,32,128]{3,2,1,0:T(8,128)}, f32[5,2,32,128]{3,2,1,0:T(8,128)S(1)}, u32[]{:S(2)}, u32[]{:S(2)}) collective-permute-start(f32[5,2,32,128]{3,2,1,0:T(8,128)} %get-tuple-element.45), channel_id=1, source_target_pairs={{0,64},{64,128},{128,192},{1,65},{65,129},{129,193},{2,66},{66,130... | collective-permute-start | bytes 491528 | tf_op jit(solution)/shard_map/ppermute | solution.py:420
  12.6 1.3 collective-permute-start.1
  14.0 3.5 %collective-permute-start.3 = (f32[8,1280]{1,0:T(8,128)}, f32[8,1280]{1,0:T(8,128)S(1)}, u32[]{:S(2)}, u32[]{:S(2)}) collective-permute-start(f32[8,1280]{1,0:T(8,128)} %get-tuple-element.50), channel_id=1, source_target_pairs={{0,1},{1,2},{2,3},{3,4},{4,5},{5,6},{6,7},{7,8},{8,9},{9,10},{10,1... | collective-permute-start | bytes 122888 | tf_op jit(solution)/shard_map/ppermute | solution.py:420
  17.6 2.5 %collective-permute-start.4 = (f32[8,1280]{1,0:T(8,128)}, f32[8,1280]{1,0:T(8,128)S(1)}, u32[]{:S(2)}, u32[]{:S(2)}) collective-permute-start(f32[8,1280]{1,0:T(8,128)} %get-tuple-element.51), channel_id=1, source_target_pairs={{1,0},{2,1},{3,2},{4,3},{5,4},{6,5},{7,6},{8,7},{9,8},{10,9},{11,1... | collective-permute-start | bytes 122888 | tf_op jit(solution)/shard_map/ppermute | solution.py:420
  20.1 4.5 %pick.1 = (f32[8,3,64,128]{3,2,1,0:T(8,128)}, f32[8,2,64,128]{3,2,1,0:T(8,128)}, f32[8,5,64,128]{3,2,1,0:T(8,128)}, f32[8,5,64,128]{3,2,1,0:T(8,128)}) custom-call(f32[5,128,4096]{2,1,0:T(8,128)} %inv.2), custom_call_target="tpu_custom_call" | custom-call | tf_op jit(solution)/shard_map/pick/pallas_call | solution.py:276
  24.6 1.3 collective-permute-done.4.znext
  26.0 3.8 %residual.1 = (f32[5,8,32,128]{3,2,1,0:T(8,128)}, f32[5,9,8,128]{3,2,1,0:T(8,128)S(1)}, f32[5,9,8,128]{3,2,1,0:T(8,128)S(1)}, f32[5,9,8,128]{3,2,1,0:T(8,128)S(1)}, f32[5,9,8,128]{3,2,1,0:T(8,128)S(1)}) custom-call(f32[3,5]{1,0:T(4,128)S(1)} %copy-done.15, f32[4,5,5]{2,1,0:T(8,128)S(1)} %copy.14.t_ref, f32[5,8,32,128]{3,2,1,0:T(8,128)S(1)} %copy-done.1, ...), custom_call_target="tpu_custom_call" | custom-call | tf_op jit(solution)/shard_map/residual/pallas_call | solution.py:156
  29.9 2.7 %collective-permute-start.5 = (f32[5,9,8,128]{3,2,1,0:T(8,128)S(1)}, f32[5,9,8,128]{3,2,1,0:T(8,128)S(1)}, u32[]{:S(2)}, u32[]{:S(2)}) collective-permute-start(f32[5,9,8,128]{3,2,1,0:T(8,128)S(1)} %get-tuple-element.54), channel_id=1, source_target_pairs={{0,64},{64,128},{128,192},{192,0},{1,65},{65,129},{129,193},{193,1... | collective-permute-start | bytes 552968 | tf_op jit(solution)/shard_map/ppermute | solution.py:405
  32.6 2.7 %collective-permute-start.6 = (f32[5,9,8,128]{3,2,1,0:T(8,128)S(1)}, f32[5,9,8,128]{3,2,1,0:T(8,128)S(1)}, u32[]{:S(2)}, u32[]{:S(2)}) collective-permute-start(f32[5,9,8,128]{3,2,1,0:T(8,128)S(1)} %get-tuple-element.55), channel_id=1, source_target_pairs={{0,128},{64,192},{128,0},{192,64},{1,129},{65,193},{129,1},{193,65... | collective-permute-start | bytes 552968 | tf_op jit(solution)/shard_map/ppermute | solution.py:405
  35.4 1.4 collective-permute-start.7
  36.8 1.7 collective-permute-done.5.r1
  38.5 4.8 %collective-permute-done.6.r2 = f32[5,9,8,128]{3,2,1,0:T(8,128)S(1)} collective-permute-done((f32[5,9,8,128]{3,2,1,0:T(8,128)S(1)}, f32[5,9,8,128]{3,2,1,0:T(8,128)S(1)}, u32[]{:S(2)}, u32[]{:S(2)}) %collective-permute-start.6) | collective-permute-done | bytes 184352 | tf_op jit(solution)/shard_map/ppermute | solution.py:405
  43.4 3.3 %xi_lines.1 = (f32[5,8,8,128]{3,2,1,0:T(8,128)S(1)}, f32[5,8,8,128]{3,2,1,0:T(8,128)S(1)}, f32[5,8,8,128]{3,2,1,0:T(8,128)S(1)}, f32[5,8,8,128]{3,2,1,0:T(8,128)S(1)}) custom-call(f32[4,5,5]{2,1,0:T(8,128)S(1)} %copy.14.t_ref, f32[5,9,8,128]{3,2,1,0:T(8,128)S(1)} %get-tuple-element.53.r0, f32[5,9,8,128]{3,2,1,0:T(8,128)S(1)} %collective-permute-done.5.r1, ...), custom_call_target="tpu_custom_call" | custom-call | tf_op jit(solution)/shard_map/xi_lines/pallas_call | solution.py:209
  46.7 1.2 collective-permute-start.9
  47.9 2.4 %collective-permute-start.10 = (f32[5,8,8,128]{3,2,1,0:T(8,128)S(1)}, f32[5,8,8,128]{3,2,1,0:T(8,128)S(1)}, u32[]{:S(2)}, u32[]{:S(2)}) collective-permute-start(f32[5,8,8,128]{3,2,1,0:T(8,128)S(1)} %get-tuple-element.61), channel_id=1, source_target_pairs={{0,128},{64,192},{128,0},{192,64},{1,129},{65,193},{129,1},{193,65... | collective-permute-start | bytes 491528 | tf_op jit(solution)/shard_map/ppermute | solution.py:405
  50.3 1.8 collective-permute-start.11
  52.1 2.8 %collective-permute-done.9.p1 = f32[5,8,8,128]{3,2,1,0:T(8,128)S(1)} collective-permute-done((f32[5,8,8,128]{3,2,1,0:T(8,128)S(1)}, f32[5,8,8,128]{3,2,1,0:T(8,128)S(1)}, u32[]{:S(2)}, u32[]{:S(2)}) %collective-permute-start.9) | collective-permute-done | bytes 163872 | tf_op jit(solution)/shard_map/ppermute | solution.py:405
  54.8 2.3 %collective-permute-done.10.p2 = f32[5,8,8,128]{3,2,1,0:T(8,128)S(1)} collective-permute-done((f32[5,8,8,128]{3,2,1,0:T(8,128)S(1)}, f32[5,8,8,128]{3,2,1,0:T(8,128)S(1)}, u32[]{:S(2)}, u32[]{:S(2)}) %collective-permute-start.10) | collective-permute-done | bytes 163872 | tf_op jit(solution)/shard_map/ppermute | solution.py:405
  57.6 0.9 collective-permute-done.14.q2
  58.7 2.5 %eta_lines.1 = f32[5,8,32,128]{3,2,1,0:T(8,128)} custom-call(f32[4,5,5]{2,1,0:T(8,128)S(1)} %copy.14.t_ref, f32[5,32,64]{2,1,0:T(8,128)S(1)} %copy-done.13, f32[5,8,8,128]{3,2,1,0:T(8,128)S(1)} %get-tuple-element.59.p0, f32[5,8,8,128]{3,2,1,0:T(8,128)S(1)} %collective-permute-done.9.p1, f32[5,8,8,128]{3,2,1,0:T(8,128)S(1)} %collective-permute-done.10.p2, ...), custom_call_target="tpu_custom_call" | custom-call | tf_op jit(solution)/shard_map/eta_lines/pallas_call | solution.py:246
  61.9 2.7 %collective-permute-start.17 = (f32[8,5,64,128]{3,2,1,0:T(8,128)}, f32[8,5,64,128]{3,2,1,0:T(8,128)S(1)}, u32[]{:S(2)}, u32[]{:S(2)}) collective-permute-start(f32[8,5,64,128]{3,2,1,0:T(8,128)} %get-tuple-element.66), channel_id=1, source_target_pairs={{0,1},{1,2},{2,3},{3,0},{4,5},{5,6},{6,7},{7,4},{8,9},{9,10},{10,1... | collective-permute-start | bytes 3932168 | tf_op jit(solution)/shard_map/ppermute | solution.py:410
  64.6 4.0 %copy-done = f32[5,128,4096]{2,1,0:T(8,128)S(1)} copy-done((f32[5,128,4096]{2,1,0:T(8,128)S(1)}, f32[5,128,4096]{2,1,0:T(8,128)}, u32[]{:S(2)}) %copy-start) | copy-done | bytes 10485784
  68.6 1.1 prepare_own.1
  69.7 24.1 %collective-permute-done.18.refs_3_ = f32[8,5,64,128]{3,2,1,0:T(8,128)S(1)} collective-permute-done((f32[8,5,64,128]{3,2,1,0:T(8,128)}, f32[8,5,64,128]{3,2,1,0:T(8,128)S(1)}, u32[]{:S(2)}, u32[]{:S(2)}) %collective-permute-start.18) | collective-permute-done | bytes 1310752 | tf_op jit(solution)/shard_map/ppermute | solution.py:410
  94.3 1.8 %collective-permute-start.16 = (f32[8,2,64,128]{3,2,1,0:T(8,128)S(1)}, f32[8,2,64,128]{3,2,1,0:T(8,128)S(1)}, u32[]{:S(2)}, u32[]{:S(2)}) collective-permute-start(f32[8,2,64,128]{3,2,1,0:T(8,128)S(1)} %copy-done.22), channel_id=1, source_target_pairs={{0,2},{1,3},{2,0},{3,1},{4,6},{5,7},{6,4},{7,5},{8,10},{9,11},{10,... | collective-permute-start | bytes 1572872 | tf_op jit(solution)/shard_map/ppermute | solution.py:410
  96.3 13.4 %collective-permute-done.16.refs_1_ = f32[8,2,64,128]{3,2,1,0:T(8,128)S(1)} collective-permute-done((f32[8,2,64,128]{3,2,1,0:T(8,128)S(1)}, f32[8,2,64,128]{3,2,1,0:T(8,128)S(1)}, u32[]{:S(2)}, u32[]{:S(2)}) %collective-permute-start.16) | collective-permute-done | bytes 524320 | tf_op jit(solution)/shard_map/ppermute | solution.py:410
  109.7 1.9 %collective-permute-done.20.refs_5_ = f32[8,2,64,128]{3,2,1,0:T(8,128)S(1)} collective-permute-done((f32[8,2,64,128]{3,2,1,0:T(8,128)S(1)}, f32[8,2,64,128]{3,2,1,0:T(8,128)S(1)}, u32[]{:S(2)}, u32[]{:S(2)}) %collective-permute-start.20) | collective-permute-done | bytes 524320 | tf_op jit(solution)/shard_map/ppermute | solution.py:414
  111.6 4.8 %prepare.1 = (bf16[5,1024,128]{2,1,0:T(8,128)(2,1)S(1)}, bf16[5,1024,128]{2,1,0:T(8,128)(2,1)S(1)}, bf16[5,1024,256]{2,1,0:T(8,128)(2,1)S(1)}, bf16[5,1024,256]{2,1,0:T(8,128)(2,1)S(1)}) custom-call(f32[8,3,64,128]{3,2,1,0:T(8,128)S(1)} %collective-permute-done.8.refs_0_, f32[8,2,64,128]{3,2,1,0:T(8,128)S(1)} %collective-permute-done.16.refs_1_, ...), custom_call_target="tpu_custom_call" | custom-call | tf_op jit(solution)/shard_map/prepare/pallas_call | solution.py:342
  116.5 1.5 copy-done.2
  118.0 1.6 copy-done.3
  119.6 1.1 copy-done.4
  120.6 1.1 copy-done.6
  121.7 8.7 %all-gather.3.cloned.1.call-done = f32[40,8,32,128]{3,2,1,0:T(8,128)} async-done(((f32[5,8,32,128]{3,2,1,0:T(8,128)}), f32[40,8,32,128]{3,2,1,0:T(8,128)}) %all-gather.3.cloned.1.call-update) | async-done | bytes 5242896 | tf_op jit(solution)/shard_map/all_gather | solution.py:450
  130.5 1.3 copy-done.5
  131.8 1.3 copy-done.7
  133.1 5.5 %zeta_lines.3 = (f32[5,128,128]{2,1,0:T(8,128)S(1)}, f32[5,128,128]{2,1,0:T(8,128)S(1)}) custom-call(f32[8,5,8,32,128]{4,3,2,1,0:T(8,128)} %bitcast.1, bf16[5,1024,128]{2,1,0:T(8,128)(2,1)S(1)} %copy-done.5, bf16[5,1024,128]{2,1,0:T(8,128)(2,1)S(1)} %copy-done.7), custom_call_target="tpu_custom_call" | custom-call | tf_op jit(solution)/shard_map/zeta_lines/pallas_call | solution.py:368
  138.5 0.9 collective-permute-start.27
  139.5 2.4 %collective-permute-start.23 = (f32[5,128,128]{2,1,0:T(8,128)S(1)}, f32[5,128,128]{2,1,0:T(8,128)S(1)}, u32[]{:S(2)}, u32[]{:S(2)}) collective-permute-start(f32[5,128,128]{2,1,0:T(8,128)S(1)} %get-tuple-element.83), channel_id=1, source_target_pairs={{0,1},{1,2},{2,3},{3,0},{4,5},{5,6},{6,7},{7,4},{8,9},{9,10},{10,1... | collective-permute-start | bytes 983048 | tf_op jit(solution)/shard_map/ppermute | solution.py:410
  141.9 7.6 %zeta_lines.2 = (f32[5,128,128]{2,1,0:T(8,128)S(1)}, f32[5,128,128]{2,1,0:T(8,128)S(1)}, f32[5,128,128]{2,1,0:T(8,128)S(1)}, f32[5,128,128]{2,1,0:T(8,128)S(1)},...) custom-call(f32[8,5,8,32,128]{4,3,2,1,0:T(8,128)} %bitcast.2, bf16[5,1024,256]{2,1,0:T(8,128)(2,1)} %copy-done.2, ...), custom_call_target="tpu_custom_call" | custom-call | tf_op jit(solution)/shard_map/zeta_lines/pallas_call | solution.py:368
  149.4 0.7 copy-done.9
  150.2 0.7 copy-done.10
  150.9 2.0 %collective-permute-start.26 = (f32[5,128,128]{2,1,0:T(8,128)S(1)}, f32[5,128,128]{2,1,0:T(8,128)S(1)}, u32[]{:S(2)}, u32[]{:S(2)}) collective-permute-start(f32[5,128,128]{2,1,0:T(8,128)S(1)} %get-tuple-element.85), channel_id=1, source_target_pairs={{0,3},{1,0},{2,1},{3,2},{4,7},{5,4},{6,5},{7,6},{8,11},{9,8},{10,9... | collective-permute-start | bytes 983048 | tf_op jit(solution)/shard_map/ppermute | solution.py:410
  153.1 3.3 %collective-permute-start.24 = (f32[5,128,128]{2,1,0:T(8,128)S(1)}, f32[5,128,128]{2,1,0:T(8,128)S(1)}, u32[]{:S(2)}, u32[]{:S(2)}) collective-permute-start(f32[5,128,128]{2,1,0:T(8,128)S(1)} %add.6), channel_id=1, source_target_pairs={{0,1},{1,2},{2,3},{3,0},{4,5},{5,6},{6,7},{7,4},{8,9},{9,10},{10,1... | collective-permute-start | bytes 983048 | tf_op jit(solution)/shard_map/ppermute | solution.py:410
  156.4 5.1 %collective-permute-done.25.low1 = f32[5,128,128]{2,1,0:T(8,128)S(1)} collective-permute-done((f32[5,128,128]{2,1,0:T(8,128)S(1)}, f32[5,128,128]{2,1,0:T(8,128)S(1)}, u32[]{:S(2)}, u32[]{:S(2)}) %collective-permute-start.25) | collective-permute-done | bytes 327712 | tf_op jit(solution)/shard_map/ppermute | solution.py:410
  161.5 1.2 collective-permute-done.26.high0
  162.8 5.3 %collective-permute-done.28.high1 = f32[5,128,128]{2,1,0:T(8,128)S(1)} collective-permute-done((f32[5,128,128]{2,1,0:T(8,128)S(1)}, f32[5,128,128]{2,1,0:T(8,128)S(1)}, u32[]{:S(2)}, u32[]{:S(2)}) %collective-permute-start.28) | collective-permute-done | bytes 327712 | tf_op jit(solution)/shard_map/ppermute | solution.py:410
  168.9 2.9 %final.1 = f32[5,8,32,128]{3,2,1,0:T(8,128)} custom-call(f32[4,5,5]{2,1,0:T(8,128)} %copy-done.8, f32[5,8,32,128]{3,2,1,0:T(8,128)} %state.5, f32[5,128,128]{2,1,0:T(8,128)} %copy-done.9, f32[5,128,128]{2,1,0:T(8,128)} %copy-done.10, f32[5,128,128]{2,1,0:T(8,128)} %copy-done.19, f32[5,128,128]{2,1,0:T(8,128)} %copy-done.16, f32[5,128,128]{2,1,0:T(8,128)} %copy-done.17, ...), custom_call_target="tpu_custom_call" | custom-call | tf_op jit(solution)/shard_map/final/pallas_call | solution.py:394
  (72 shorter events, 3.5 us)
Async XLA Ops:
  7.2 123.3 %all-gather.3.cloned.1.call-start = ((), (), s32[]{:S(2)}) async-start(), calls=%async_computation | async-start | bytes 5898240 | tf_op jit(solution)/shard_map/all_gather | solution.py:450
  9.2 15.4 %collective-permute-start = (f32[5,2,32,128]{3,2,1,0:T(8,128)}, f32[5,2,32,128]{3,2,1,0:T(8,128)S(1)}, u32[]{:S(2)}, u32[]{:S(2)}) collective-permute-start(f32[5,2,32,128]{3,2,1,0:T(8,128)} %get-tuple-element.45), channel_id=1, source_target_pairs={{0,64},{64,128},{128,192},{1,65},{65,129},{129,193},{2,66},{66,130... | collective-permute-start | bytes 491528 | tf_op jit(solution)/shard_map/ppermute | solution.py:420
  12.6 13.3 %collective-permute-start.1 = (f32[5,2,32,128]{3,2,1,0:T(8,128)}, f32[5,2,32,128]{3,2,1,0:T(8,128)S(1)}, u32[]{:S(2)}, u32[]{:S(2)}) collective-permute-start(f32[5,2,32,128]{3,2,1,0:T(8,128)} %get-tuple-element.48), channel_id=1, source_target_pairs={{64,0},{128,64},{192,128},{65,1},{129,65},{193,129},{66,2},{130,66... | collective-permute-start | bytes 491528 | tf_op jit(solution)/shard_map/ppermute | solution.py:420
  13.9 12.0 %collective-permute-start.2 = (f32[5,8,8,128]{3,2,1,0:T(8,128)}, f32[5,8,8,128]{3,2,1,0:T(8,128)S(1)}, u32[]{:S(2)}, u32[]{:S(2)}) collective-permute-start(f32[5,8,8,128]{3,2,1,0:T(8,128)} %get-tuple-element.49), channel_id=1, source_target_pairs={{0,32},{32,0},{1,33},{33,1},{2,34},{34,2},{3,35},{35,3},{4,36},{36... | collective-permute-start | bytes 491528 | tf_op jit(solution)/shard_map/ppermute | solution.py:414
  14.0 10.6 %collective-permute-start.3 = (f32[8,1280]{1,0:T(8,128)}, f32[8,1280]{1,0:T(8,128)S(1)}, u32[]{:S(2)}, u32[]{:S(2)}) collective-permute-start(f32[8,1280]{1,0:T(8,128)} %get-tuple-element.50), channel_id=1, source_target_pairs={{0,1},{1,2},{2,3},{3,4},{4,5},{5,6},{6,7},{7,8},{8,9},{9,10},{10,1... | collective-permute-start | bytes 122888 | tf_op jit(solution)/shard_map/ppermute | solution.py:420
  17.5 7.1 %copy-start.20 = (f32[4,5,5]{2,0,1:T(4,128)S(1)}, f32[4,5,5]{2,0,1:T(4,128)}, u32[]{:S(2)}) copy-start(f32[4,5,5]{2,0,1:T(4,128)} %param.12) | copy-start | bytes 1204
  17.5 8.4 %copy-start.1 = (f32[5,8,32,128]{3,2,1,0:T(8,128)S(1)}, f32[5,8,32,128]{3,2,1,0:T(8,128)}, u32[]{:S(2)}) copy-start(f32[5,8,32,128]{3,2,1,0:T(8,128)} %state.5) | copy-start | bytes 1966084
  17.5 8.4 %copy-start.11 = (f32[8,32,128]{2,1,0:T(8,128)S(1)}, f32[8,32,128]{2,1,0:T(8,128)}, u32[]{:S(2)}) copy-start(f32[8,32,128]{2,1,0:T(8,128)} %radius_hbm.1) | copy-start | bytes 393220
  17.5 8.4 %copy-start.12 = (s32[8,32,128]{2,1,0:T(8,128)S(1)}, s32[8,32,128]{2,1,0:T(8,128)}, u32[]{:S(2)}) copy-start(s32[8,32,128]{2,1,0:T(8,128)} %iblank_hbm.1) | copy-start | bytes 393220
  17.5 8.4 %copy-start.14 = (f32[5,8,32]{2,1,0:T(8,128)S(1)}, f32[5,8,32]{2,1,0:T(8,128)}, u32[]{:S(2)}) copy-start(f32[5,8,32]{2,1,0:T(8,128)} %inv_xi_hbm.1) | copy-start | bytes 15364
  17.6 8.4 %copy-start.15 = (f32[3,5]{1,0:T(4,128)S(1)}, f32[3,5]{1,0:T(4,128)}, u32[]{:S(2)}) copy-start(f32[3,5]{1,0:T(4,128)} %speeds.1) | copy-start | bytes 184
  17.6 8.3 %collective-permute-start.4 = (f32[8,1280]{1,0:T(8,128)}, f32[8,1280]{1,0:T(8,128)S(1)}, u32[]{:S(2)}, u32[]{:S(2)}) collective-permute-start(f32[8,1280]{1,0:T(8,128)} %get-tuple-element.51), channel_id=1, source_target_pairs={{1,0},{2,1},{3,2},{4,3},{5,4},{6,5},{7,6},{8,7},{9,8},{10,9},{11,1... | collective-permute-start | bytes 122888 | tf_op jit(solution)/shard_map/ppermute | solution.py:420
  24.6 5.2 %copy-start.21 = (f32[8,3,64,128]{3,2,1,0:T(8,128)S(1)}, f32[8,3,64,128]{3,2,1,0:T(8,128)}, u32[]{:S(2)}) copy-start(f32[8,3,64,128]{3,2,1,0:T(8,128)} %get-tuple-element.58) | copy-start | bytes 2359300
  24.6 34.2 %copy-start.13 = (f32[5,32,64]{2,1,0:T(8,128)S(1)}, f32[5,32,64]{2,1,0:T(8,128)}, u32[]{:S(2)}) copy-start(f32[5,32,64]{2,1,0:T(8,128)} %inv_eta.1) | copy-start | bytes 122884
  24.6 36.7 %copy-start.8 = (f32[4,5,5]{2,1,0:T(8,128)}, f32[4,5,5]{2,1,0:T(8,128)S(1)}, u32[]{:S(2)}) copy-start(f32[4,5,5]{2,1,0:T(8,128)S(1)} %copy.14.t_ref) | copy-start | bytes 1204
  29.8 27.8 %collective-permute-start.8 = (f32[8,3,64,128]{3,2,1,0:T(8,128)S(1)}, f32[8,3,64,128]{3,2,1,0:T(8,128)S(1)}, u32[]{:S(2)}, u32[]{:S(2)}) collective-permute-start(f32[8,3,64,128]{3,2,1,0:T(8,128)S(1)} %copy-done.21), channel_id=1, source_target_pairs={{0,2},{1,3},{2,0},{3,1},{4,6},{5,7},{6,4},{7,5},{8,10},{9,11},{10,... | collective-permute-start | bytes 2359304 | tf_op jit(solution)/shard_map/ppermute | solution.py:410
  29.9 8.6 %collective-permute-start.5 = (f32[5,9,8,128]{3,2,1,0:T(8,128)S(1)}, f32[5,9,8,128]{3,2,1,0:T(8,128)S(1)}, u32[]{:S(2)}, u32[]{:S(2)}) collective-permute-start(f32[5,9,8,128]{3,2,1,0:T(8,128)S(1)} %get-tuple-element.54), channel_id=1, source_target_pairs={{0,64},{64,128},{128,192},{192,0},{1,65},{65,129},{129,193},{193,1... | collective-permute-start | bytes 552968 | tf_op jit(solution)/shard_map/ppermute | solution.py:405
  32.6 10.7 %collective-permute-start.6 = (f32[5,9,8,128]{3,2,1,0:T(8,128)S(1)}, f32[5,9,8,128]{3,2,1,0:T(8,128)S(1)}, u32[]{:S(2)}, u32[]{:S(2)}) collective-permute-start(f32[5,9,8,128]{3,2,1,0:T(8,128)S(1)} %get-tuple-element.55), channel_id=1, source_target_pairs={{0,128},{64,192},{128,0},{192,64},{1,129},{65,193},{129,1},{193,65... | collective-permute-start | bytes 552968 | tf_op jit(solution)/shard_map/ppermute | solution.py:405
  35.4 8.0 %collective-permute-start.7 = (f32[5,9,8,128]{3,2,1,0:T(8,128)S(1)}, f32[5,9,8,128]{3,2,1,0:T(8,128)S(1)}, u32[]{:S(2)}, u32[]{:S(2)}) collective-permute-start(f32[5,9,8,128]{3,2,1,0:T(8,128)S(1)} %get-tuple-element.56), channel_id=1, source_target_pairs={{0,192},{64,0},{128,64},{192,128},{1,193},{65,1},{129,65},{193,129... | collective-permute-start | bytes 552968 | tf_op jit(solution)/shard_map/ppermute | solution.py:405
  46.7 8.1 %collective-permute-start.9 = (f32[5,8,8,128]{3,2,1,0:T(8,128)S(1)}, f32[5,8,8,128]{3,2,1,0:T(8,128)S(1)}, u32[]{:S(2)}, u32[]{:S(2)}) collective-permute-start(f32[5,8,8,128]{3,2,1,0:T(8,128)S(1)} %get-tuple-element.60), channel_id=1, source_target_pairs={{0,64},{64,128},{128,192},{192,0},{1,65},{65,129},{129,193},{193,1... | collective-permute-start | bytes 491528 | tf_op jit(solution)/shard_map/ppermute | solution.py:405
  47.9 9.2 %collective-permute-start.10 = (f32[5,8,8,128]{3,2,1,0:T(8,128)S(1)}, f32[5,8,8,128]{3,2,1,0:T(8,128)S(1)}, u32[]{:S(2)}, u32[]{:S(2)}) collective-permute-start(f32[5,8,8,128]{3,2,1,0:T(8,128)S(1)} %get-tuple-element.61), channel_id=1, source_target_pairs={{0,128},{64,192},{128,0},{192,64},{1,129},{65,193},{129,1},{193,65... | collective-permute-start | bytes 491528 | tf_op jit(solution)/shard_map/ppermute | solution.py:405
  50.3 6.8 %collective-permute-start.11 = (f32[5,8,8,128]{3,2,1,0:T(8,128)S(1)}, f32[5,8,8,128]{3,2,1,0:T(8,128)S(1)}, u32[]{:S(2)}, u32[]{:S(2)}) collective-permute-start(f32[5,8,8,128]{3,2,1,0:T(8,128)S(1)} %get-tuple-element.62), channel_id=1, source_target_pairs={{0,192},{64,0},{128,64},{192,128},{1,193},{65,1},{129,65},{193,129... | collective-permute-start | bytes 491528 | tf_op jit(solution)/shard_map/ppermute | solution.py:405
  52.1 5.6 %collective-permute-start.12 = (f32[5,8,8,128]{3,2,1,0:T(8,128)S(1)}, f32[5,8,8,128]{3,2,1,0:T(8,128)S(1)}, u32[]{:S(2)}, u32[]{:S(2)}) collective-permute-start(f32[5,8,8,128]{3,2,1,0:T(8,128)S(1)} %get-tuple-element.59.p0), channel_id=1, source_target_pairs={{0,32},{32,0},{1,33},{33,1},{2,34},{34,2},{3,35},{35,3},{4,36},{36... | collective-permute-start | bytes 491528 | tf_op jit(solution)/shard_map/ppermute | solution.py:414
  54.8 2.8 %collective-permute-start.13 = (f32[5,8,8,128]{3,2,1,0:T(8,128)S(1)}, f32[5,8,8,128]{3,2,1,0:T(8,128)S(1)}, u32[]{:S(2)}, u32[]{:S(2)}) collective-permute-start(f32[5,8,8,128]{3,2,1,0:T(8,128)S(1)} %collective-permute-done.9.p1), channel_id=1, source_target_pairs={{0,32},{32,0},{1,33},{33,1},{2,34},{34,2},{3,35},{35,3},{4,36},{36... | collective-permute-start | bytes 491528 | tf_op jit(solution)/shard_map/ppermute | solution.py:414
  57.1 1.4 collective-permute-start.14
  57.1 1.6 collective-permute-start.15
  61.3 32.5 %collective-permute-start.18 = (f32[8,5,64,128]{3,2,1,0:T(8,128)}, f32[8,5,64,128]{3,2,1,0:T(8,128)S(1)}, u32[]{:S(2)}, u32[]{:S(2)}) collective-permute-start(f32[8,5,64,128]{3,2,1,0:T(8,128)} %get-tuple-element.68), channel_id=1, source_target_pairs={{0,3},{1,0},{2,1},{3,2},{4,7},{5,4},{6,5},{7,6},{8,11},{9,8},{10,9... | collective-permute-start | bytes 3932168 | tf_op jit(solution)/shard_map/ppermute | solution.py:410
  61.9 31.8 %collective-permute-start.17 = (f32[8,5,64,128]{3,2,1,0:T(8,128)}, f32[8,5,64,128]{3,2,1,0:T(8,128)S(1)}, u32[]{:S(2)}, u32[]{:S(2)}) collective-permute-start(f32[8,5,64,128]{3,2,1,0:T(8,128)} %get-tuple-element.66), channel_id=1, source_target_pairs={{0,1},{1,2},{2,3},{3,0},{4,5},{5,6},{6,7},{7,4},{8,9},{9,10},{10,1... | collective-permute-start | bytes 3932168 | tf_op jit(solution)/shard_map/ppermute | solution.py:410
  64.6 4.0 %copy-start = (f32[5,128,4096]{2,1,0:T(8,128)S(1)}, f32[5,128,4096]{2,1,0:T(8,128)}, u32[]{:S(2)}) copy-start(f32[5,128,4096]{2,1,0:T(8,128)} %inv.2) | copy-start | bytes 31457284
  68.6 25.7 %copy-start.22 = (f32[8,2,64,128]{3,2,1,0:T(8,128)S(1)}, f32[8,2,64,128]{3,2,1,0:T(8,128)}, u32[]{:S(2)}) copy-start(f32[8,2,64,128]{3,2,1,0:T(8,128)} %get-tuple-element.64) | copy-start | bytes 1572868
  93.8 17.9 %collective-permute-start.22 = (f32[8,5,64,128]{3,2,1,0:T(8,128)S(1)}, f32[8,5,64,128]{3,2,1,0:T(8,128)S(1)}, u32[]{:S(2)}, u32[]{:S(2)}) collective-permute-start(f32[8,5,64,128]{3,2,1,0:T(8,128)S(1)} %collective-permute-done.18.refs_3_), channel_id=1, source_target_pairs={{0,32},{32,0},{1,33},{33,1},{2,34},{34,2},{3,35},{35,3},{4,36},{36... | collective-permute-start | bytes 3932168 | tf_op jit(solution)/shard_map/ppermute | solution.py:414
  93.8 17.9 %collective-permute-start.21 = (f32[8,5,64,128]{3,2,1,0:T(8,128)S(1)}, f32[8,5,64,128]{3,2,1,0:T(8,128)S(1)}, u32[]{:S(2)}, u32[]{:S(2)}) collective-permute-start(f32[8,5,64,128]{3,2,1,0:T(8,128)S(1)} %collective-permute-done.17.refs_2_), channel_id=1, source_target_pairs={{0,32},{32,0},{1,33},{33,1},{2,34},{34,2},{3,35},{35,3},{4,36},{36... | collective-permute-start | bytes 3932168 | tf_op jit(solution)/shard_map/ppermute | solution.py:414
  94.3 15.4 %collective-permute-start.16 = (f32[8,2,64,128]{3,2,1,0:T(8,128)S(1)}, f32[8,2,64,128]{3,2,1,0:T(8,128)S(1)}, u32[]{:S(2)}, u32[]{:S(2)}) collective-permute-start(f32[8,2,64,128]{3,2,1,0:T(8,128)S(1)} %copy-done.22), channel_id=1, source_target_pairs={{0,2},{1,3},{2,0},{3,1},{4,6},{5,7},{6,4},{7,5},{8,10},{9,11},{10,... | collective-permute-start | bytes 1572872 | tf_op jit(solution)/shard_map/ppermute | solution.py:410
  96.1 13.6 %collective-permute-start.19 = (f32[8,3,64,128]{3,2,1,0:T(8,128)S(1)}, f32[8,3,64,128]{3,2,1,0:T(8,128)S(1)}, u32[]{:S(2)}, u32[]{:S(2)}) collective-permute-start(f32[8,3,64,128]{3,2,1,0:T(8,128)S(1)} %collective-permute-done.8.refs_0_), channel_id=1, source_target_pairs={{0,32},{32,0},{1,33},{33,1},{2,34},{34,2},{3,35},{35,3},{4,36},{36... | collective-permute-start | bytes 2359304 | tf_op jit(solution)/shard_map/ppermute | solution.py:414
  109.7 1.9 %collective-permute-start.20 = (f32[8,2,64,128]{3,2,1,0:T(8,128)S(1)}, f32[8,2,64,128]{3,2,1,0:T(8,128)S(1)}, u32[]{:S(2)}, u32[]{:S(2)}) collective-permute-start(f32[8,2,64,128]{3,2,1,0:T(8,128)S(1)} %collective-permute-done.16.refs_1_), channel_id=1, source_target_pairs={{0,32},{32,0},{1,33},{33,1},{2,34},{34,2},{3,35},{35,3},{4,36},{36... | collective-permute-start | bytes 1572872 | tf_op jit(solution)/shard_map/ppermute | solution.py:414
  116.4 1.6 copy-start.2
  118.0 1.6 copy-start.3
  120.6 1.1 copy-start.6
  130.5 1.3 copy-start.5
  131.8 1.3 copy-start.7
  138.5 14.4 %collective-permute-start.27 = (f32[5,128,128]{2,1,0:T(8,128)S(1)}, f32[5,128,128]{2,1,0:T(8,128)S(1)}, u32[]{:S(2)}, u32[]{:S(2)}) collective-permute-start(f32[5,128,128]{2,1,0:T(8,128)S(1)} %get-tuple-element.87), channel_id=1, source_target_pairs={{0,3},{1,0},{2,1},{3,2},{4,7},{5,4},{6,5},{7,6},{8,11},{9,8},{10,9... | collective-permute-start | bytes 983048 | tf_op jit(solution)/shard_map/ppermute | solution.py:410
  139.5 13.6 %collective-permute-start.23 = (f32[5,128,128]{2,1,0:T(8,128)S(1)}, f32[5,128,128]{2,1,0:T(8,128)S(1)}, u32[]{:S(2)}, u32[]{:S(2)}) collective-permute-start(f32[5,128,128]{2,1,0:T(8,128)S(1)} %get-tuple-element.83), channel_id=1, source_target_pairs={{0,1},{1,2},{2,3},{3,0},{4,5},{5,6},{6,7},{7,4},{8,9},{9,10},{10,1... | collective-permute-start | bytes 983048 | tf_op jit(solution)/shard_map/ppermute | solution.py:410
  150.9 10.6 %collective-permute-start.25 = (f32[5,128,128]{2,1,0:T(8,128)S(1)}, f32[5,128,128]{2,1,0:T(8,128)S(1)}, u32[]{:S(2)}, u32[]{:S(2)}) collective-permute-start(f32[5,128,128]{2,1,0:T(8,128)S(1)} %get-tuple-element.84), channel_id=1, source_target_pairs={{0,1},{1,2},{2,3},{3,0},{4,5},{5,6},{6,7},{7,4},{8,9},{9,10},{10,1... | collective-permute-start | bytes 983048 | tf_op jit(solution)/shard_map/ppermute | solution.py:410
  150.9 11.9 %collective-permute-start.26 = (f32[5,128,128]{2,1,0:T(8,128)S(1)}, f32[5,128,128]{2,1,0:T(8,128)S(1)}, u32[]{:S(2)}, u32[]{:S(2)}) collective-permute-start(f32[5,128,128]{2,1,0:T(8,128)S(1)} %get-tuple-element.85), channel_id=1, source_target_pairs={{0,3},{1,0},{2,1},{3,2},{4,7},{5,4},{6,5},{7,6},{8,11},{9,8},{10,9... | collective-permute-start | bytes 983048 | tf_op jit(solution)/shard_map/ppermute | solution.py:410
  153.0 15.1 %collective-permute-start.28 = (f32[5,128,128]{2,1,0:T(8,128)S(1)}, f32[5,128,128]{2,1,0:T(8,128)S(1)}, u32[]{:S(2)}, u32[]{:S(2)}) collective-permute-start(f32[5,128,128]{2,1,0:T(8,128)S(1)} %add.7), channel_id=1, source_target_pairs={{0,3},{1,0},{2,1},{3,2},{4,7},{5,4},{6,5},{7,6},{8,11},{9,8},{10,9... | collective-permute-start | bytes 983048 | tf_op jit(solution)/shard_map/ppermute | solution.py:410
  153.1 14.9 %collective-permute-start.24 = (f32[5,128,128]{2,1,0:T(8,128)S(1)}, f32[5,128,128]{2,1,0:T(8,128)S(1)}, u32[]{:S(2)}, u32[]{:S(2)}) collective-permute-start(f32[5,128,128]{2,1,0:T(8,128)S(1)} %add.6), channel_id=1, source_target_pairs={{0,1},{1,2},{2,3},{3,0},{4,5},{5,6},{6,7},{7,4},{8,9},{9,10},{10,1... | collective-permute-start | bytes 983048 | tf_op jit(solution)/shard_map/ppermute | solution.py:410
  161.5 6.5 %copy-start.16 = (f32[5,128,128]{2,1,0:T(8,128)}, f32[5,128,128]{2,1,0:T(8,128)S(1)}, u32[]{:S(2)}) copy-start(f32[5,128,128]{2,1,0:T(8,128)S(1)} %collective-permute-done.25.low1) | copy-start | bytes 983044
  162.8 5.3 %copy-start.17 = (f32[5,128,128]{2,1,0:T(8,128)}, f32[5,128,128]{2,1,0:T(8,128)S(1)}, u32[]{:S(2)}) copy-start(f32[5,128,128]{2,1,0:T(8,128)S(1)} %collective-permute-done.26.high0) | copy-start | bytes 983044
  (5 other events, 4.1 us)
Sparse Core Ops, SparseCore 0:
  61.4 68.9 all-gather.2
where the time goes:
time: 179 us
  waiting for transfers between devices  73.7 us (41%)
  starting transfers between devices  38.2 us (21%)
  Pallas kernels  37.9 us (21%)
  between operations  14.4 us (8%)
  local copies, waits for them, and re-layouts  14.3 us (8%)
    ppermute x10, waiting for transfers between devices, over_y(): return lax.ppermute(array, 'zeta', pairs)  49.1 us
    unnamed x47, local copies, waits for them, and re-layouts  14.3 us
    ppermute x10, starting transfers between devices, over_y(): return lax.ppermute(array, 'zeta', pairs)  13.9 us
    pallas_call x2, Pallas kernels, zeta_step(): pl.pallas_call(functools.partial(zeta_kernel, len(lines) // 2), grid=(5,)...  13 us
    ppermute x6, starting transfers between devices, over_x(): return lax.ppermute(array, 'xi', [(i, (i + s) % 4) for i in range(4)])  12.2 us
    ppermute x6, waiting for transfers between devices, over_x(): return lax.ppermute(array, 'xi', [(i, (i + s) % 4) for i in range(4)])  11.6 us
    ppermute x4, starting transfers between devices, shift_line(): return lax.ppermute(array, axis, pairs)  10.7 us
    all_gather x1, waiting for transfers between devices, local(): gathered = lax.all_gather(work, 'zeta', axis_index_groups=columns)  8.71 us
  transfers between devices with their start and end apart: 30, of which 14 were waited for; matrix products, arithmetic and copies ran while one was open for 0% of the time, Pallas kernels for 12%

commit v1 on v0

--- a/solution.py
+++ b/solution.py
@@ -284,26 +284,6 @@
     )(inv_zeta)
 
 
-def own_kernel(inv, high, low):
-    _, _, _, y = position()
-    for z in range(NZC):
-        block = inv[0, :, pl.ds(pl.multiple_of(512 * z + 128 * y, 128), 128)]
-        rows = slice(128 * z, 128 * (z + 1))
-        high[0, rows], low[0, rows] = split(block.T)
-
-
-def prepare_own(inv_zeta):
-    return pl.pallas_call(
-        own_kernel,
-        grid=(5,),
-        in_specs=[pl.BlockSpec((1, 128, 4096), lambda v: (v, 0, 0))],
-        out_specs=[pl.BlockSpec((1, 1024, 128), lambda v: (v, 0, 0))] * 2,
-        out_shape=[shape(5, 1024, 128, dtype=BF16)] * 2,
-        compiler_params=pltpu.CompilerParams(vmem_limit_bytes=24 << 20),
-        name="prepare_own",
-    )(inv_zeta)
-
-
 def prepare_kernel(*refs):
     _, eta, _, _ = position()
     own_parts, other_parts, (high2, low2, high, low, lines) = refs[:4], refs[4:8], refs[8:]
@@ -372,9 +352,34 @@
         + [pl.BlockSpec((1, 1024, w), lambda v: (v, 0, 0)) for w in widths],
         out_specs=[pl.BlockSpec((1, 128, 128), lambda v: (v, 0, 0))] * count,
         out_shape=[shape(5, 128, 128)] * count,
-        compiler_params=pltpu.CompilerParams(vmem_limit_bytes=48 << 20),
+        compiler_params=pltpu.CompilerParams(vmem_limit_bytes=56 << 20),
         name="zeta_lines",
     )(gathered, *lines)
+
+
+def own_kernel(b_ref, inv, out0, out1):
+    _, _, _, y = position()
+    b = split(jnp.concatenate([b_ref[z, 0].reshape(256, 128) for z in range(NZC)], axis=1))
+    lanes = [pl.multiple_of(512 * z + 128 * y, 128) for z in range(NZC)]
+    lines = jnp.concatenate([inv[0, :, pl.ds(lane, 128)] for lane in lanes], axis=1)
+    value = dot3(b, split(lines), ((1,), (1,)))
+    out0[0] = value[:128]
+    out1[0] = value[128:]
+
+
+def own_step(gathered, inv_zeta):
+    return pl.pallas_call(
+        own_kernel,
+        grid=(5,),
+        in_specs=[
+            pl.BlockSpec((NZC, 1, 8, 32, 128), lambda v: (0, v, 0, 0, 0)),
+            pl.BlockSpec((1, 128, 4096), lambda v: (v, 0, 0)),
+        ],
+        out_specs=[pl.BlockSpec((1, 128, 128), lambda v: (v, 0, 0))] * 2,
+        out_shape=[shape(5, 128, 128)] * 2,
+        compiler_params=pltpu.CompilerParams(vmem_limit_bytes=24 << 20),
+        name="own_lines",
+    )(gathered, inv_zeta)
 
 
 def final_kernel(t_ref, state, own0, own1, low0, low1, high0, high1, out):
@@ -396,7 +401,7 @@
         in_specs=[SMEM] + [VMEM] * 7,
         out_specs=VMEM,
         out_shape=shape(5, 8, 32, 128),
-        compiler_params=pltpu.CompilerParams(vmem_limit_bytes=56 << 20),
+        compiler_params=pltpu.CompilerParams(vmem_limit_bytes=16 << 20),
         name="final",
     )(transforms, state, *parts)
 
@@ -449,13 +454,13 @@
     columns = [[4 * z + y for z in range(NZC)] for y in range(NYC)]
     gathered = lax.all_gather(work, "zeta", axis_index_groups=columns)
     sent += [over_y(after(picked[i], work), PICKED_STEP[i]) for i in range(1, 4)]
-    own_lines = prepare_own(after(inv_zeta, work))
-    swapped = [over_core(after(part, *own_lines)) for part in sent]
+    swapped = [over_core(after(part, work)) for part in sent]
     high2, low2, high, low = prepare(sent, swapped)
 
     far0, far1 = zeta_step(gathered, high2, low2)
     far0, far1 = over_y(far0, 1), over_y(far1, -1)
-    down0, down1, up0, up1, own0, own1 = zeta_step(gathered, high, low, *own_lines)
+    down0, down1, up0, up1 = zeta_step(gathered, high, low)
+    own0, own1 = own_step(gathered, after(inv_zeta, down0, up1))
     up1, down0 = over_y(up1, 1), over_y(down0, -1)
     up0, down1 = over_y(up0 + far0, 1), over_y(down1 + far1, -1)
     advanced = final_step(transforms, state, (own0, own1, up0, up1, down0, down1))

time: 179 us -> 175 us (0.978)
  local copies, waits for them, and re-layouts: 14.3 us -> 9.38 us
  waiting for transfers between devices: 73.7 us -> 69.9 us
  Pallas kernels: 37.9 us -> 40.9 us
  other arithmetic: 0.07 us -> 2.02 us
    unnamed x47 -> x35, local copies, waits for them, and re-layouts: 14.3 us -> 9.38 us
    ppermute x10, waiting for transfers between devices: 49.1 us -> 45.3 us  [over_y(): return lax.ppermute(array, 'zeta', pairs)]
    pallas_call x1, Pallas kernels: 1.11 us -> 3.42 us  [own_step(): pl.pallas_call(own_kernel, grid=(5,), in_specs=[pl.BlockSpec((NZC, 1, 8,...]
    add x2, other arithmetic: 0.07 us -> 2.02 us  [local(): up0, down1 = (over_y(up0 + far0, 1), over_y(down1 + far1, -1))]
  transfers between devices with their start and end apart: 30 -> 30, of which waited for: 14 -> 12; matrix products, arithmetic and copies ran while one was open for 0% -> 1% of each run, Pallas kernels for 12% -> 14%
where the time goes in v1:
time: 175 us
  waiting for transfers between devices  69.9 us (40%)
  Pallas kernels  40.9 us (23%)
  starting transfers between devices  38 us (22%)
  between operations  14.3 us (8%)
  local copies, waits for them, and re-layouts  9.38 us (5%)
  other arithmetic  2.02 us (1%)
    ppermute x10, waiting for transfers between devices, over_y(): return lax.ppermute(array, 'zeta', pairs)  45.3 us
    pallas_call x2, Pallas kernels, zeta_step(): pl.pallas_call(functools.partial(zeta_kernel, len(lines) // 2), grid=(5,)...  14.5 us
    ppermute x10, starting transfers between devices, over_y(): return lax.ppermute(array, 'zeta', pairs)  13.7 us
    ppermute x6, starting transfers between devices, over_x(): return lax.ppermute(array, 'xi', [(i, (i + s) % 4) for i in range(4)])  12.2 us
    ppermute x6, waiting for transfers between devices, over_x(): return lax.ppermute(array, 'xi', [(i, (i + s) % 4) for i in range(4)])  11.6 us
    ppermute x4, starting transfers between devices, shift_line(): return lax.ppermute(array, axis, pairs)  10.7 us
    unnamed x35, local copies, waits for them, and re-layouts  9.38 us
    all_gather x1, waiting for transfers between devices, local(): gathered = lax.all_gather(work, 'zeta', axis_index_groups=columns)  8.69 us
  transfers between devices with their start and end apart: 30, of which 12 were waited for; matrix products, arithmetic and copies ran while one was open for 1% of the time, Pallas kernels for 14%

profile of v1, /device:TPU:24, one launch (start us, length us, event | category | flops | bytes accessed | tf_op | source)
XLA Modules:
  0.0 174.5 jit_solution(4071909680909202133)
XLA Ops:
  7.2 2.0 %faces.1 = (f32[5,2,32,128]{3,2,1,0:T(8,128)}, f32[5,2,32,128]{3,2,1,0:T(8,128)}, f32[5,8,8,128]{3,2,1,0:T(8,128)}, f32[8,1280]{1,0:T(8,128)}, f32[8,1280]{1,0:T(8,128)}) custom-call(f32[5,8,32,128]{3,2,1,0:T(8,128)} %state.5), custom_call_target="tpu_custom_call" | custom-call | tf_op jit(solution)/shard_map/faces/pallas_call | solution.py:70
  9.2 3.4 %collective-permute-start = (f32[5,2,32,128]{3,2,1,0:T(8,128)}, f32[5,2,32,128]{3,2,1,0:T(8,128)S(1)}, u32[]{:S(2)}, u32[]{:S(2)}) collective-permute-start(f32[5,2,32,128]{3,2,1,0:T(8,128)} %get-tuple-element.43), channel_id=1, source_target_pairs={{0,64},{64,128},{128,192},{1,65},{65,129},{129,193},{2,66},{66,130... | collective-permute-start | bytes 491528 | tf_op jit(solution)/shard_map/ppermute | solution.py:425
  12.6 1.3 collective-permute-start.1
  14.0 3.5 %collective-permute-start.3 = (f32[8,1280]{1,0:T(8,128)}, f32[8,1280]{1,0:T(8,128)S(1)}, u32[]{:S(2)}, u32[]{:S(2)}) collective-permute-start(f32[8,1280]{1,0:T(8,128)} %get-tuple-element.48), channel_id=1, source_target_pairs={{0,1},{1,2},{2,3},{3,4},{4,5},{5,6},{6,7},{7,8},{8,9},{9,10},{10,1... | collective-permute-start | bytes 122888 | tf_op jit(solution)/shard_map/ppermute | solution.py:425
  17.6 2.5 %collective-permute-start.4 = (f32[8,1280]{1,0:T(8,128)}, f32[8,1280]{1,0:T(8,128)S(1)}, u32[]{:S(2)}, u32[]{:S(2)}) collective-permute-start(f32[8,1280]{1,0:T(8,128)} %get-tuple-element.49), channel_id=1, source_target_pairs={{1,0},{2,1},{3,2},{4,3},{5,4},{6,5},{7,6},{8,7},{9,8},{10,9},{11,1... | collective-permute-start | bytes 122888 | tf_op jit(solution)/shard_map/ppermute | solution.py:425
  20.1 4.5 %pick.1 = (f32[8,3,64,128]{3,2,1,0:T(8,128)}, f32[8,2,64,128]{3,2,1,0:T(8,128)}, f32[8,5,64,128]{3,2,1,0:T(8,128)}, f32[8,5,64,128]{3,2,1,0:T(8,128)}) custom-call(f32[5,128,4096]{2,1,0:T(8,128)} %inv.2), custom_call_target="tpu_custom_call" | custom-call | tf_op jit(solution)/shard_map/pick/pallas_call | solution.py:276
  24.6 1.3 collective-permute-done.4.znext
  26.0 3.8 %residual.1 = (f32[5,8,32,128]{3,2,1,0:T(8,128)}, f32[5,9,8,128]{3,2,1,0:T(8,128)S(1)}, f32[5,9,8,128]{3,2,1,0:T(8,128)S(1)}, f32[5,9,8,128]{3,2,1,0:T(8,128)S(1)}, f32[5,9,8,128]{3,2,1,0:T(8,128)S(1)}) custom-call(f32[3,5]{1,0:T(4,128)S(1)} %copy-done.10, f32[4,5,5]{2,1,0:T(8,128)S(1)} %copy.14.t_ref, f32[5,8,32,128]{3,2,1,0:T(8,128)S(1)} %copy-done.1, ...), custom_call_target="tpu_custom_call" | custom-call | tf_op jit(solution)/shard_map/residual/pallas_call | solution.py:156
  29.9 2.7 %collective-permute-start.5 = (f32[5,9,8,128]{3,2,1,0:T(8,128)S(1)}, f32[5,9,8,128]{3,2,1,0:T(8,128)S(1)}, u32[]{:S(2)}, u32[]{:S(2)}) collective-permute-start(f32[5,9,8,128]{3,2,1,0:T(8,128)S(1)} %get-tuple-element.52), channel_id=1, source_target_pairs={{0,64},{64,128},{128,192},{192,0},{1,65},{65,129},{129,193},{193,1... | collective-permute-start | bytes 552968 | tf_op jit(solution)/shard_map/ppermute | solution.py:410
  32.6 2.7 %collective-permute-start.6 = (f32[5,9,8,128]{3,2,1,0:T(8,128)S(1)}, f32[5,9,8,128]{3,2,1,0:T(8,128)S(1)}, u32[]{:S(2)}, u32[]{:S(2)}) collective-permute-start(f32[5,9,8,128]{3,2,1,0:T(8,128)S(1)} %get-tuple-element.53), channel_id=1, source_target_pairs={{0,128},{64,192},{128,0},{192,64},{1,129},{65,193},{129,1},{193,65... | collective-permute-start | bytes 552968 | tf_op jit(solution)/shard_map/ppermute | solution.py:410
  35.4 1.4 collective-permute-start.7
  36.8 1.8 %collective-permute-done.5.r1 = f32[5,9,8,128]{3,2,1,0:T(8,128)S(1)} collective-permute-done((f32[5,9,8,128]{3,2,1,0:T(8,128)S(1)}, f32[5,9,8,128]{3,2,1,0:T(8,128)S(1)}, u32[]{:S(2)}, u32[]{:S(2)}) %collective-permute-start.5) | collective-permute-done | bytes 184352 | tf_op jit(solution)/shard_map/ppermute | solution.py:410
  38.5 4.8 %collective-permute-done.6.r2 = f32[5,9,8,128]{3,2,1,0:T(8,128)S(1)} collective-permute-done((f32[5,9,8,128]{3,2,1,0:T(8,128)S(1)}, f32[5,9,8,128]{3,2,1,0:T(8,128)S(1)}, u32[]{:S(2)}, u32[]{:S(2)}) %collective-permute-start.6) | collective-permute-done | bytes 184352 | tf_op jit(solution)/shard_map/ppermute | solution.py:410
  43.4 3.3 %xi_lines.1 = (f32[5,8,8,128]{3,2,1,0:T(8,128)S(1)}, f32[5,8,8,128]{3,2,1,0:T(8,128)S(1)}, f32[5,8,8,128]{3,2,1,0:T(8,128)S(1)}, f32[5,8,8,128]{3,2,1,0:T(8,128)S(1)}) custom-call(f32[4,5,5]{2,1,0:T(8,128)S(1)} %copy.14.t_ref, f32[5,9,8,128]{3,2,1,0:T(8,128)S(1)} %get-tuple-element.51.r0, f32[5,9,8,128]{3,2,1,0:T(8,128)S(1)} %collective-permute-done.5.r1, ...), custom_call_target="tpu_custom_call" | custom-call | tf_op jit(solution)/shard_map/xi_lines/pallas_call | solution.py:209
  46.7 1.2 collective-permute-start.9
  47.9 2.4 %collective-permute-start.10 = (f32[5,8,8,128]{3,2,1,0:T(8,128)S(1)}, f32[5,8,8,128]{3,2,1,0:T(8,128)S(1)}, u32[]{:S(2)}, u32[]{:S(2)}) collective-permute-start(f32[5,8,8,128]{3,2,1,0:T(8,128)S(1)} %get-tuple-element.59), channel_id=1, source_target_pairs={{0,128},{64,192},{128,0},{192,64},{1,129},{65,193},{129,1},{193,65... | collective-permute-start | bytes 491528 | tf_op jit(solution)/shard_map/ppermute | solution.py:410
  50.3 1.8 %collective-permute-start.11 = (f32[5,8,8,128]{3,2,1,0:T(8,128)S(1)}, f32[5,8,8,128]{3,2,1,0:T(8,128)S(1)}, u32[]{:S(2)}, u32[]{:S(2)}) collective-permute-start(f32[5,8,8,128]{3,2,1,0:T(8,128)S(1)} %get-tuple-element.60), channel_id=1, source_target_pairs={{0,192},{64,0},{128,64},{192,128},{1,193},{65,1},{129,65},{193,129... | collective-permute-start | bytes 491528 | tf_op jit(solution)/shard_map/ppermute | solution.py:410
  52.1 2.8 %collective-permute-done.9.p1 = f32[5,8,8,128]{3,2,1,0:T(8,128)S(1)} collective-permute-done((f32[5,8,8,128]{3,2,1,0:T(8,128)S(1)}, f32[5,8,8,128]{3,2,1,0:T(8,128)S(1)}, u32[]{:S(2)}, u32[]{:S(2)}) %collective-permute-start.9) | collective-permute-done | bytes 163872 | tf_op jit(solution)/shard_map/ppermute | solution.py:410
  54.8 2.3 %collective-permute-done.10.p2 = f32[5,8,8,128]{3,2,1,0:T(8,128)S(1)} collective-permute-done((f32[5,8,8,128]{3,2,1,0:T(8,128)S(1)}, f32[5,8,8,128]{3,2,1,0:T(8,128)S(1)}, u32[]{:S(2)}, u32[]{:S(2)}) %collective-permute-start.10) | collective-permute-done | bytes 163872 | tf_op jit(solution)/shard_map/ppermute | solution.py:410
  57.1 0.5 collective-permute-start.15
  57.6 0.9 collective-permute-done.14.q2
  58.5 0.2 collective-permute-done.15.q3
  58.7 2.5 %eta_lines.1 = f32[5,8,32,128]{3,2,1,0:T(8,128)} custom-call(f32[4,5,5]{2,1,0:T(8,128)S(1)} %copy.14.t_ref, f32[5,32,64]{2,1,0:T(8,128)S(1)} %copy-done.8, f32[5,8,8,128]{3,2,1,0:T(8,128)S(1)} %get-tuple-element.57.p0, f32[5,8,8,128]{3,2,1,0:T(8,128)S(1)} %collective-permute-done.9.p1, f32[5,8,8,128]{3,2,1,0:T(8,128)S(1)} %collective-permute-done.10.p2, ...), custom_call_target="tpu_custom_call" | custom-call | tf_op jit(solution)/shard_map/eta_lines/pallas_call | solution.py:246
  61.3 0.6 collective-permute-start.18
  61.9 2.7 %collective-permute-start.17 = (f32[8,5,64,128]{3,2,1,0:T(8,128)S(1)}, f32[8,5,64,128]{3,2,1,0:T(8,128)S(1)}, u32[]{:S(2)}, u32[]{:S(2)}) collective-permute-start(f32[8,5,64,128]{3,2,1,0:T(8,128)S(1)} %copy-done.12), channel_id=1, source_target_pairs={{0,1},{1,2},{2,3},{3,0},{4,5},{5,6},{6,7},{7,4},{8,9},{9,10},{10,1... | collective-permute-start | bytes 3932168 | tf_op jit(solution)/shard_map/ppermute | solution.py:415
  64.6 29.1 %collective-permute-done.18.refs_3_ = f32[8,5,64,128]{3,2,1,0:T(8,128)S(1)} collective-permute-done((f32[8,5,64,128]{3,2,1,0:T(8,128)}, f32[8,5,64,128]{3,2,1,0:T(8,128)S(1)}, u32[]{:S(2)}, u32[]{:S(2)}) %collective-permute-start.18) | collective-permute-done | bytes 1310752 | tf_op jit(solution)/shard_map/ppermute | solution.py:415
  93.8 0.5 collective-permute-start.21
  94.3 1.6 collective-permute-start.16
  96.1 13.6 %collective-permute-done.16.refs_1_ = f32[8,2,64,128]{3,2,1,0:T(8,128)S(1)} collective-permute-done((f32[8,2,64,128]{3,2,1,0:T(8,128)S(1)}, f32[8,2,64,128]{3,2,1,0:T(8,128)S(1)}, u32[]{:S(2)}, u32[]{:S(2)}) %collective-permute-start.16) | collective-permute-done | bytes 524320 | tf_op jit(solution)/shard_map/ppermute | solution.py:415
  109.7 1.9 %collective-permute-done.20.refs_5_ = f32[8,2,64,128]{3,2,1,0:T(8,128)S(1)} collective-permute-done((f32[8,2,64,128]{3,2,1,0:T(8,128)S(1)}, f32[8,2,64,128]{3,2,1,0:T(8,128)S(1)}, u32[]{:S(2)}, u32[]{:S(2)}) %collective-permute-start.20) | collective-permute-done | bytes 524320 | tf_op jit(solution)/shard_map/ppermute | solution.py:419
  111.6 4.8 %prepare.1 = (bf16[5,1024,128]{2,1,0:T(8,128)(2,1)S(1)}, bf16[5,1024,128]{2,1,0:T(8,128)(2,1)S(1)}, bf16[5,1024,256]{2,1,0:T(8,128)(2,1)S(1)}, bf16[5,1024,256]{2,1,0:T(8,128)(2,1)S(1)}) custom-call(f32[8,3,64,128]{3,2,1,0:T(8,128)S(1)} %collective-permute-done.8.refs_0_, f32[8,2,64,128]{3,2,1,0:T(8,128)S(1)} %collective-permute-done.16.refs_1_, ...), custom_call_target="tpu_custom_call" | custom-call | tf_op jit(solution)/shard_map/prepare/pallas_call | solution.py:322
  116.4 1.5 copy-done.2
  118.0 1.6 copy-done.3
  119.6 1.1 copy-done.4
  120.6 1.1 copy-done.5
  121.8 8.7 %all-gather.3.cloned.1.call-done = f32[40,8,32,128]{3,2,1,0:T(8,128)} async-done(((f32[5,8,32,128]{3,2,1,0:T(8,128)}), f32[40,8,32,128]{3,2,1,0:T(8,128)}) %all-gather.3.cloned.1.call-update) | async-done | bytes 5242896 | tf_op jit(solution)/shard_map/all_gather | solution.py:455
  130.5 6.5 %zeta_lines.3 = (f32[5,128,128]{2,1,0:T(8,128)}, f32[5,128,128]{2,1,0:T(8,128)}) custom-call(f32[8,5,8,32,128]{4,3,2,1,0:T(8,128)} %bitcast.1, bf16[5,1024,128]{2,1,0:T(8,128)(2,1)} %copy-done.4, bf16[5,1024,128]{2,1,0:T(8,128)(2,1)} %copy-done.5), custom_call_target="tpu_custom_call" | custom-call | tf_op jit(solution)/shard_map/zeta_lines/pallas_call | solution.py:348
  136.9 0.8 collective-permute-start.27
  137.8 2.4 %collective-permute-start.23 = (f32[5,128,128]{2,1,0:T(8,128)}, f32[5,128,128]{2,1,0:T(8,128)S(1)}, u32[]{:S(2)}, u32[]{:S(2)}) collective-permute-start(f32[5,128,128]{2,1,0:T(8,128)} %get-tuple-element.81), channel_id=1, source_target_pairs={{0,1},{1,2},{2,3},{3,0},{4,5},{5,6},{6,7},{7,4},{8,9},{9,10},{10,1... | collective-permute-start | bytes 983048 | tf_op jit(solution)/shard_map/ppermute | solution.py:415
  140.2 8.1 %zeta_lines.2 = (f32[5,128,128]{2,1,0:T(8,128)}, f32[5,128,128]{2,1,0:T(8,128)}, f32[5,128,128]{2,1,0:T(8,128)}, f32[5,128,128]{2,1,0:T(8,128)}) custom-call(f32[8,5,8,32,128]{4,3,2,1,0:T(8,128)} %bitcast.2, bf16[5,1024,256]{2,1,0:T(8,128)(2,1)} %copy-done.2, bf16[5,1024,256]{2,1,0:T(8,128)(2,1)} %copy-done.3), custom_call_target="tpu_custom_call" | custom-call | tf_op jit(solution)/shard_map/zeta_lines/pallas_call | solution.py:348
  148.3 2.0 %collective-permute-start.26 = (f32[5,128,128]{2,1,0:T(8,128)}, f32[5,128,128]{2,1,0:T(8,128)S(1)}, u32[]{:S(2)}, u32[]{:S(2)}) collective-permute-start(f32[5,128,128]{2,1,0:T(8,128)} %get-tuple-element.73), channel_id=1, source_target_pairs={{0,3},{1,0},{2,1},{3,2},{4,7},{5,4},{6,5},{7,6},{8,11},{9,8},{10,9... | collective-permute-start | bytes 983048 | tf_op jit(solution)/shard_map/ppermute | solution.py:415
  150.3 1.0 add.7
  151.4 1.0 add.6
  152.4 3.3 %collective-permute-start.24 = (f32[5,128,128]{2,1,0:T(8,128)S(1)}, f32[5,128,128]{2,1,0:T(8,128)S(1)}, u32[]{:S(2)}, u32[]{:S(2)}) collective-permute-start(f32[5,128,128]{2,1,0:T(8,128)S(1)} %add.6), channel_id=1, source_target_pairs={{0,1},{1,2},{2,3},{3,0},{4,5},{5,6},{6,7},{7,4},{8,9},{9,10},{10,1... | collective-permute-start | bytes 983048 | tf_op jit(solution)/shard_map/ppermute | solution.py:415
  155.7 4.0 %copy-done = f32[5,128,4096]{2,1,0:T(8,128)S(1)} copy-done((f32[5,128,4096]{2,1,0:T(8,128)S(1)}, f32[5,128,4096]{2,1,0:T(8,128)}, u32[]{:S(2)}) %copy-start) | copy-done | bytes 10485784
  159.7 3.4 %own_lines.1 = (f32[5,128,128]{2,1,0:T(8,128)S(1)}, f32[5,128,128]{2,1,0:T(8,128)S(1)}) custom-call(f32[8,5,8,32,128]{4,3,2,1,0:T(8,128)S(1)} %bitcast.5, f32[5,128,4096]{2,1,0:T(8,128)S(1)} %copy-done), custom_call_target="tpu_custom_call" | custom-call | tf_op jit(solution)/shard_map/own_lines/pallas_call | solution.py:371
  163.1 2.5 %collective-permute-done.28.high1 = f32[5,128,128]{2,1,0:T(8,128)S(1)} collective-permute-done((f32[5,128,128]{2,1,0:T(8,128)S(1)}, f32[5,128,128]{2,1,0:T(8,128)S(1)}, u32[]{:S(2)}, u32[]{:S(2)}) %collective-permute-start.28) | collective-permute-done | bytes 327712 | tf_op jit(solution)/shard_map/ppermute | solution.py:415
  165.7 2.0 %final.1 = f32[5,8,32,128]{3,2,1,0:T(8,128)} custom-call(f32[4,5,5]{2,1,0:T(8,128)S(1)} %copy.14.t_ref, f32[5,8,32,128]{3,2,1,0:T(8,128)S(1)} %copy-done.1, f32[5,128,128]{2,1,0:T(8,128)S(1)} %get-tuple-element.76.own0, f32[5,128,128]{2,1,0:T(8,128)S(1)} %get-tuple-element.77.own1, f32[5,128,128]{2,1,0:T(8,128)S(1)} %collective-permute-done.24.low0, ...), custom_call_target="tpu_custom_call" | custom-call | tf_op jit(solution)/shard_map/final/pallas_call | solution.py:399
  (61 shorter events, 0.7 us)
Async XLA Ops:
  7.2 123.3 %all-gather.3.cloned.1.call-start = ((), (), s32[]{:S(2)}) async-start(), calls=%async_computation | async-start | bytes 5898240 | tf_op jit(solution)/shard_map/all_gather | solution.py:455
  9.2 15.4 %collective-permute-start = (f32[5,2,32,128]{3,2,1,0:T(8,128)}, f32[5,2,32,128]{3,2,1,0:T(8,128)S(1)}, u32[]{:S(2)}, u32[]{:S(2)}) collective-permute-start(f32[5,2,32,128]{3,2,1,0:T(8,128)} %get-tuple-element.43), channel_id=1, source_target_pairs={{0,64},{64,128},{128,192},{1,65},{65,129},{129,193},{2,66},{66,130... | collective-permute-start | bytes 491528 | tf_op jit(solution)/shard_map/ppermute | solution.py:425
  12.6 13.3 %collective-permute-start.1 = (f32[5,2,32,128]{3,2,1,0:T(8,128)}, f32[5,2,32,128]{3,2,1,0:T(8,128)S(1)}, u32[]{:S(2)}, u32[]{:S(2)}) collective-permute-start(f32[5,2,32,128]{3,2,1,0:T(8,128)} %get-tuple-element.46), channel_id=1, source_target_pairs={{64,0},{128,64},{192,128},{65,1},{129,65},{193,129},{66,2},{130,66... | collective-permute-start | bytes 491528 | tf_op jit(solution)/shard_map/ppermute | solution.py:425
  13.9 12.0 %collective-permute-start.2 = (f32[5,8,8,128]{3,2,1,0:T(8,128)}, f32[5,8,8,128]{3,2,1,0:T(8,128)S(1)}, u32[]{:S(2)}, u32[]{:S(2)}) collective-permute-start(f32[5,8,8,128]{3,2,1,0:T(8,128)} %get-tuple-element.47), channel_id=1, source_target_pairs={{0,32},{32,0},{1,33},{33,1},{2,34},{34,2},{3,35},{35,3},{4,36},{36... | collective-permute-start | bytes 491528 | tf_op jit(solution)/shard_map/ppermute | solution.py:419
  14.0 10.6 %collective-permute-start.3 = (f32[8,1280]{1,0:T(8,128)}, f32[8,1280]{1,0:T(8,128)S(1)}, u32[]{:S(2)}, u32[]{:S(2)}) collective-permute-start(f32[8,1280]{1,0:T(8,128)} %get-tuple-element.48), channel_id=1, source_target_pairs={{0,1},{1,2},{2,3},{3,4},{4,5},{5,6},{6,7},{7,8},{8,9},{9,10},{10,1... | collective-permute-start | bytes 122888 | tf_op jit(solution)/shard_map/ppermute | solution.py:425
  17.5 7.1 %copy-start.11 = (f32[4,5,5]{2,0,1:T(4,128)S(1)}, f32[4,5,5]{2,0,1:T(4,128)}, u32[]{:S(2)}) copy-start(f32[4,5,5]{2,0,1:T(4,128)} %param.12) | copy-start | bytes 1204
  17.5 8.4 %copy-start.1 = (f32[5,8,32,128]{3,2,1,0:T(8,128)S(1)}, f32[5,8,32,128]{3,2,1,0:T(8,128)}, u32[]{:S(2)}) copy-start(f32[5,8,32,128]{3,2,1,0:T(8,128)} %state.5) | copy-start | bytes 1966084
  17.5 8.4 %copy-start.6 = (f32[8,32,128]{2,1,0:T(8,128)S(1)}, f32[8,32,128]{2,1,0:T(8,128)}, u32[]{:S(2)}) copy-start(f32[8,32,128]{2,1,0:T(8,128)} %radius_hbm.1) | copy-start | bytes 393220
  17.5 8.4 %copy-start.7 = (s32[8,32,128]{2,1,0:T(8,128)S(1)}, s32[8,32,128]{2,1,0:T(8,128)}, u32[]{:S(2)}) copy-start(s32[8,32,128]{2,1,0:T(8,128)} %iblank_hbm.1) | copy-start | bytes 393220
  17.5 8.4 %copy-start.9 = (f32[5,8,32]{2,1,0:T(8,128)S(1)}, f32[5,8,32]{2,1,0:T(8,128)}, u32[]{:S(2)}) copy-start(f32[5,8,32]{2,1,0:T(8,128)} %inv_xi_hbm.1) | copy-start | bytes 15364
  17.6 8.4 %copy-start.10 = (f32[3,5]{1,0:T(4,128)S(1)}, f32[3,5]{1,0:T(4,128)}, u32[]{:S(2)}) copy-start(f32[3,5]{1,0:T(4,128)} %speeds.1) | copy-start | bytes 184
  17.6 8.3 %collective-permute-start.4 = (f32[8,1280]{1,0:T(8,128)}, f32[8,1280]{1,0:T(8,128)S(1)}, u32[]{:S(2)}, u32[]{:S(2)}) collective-permute-start(f32[8,1280]{1,0:T(8,128)} %get-tuple-element.49), channel_id=1, source_target_pairs={{1,0},{2,1},{3,2},{4,3},{5,4},{6,5},{7,6},{8,7},{9,8},{10,9},{11,1... | collective-permute-start | bytes 122888 | tf_op jit(solution)/shard_map/ppermute | solution.py:425
  24.6 5.2 %copy-start.13 = (f32[8,3,64,128]{3,2,1,0:T(8,128)S(1)}, f32[8,3,64,128]{3,2,1,0:T(8,128)}, u32[]{:S(2)}) copy-start(f32[8,3,64,128]{3,2,1,0:T(8,128)} %get-tuple-element.56) | copy-start | bytes 2359300
  24.6 34.1 %copy-start.8 = (f32[5,32,64]{2,1,0:T(8,128)S(1)}, f32[5,32,64]{2,1,0:T(8,128)}, u32[]{:S(2)}) copy-start(f32[5,32,64]{2,1,0:T(8,128)} %inv_eta.1) | copy-start | bytes 122884
  29.8 27.8 %collective-permute-start.8 = (f32[8,3,64,128]{3,2,1,0:T(8,128)S(1)}, f32[8,3,64,128]{3,2,1,0:T(8,128)S(1)}, u32[]{:S(2)}, u32[]{:S(2)}) collective-permute-start(f32[8,3,64,128]{3,2,1,0:T(8,128)S(1)} %copy-done.13), channel_id=1, source_target_pairs={{0,2},{1,3},{2,0},{3,1},{4,6},{5,7},{6,4},{7,5},{8,10},{9,11},{10,... | collective-permute-start | bytes 2359304 | tf_op jit(solution)/shard_map/ppermute | solution.py:415
  29.9 8.6 %collective-permute-start.5 = (f32[5,9,8,128]{3,2,1,0:T(8,128)S(1)}, f32[5,9,8,128]{3,2,1,0:T(8,128)S(1)}, u32[]{:S(2)}, u32[]{:S(2)}) collective-permute-start(f32[5,9,8,128]{3,2,1,0:T(8,128)S(1)} %get-tuple-element.52), channel_id=1, source_target_pairs={{0,64},{64,128},{128,192},{192,0},{1,65},{65,129},{129,193},{193,1... | collective-permute-start | bytes 552968 | tf_op jit(solution)/shard_map/ppermute | solution.py:410
  32.6 10.7 %collective-permute-start.6 = (f32[5,9,8,128]{3,2,1,0:T(8,128)S(1)}, f32[5,9,8,128]{3,2,1,0:T(8,128)S(1)}, u32[]{:S(2)}, u32[]{:S(2)}) collective-permute-start(f32[5,9,8,128]{3,2,1,0:T(8,128)S(1)} %get-tuple-element.53), channel_id=1, source_target_pairs={{0,128},{64,192},{128,0},{192,64},{1,129},{65,193},{129,1},{193,65... | collective-permute-start | bytes 552968 | tf_op jit(solution)/shard_map/ppermute | solution.py:410
  35.4 8.0 %collective-permute-start.7 = (f32[5,9,8,128]{3,2,1,0:T(8,128)S(1)}, f32[5,9,8,128]{3,2,1,0:T(8,128)S(1)}, u32[]{:S(2)}, u32[]{:S(2)}) collective-permute-start(f32[5,9,8,128]{3,2,1,0:T(8,128)S(1)} %get-tuple-element.54), channel_id=1, source_target_pairs={{0,192},{64,0},{128,64},{192,128},{1,193},{65,1},{129,65},{193,129... | collective-permute-start | bytes 552968 | tf_op jit(solution)/shard_map/ppermute | solution.py:410
  46.7 8.1 %collective-permute-start.9 = (f32[5,8,8,128]{3,2,1,0:T(8,128)S(1)}, f32[5,8,8,128]{3,2,1,0:T(8,128)S(1)}, u32[]{:S(2)}, u32[]{:S(2)}) collective-permute-start(f32[5,8,8,128]{3,2,1,0:T(8,128)S(1)} %get-tuple-element.58), channel_id=1, source_target_pairs={{0,64},{64,128},{128,192},{192,0},{1,65},{65,129},{129,193},{193,1... | collective-permute-start | bytes 491528 | tf_op jit(solution)/shard_map/ppermute | solution.py:410
  47.9 9.2 %collective-permute-start.10 = (f32[5,8,8,128]{3,2,1,0:T(8,128)S(1)}, f32[5,8,8,128]{3,2,1,0:T(8,128)S(1)}, u32[]{:S(2)}, u32[]{:S(2)}) collective-permute-start(f32[5,8,8,128]{3,2,1,0:T(8,128)S(1)} %get-tuple-element.59), channel_id=1, source_target_pairs={{0,128},{64,192},{128,0},{192,64},{1,129},{65,193},{129,1},{193,65... | collective-permute-start | bytes 491528 | tf_op jit(solution)/shard_map/ppermute | solution.py:410
  50.3 6.8 %collective-permute-start.11 = (f32[5,8,8,128]{3,2,1,0:T(8,128)S(1)}, f32[5,8,8,128]{3,2,1,0:T(8,128)S(1)}, u32[]{:S(2)}, u32[]{:S(2)}) collective-permute-start(f32[5,8,8,128]{3,2,1,0:T(8,128)S(1)} %get-tuple-element.60), channel_id=1, source_target_pairs={{0,192},{64,0},{128,64},{192,128},{1,193},{65,1},{129,65},{193,129... | collective-permute-start | bytes 491528 | tf_op jit(solution)/shard_map/ppermute | solution.py:410
  52.1 9.9 %copy-start.12 = (f32[8,5,64,128]{3,2,1,0:T(8,128)S(1)}, f32[8,5,64,128]{3,2,1,0:T(8,128)}, u32[]{:S(2)}) copy-start(f32[8,5,64,128]{3,2,1,0:T(8,128)} %get-tuple-element.64) | copy-start | bytes 3932164
  52.1 42.2 %copy-start.14 = (f32[8,2,64,128]{3,2,1,0:T(8,128)S(1)}, f32[8,2,64,128]{3,2,1,0:T(8,128)}, u32[]{:S(2)}) copy-start(f32[8,2,64,128]{3,2,1,0:T(8,128)} %get-tuple-element.62) | copy-start | bytes 1572868
  52.1 5.6 %collective-permute-start.12 = (f32[5,8,8,128]{3,2,1,0:T(8,128)S(1)}, f32[5,8,8,128]{3,2,1,0:T(8,128)S(1)}, u32[]{:S(2)}, u32[]{:S(2)}) collective-permute-start(f32[5,8,8,128]{3,2,1,0:T(8,128)S(1)} %get-tuple-element.57.p0), channel_id=1, source_target_pairs={{0,32},{32,0},{1,33},{33,1},{2,34},{34,2},{3,35},{35,3},{4,36},{36... | collective-permute-start | bytes 491528 | tf_op jit(solution)/shard_map/ppermute | solution.py:419
  54.8 2.8 %collective-permute-start.13 = (f32[5,8,8,128]{3,2,1,0:T(8,128)S(1)}, f32[5,8,8,128]{3,2,1,0:T(8,128)S(1)}, u32[]{:S(2)}, u32[]{:S(2)}) collective-permute-start(f32[5,8,8,128]{3,2,1,0:T(8,128)S(1)} %collective-permute-done.9.p1), channel_id=1, source_target_pairs={{0,32},{32,0},{1,33},{33,1},{2,34},{34,2},{3,35},{35,3},{4,36},{36... | collective-permute-start | bytes 491528 | tf_op jit(solution)/shard_map/ppermute | solution.py:419
  57.1 1.4 collective-permute-start.14
  57.1 1.6 collective-permute-start.15
  61.3 32.5 %collective-permute-start.18 = (f32[8,5,64,128]{3,2,1,0:T(8,128)}, f32[8,5,64,128]{3,2,1,0:T(8,128)S(1)}, u32[]{:S(2)}, u32[]{:S(2)}) collective-permute-start(f32[8,5,64,128]{3,2,1,0:T(8,128)} %get-tuple-element.66), channel_id=1, source_target_pairs={{0,3},{1,0},{2,1},{3,2},{4,7},{5,4},{6,5},{7,6},{8,11},{9,8},{10,9... | collective-permute-start | bytes 3932168 | tf_op jit(solution)/shard_map/ppermute | solution.py:415
  61.9 31.8 %collective-permute-start.17 = (f32[8,5,64,128]{3,2,1,0:T(8,128)S(1)}, f32[8,5,64,128]{3,2,1,0:T(8,128)S(1)}, u32[]{:S(2)}, u32[]{:S(2)}) collective-permute-start(f32[8,5,64,128]{3,2,1,0:T(8,128)S(1)} %copy-done.12), channel_id=1, source_target_pairs={{0,1},{1,2},{2,3},{3,0},{4,5},{5,6},{6,7},{7,4},{8,9},{9,10},{10,1... | collective-permute-start | bytes 3932168 | tf_op jit(solution)/shard_map/ppermute | solution.py:415
  93.7 17.9 %collective-permute-start.22 = (f32[8,5,64,128]{3,2,1,0:T(8,128)S(1)}, f32[8,5,64,128]{3,2,1,0:T(8,128)S(1)}, u32[]{:S(2)}, u32[]{:S(2)}) collective-permute-start(f32[8,5,64,128]{3,2,1,0:T(8,128)S(1)} %collective-permute-done.18.refs_3_), channel_id=1, source_target_pairs={{0,32},{32,0},{1,33},{33,1},{2,34},{34,2},{3,35},{35,3},{4,36},{36... | collective-permute-start | bytes 3932168 | tf_op jit(solution)/shard_map/ppermute | solution.py:419
  93.8 17.9 %collective-permute-start.21 = (f32[8,5,64,128]{3,2,1,0:T(8,128)S(1)}, f32[8,5,64,128]{3,2,1,0:T(8,128)S(1)}, u32[]{:S(2)}, u32[]{:S(2)}) collective-permute-start(f32[8,5,64,128]{3,2,1,0:T(8,128)S(1)} %collective-permute-done.17.refs_2_), channel_id=1, source_target_pairs={{0,32},{32,0},{1,33},{33,1},{2,34},{34,2},{3,35},{35,3},{4,36},{36... | collective-permute-start | bytes 3932168 | tf_op jit(solution)/shard_map/ppermute | solution.py:419
  94.3 15.4 %collective-permute-start.16 = (f32[8,2,64,128]{3,2,1,0:T(8,128)S(1)}, f32[8,2,64,128]{3,2,1,0:T(8,128)S(1)}, u32[]{:S(2)}, u32[]{:S(2)}) collective-permute-start(f32[8,2,64,128]{3,2,1,0:T(8,128)S(1)} %copy-done.14), channel_id=1, source_target_pairs={{0,2},{1,3},{2,0},{3,1},{4,6},{5,7},{6,4},{7,5},{8,10},{9,11},{10,... | collective-permute-start | bytes 1572872 | tf_op jit(solution)/shard_map/ppermute | solution.py:415
  95.9 13.8 %collective-permute-start.19 = (f32[8,3,64,128]{3,2,1,0:T(8,128)S(1)}, f32[8,3,64,128]{3,2,1,0:T(8,128)S(1)}, u32[]{:S(2)}, u32[]{:S(2)}) collective-permute-start(f32[8,3,64,128]{3,2,1,0:T(8,128)S(1)} %collective-permute-done.8.refs_0_), channel_id=1, source_target_pairs={{0,32},{32,0},{1,33},{33,1},{2,34},{34,2},{3,35},{35,3},{4,36},{36... | collective-permute-start | bytes 2359304 | tf_op jit(solution)/shard_map/ppermute | solution.py:419
  109.7 1.9 %collective-permute-start.20 = (f32[8,2,64,128]{3,2,1,0:T(8,128)S(1)}, f32[8,2,64,128]{3,2,1,0:T(8,128)S(1)}, u32[]{:S(2)}, u32[]{:S(2)}) collective-permute-start(f32[8,2,64,128]{3,2,1,0:T(8,128)S(1)} %collective-permute-done.16.refs_1_), channel_id=1, source_target_pairs={{0,32},{32,0},{1,33},{33,1},{2,34},{34,2},{3,35},{35,3},{4,36},{36... | collective-permute-start | bytes 1572872 | tf_op jit(solution)/shard_map/ppermute | solution.py:419
  116.4 1.6 copy-start.2
  118.0 1.6 copy-start.3
  119.6 1.1 copy-start.4
  120.6 1.1 copy-start.5
  136.9 13.3 %collective-permute-start.27 = (f32[5,128,128]{2,1,0:T(8,128)}, f32[5,128,128]{2,1,0:T(8,128)S(1)}, u32[]{:S(2)}, u32[]{:S(2)}) collective-permute-start(f32[5,128,128]{2,1,0:T(8,128)} %get-tuple-element.83), channel_id=1, source_target_pairs={{0,3},{1,0},{2,1},{3,2},{4,7},{5,4},{6,5},{7,6},{8,11},{9,8},{10,9... | collective-permute-start | bytes 983048 | tf_op jit(solution)/shard_map/ppermute | solution.py:415
  137.8 13.6 %collective-permute-start.23 = (f32[5,128,128]{2,1,0:T(8,128)}, f32[5,128,128]{2,1,0:T(8,128)S(1)}, u32[]{:S(2)}, u32[]{:S(2)}) collective-permute-start(f32[5,128,128]{2,1,0:T(8,128)} %get-tuple-element.81), channel_id=1, source_target_pairs={{0,1},{1,2},{2,3},{3,0},{4,5},{5,6},{6,7},{7,4},{8,9},{9,10},{10,1... | collective-permute-start | bytes 983048 | tf_op jit(solution)/shard_map/ppermute | solution.py:415
  140.2 15.5 %slice-start = ((s8[5242880]{0:T(1024)(128)(4,1)}), s8[4194304]{0:T(1024)(128)(4,1)S(1)}, s32[]{:S(2)}) async-start(s8[5242880]{0:T(1024)(128)(4,1)} %bitcast.3), calls=%async_computation.1 | async-start | bytes 8388608
  140.2 15.5 %slice-start.1 = ((s8[5242880]{0:T(1024)(128)(4,1)}), s8[1048576]{0:T(1024)(128)(4,1)S(1)}, s32[]{:S(2)}) async-start(s8[5242880]{0:T(1024)(128)(4,1)} %bitcast.3), calls=%async_computation.2 | async-start | bytes 2097152
  148.2 14.9 %collective-permute-start.25 = (f32[5,128,128]{2,1,0:T(8,128)}, f32[5,128,128]{2,1,0:T(8,128)S(1)}, u32[]{:S(2)}, u32[]{:S(2)}) collective-permute-start(f32[5,128,128]{2,1,0:T(8,128)} %get-tuple-element.74), channel_id=1, source_target_pairs={{0,1},{1,2},{2,3},{3,0},{4,5},{5,6},{6,7},{7,4},{8,9},{9,10},{10,1... | collective-permute-start | bytes 983048 | tf_op jit(solution)/shard_map/ppermute | solution.py:415
  148.3 14.9 %collective-permute-start.26 = (f32[5,128,128]{2,1,0:T(8,128)}, f32[5,128,128]{2,1,0:T(8,128)S(1)}, u32[]{:S(2)}, u32[]{:S(2)}) collective-permute-start(f32[5,128,128]{2,1,0:T(8,128)} %get-tuple-element.73), channel_id=1, source_target_pairs={{0,3},{1,0},{2,1},{3,2},{4,7},{5,4},{6,5},{7,6},{8,11},{9,8},{10,9... | collective-permute-start | bytes 983048 | tf_op jit(solution)/shard_map/ppermute | solution.py:415
  151.3 14.4 %collective-permute-start.28 = (f32[5,128,128]{2,1,0:T(8,128)S(1)}, f32[5,128,128]{2,1,0:T(8,128)S(1)}, u32[]{:S(2)}, u32[]{:S(2)}) collective-permute-start(f32[5,128,128]{2,1,0:T(8,128)S(1)} %add.7), channel_id=1, source_target_pairs={{0,3},{1,0},{2,1},{3,2},{4,7},{5,4},{6,5},{7,6},{8,11},{9,8},{10,9... | collective-permute-start | bytes 983048 | tf_op jit(solution)/shard_map/ppermute | solution.py:415
  152.4 13.3 %collective-permute-start.24 = (f32[5,128,128]{2,1,0:T(8,128)S(1)}, f32[5,128,128]{2,1,0:T(8,128)S(1)}, u32[]{:S(2)}, u32[]{:S(2)}) collective-permute-start(f32[5,128,128]{2,1,0:T(8,128)S(1)} %add.6), channel_id=1, source_target_pairs={{0,1},{1,2},{2,3},{3,0},{4,5},{5,6},{6,7},{7,4},{8,9},{9,10},{10,1... | collective-permute-start | bytes 983048 | tf_op jit(solution)/shard_map/ppermute | solution.py:415
  155.7 4.0 %copy-start = (f32[5,128,4096]{2,1,0:T(8,128)S(1)}, f32[5,128,4096]{2,1,0:T(8,128)}, u32[]{:S(2)}) copy-start(f32[5,128,4096]{2,1,0:T(8,128)} %inv.2) | copy-start | bytes 31457284
Sparse Core Ops, SparseCore 0:
  61.4 69.0 all-gather.2

commit v2 on v1

--- a/solution.py
+++ b/solution.py
@@ -342,7 +342,7 @@
             outs.pop(0)[0] = value[128:, lanes]
 
 
-def zeta_step(gathered, *lines):
+def zeta_step(gathered, *lines, limit):
     widths = [array.shape[2] for array in lines]
     count = sum(widths) // 128
     return pl.pallas_call(
@@ -352,7 +352,7 @@
         + [pl.BlockSpec((1, 1024, w), lambda v: (v, 0, 0)) for w in widths],
         out_specs=[pl.BlockSpec((1, 128, 128), lambda v: (v, 0, 0))] * count,
         out_shape=[shape(5, 128, 128)] * count,
-        compiler_params=pltpu.CompilerParams(vmem_limit_bytes=56 << 20),
+        compiler_params=pltpu.CompilerParams(vmem_limit_bytes=limit << 20),
         name="zeta_lines",
     )(gathered, *lines)
 
@@ -457,9 +457,9 @@
     swapped = [over_core(after(part, work)) for part in sent]
     high2, low2, high, low = prepare(sent, swapped)
 
-    far0, far1 = zeta_step(gathered, high2, low2)
+    far0, far1 = zeta_step(gathered, high2, low2, limit=56)
     far0, far1 = over_y(far0, 1), over_y(far1, -1)
-    down0, down1, up0, up1 = zeta_step(gathered, high, low)
+    down0, down1, up0, up1 = zeta_step(gathered, high, low, limit=24)
     own0, own1 = own_step(gathered, after(inv_zeta, down0, up1))
     up1, down0 = over_y(up1, 1), over_y(down0, -1)
     up0, down1 = over_y(up0 + far0, 1), over_y(down1 + far1, -1)

time: 175 us -> 174 us (level)
  Pallas kernels: 40.9 us -> 36.6 us
  local copies, waits for them, and re-layouts: 9.38 us -> 12.8 us
  other arithmetic: 2.02 us -> 0.07 us
    pallas_call x2, Pallas kernels: 14.5 us -> 10.3 us  [zeta_step(): pl.pallas_call(functools.partial(zeta_kernel, len(lines) // 2), grid=(5,)...]
    unnamed x35 -> x37, local copies, waits for them, and re-layouts: 9.38 us -> 12.8 us
    add x2, other arithmetic: 2.02 us -> 0.07 us  [local(): up0, down1 = (over_y(up0 + far0, 1), over_y(down1 + far1, -1))]
  transfers between devices with their start and end apart: 30 -> 30, of which waited for: 12 -> 12; matrix products, arithmetic and copies ran while one was open for 1% -> 0% of each run, Pallas kernels for 14% -> 11%
where the time goes in v2:
time: 174 us
  waiting for transfers between devices  71.6 us (41%)
  starting transfers between devices  38 us (22%)
  Pallas kernels  36.6 us (21%)
  between operations  14.4 us (8%)
  local copies, waits for them, and re-layouts  12.8 us (7%)
    ppermute x10, waiting for transfers between devices, over_y(): return lax.ppermute(array, 'zeta', pairs)  47 us
    ppermute x10, starting transfers between devices, over_y(): return lax.ppermute(array, 'zeta', pairs)  13.7 us
    unnamed x37, local copies, waits for them, and re-layouts  12.8 us
    ppermute x6, starting transfers between devices, over_x(): return lax.ppermute(array, 'xi', [(i, (i + s) % 4) for i in range(4)])  12.2 us
    ppermute x6, waiting for transfers between devices, over_x(): return lax.ppermute(array, 'xi', [(i, (i + s) % 4) for i in range(4)])  11.6 us
    ppermute x4, starting transfers between devices, shift_line(): return lax.ppermute(array, axis, pairs)  10.7 us
    pallas_call x2, Pallas kernels, zeta_step(): pl.pallas_call(functools.partial(zeta_kernel, len(lines) // 2), grid=(5,)...  10.3 us
    all_gather x1, waiting for transfers between devices, local(): gathered = lax.all_gather(work, 'zeta', axis_index_groups=columns)  8.71 us
  transfers between devices with their start and end apart: 30, of which 12 were waited for; matrix products, arithmetic and copies ran while one was open for 0% of the time, Pallas kernels for 11%

profile of v2, /device:TPU:24, one launch (start us, length us, event | category | flops | bytes accessed | tf_op | source)
XLA Modules:
  0.0 173.6 jit_solution(8664625095000452997)
XLA Ops:
  7.2 2.0 %faces.1 = (f32[5,2,32,128]{3,2,1,0:T(8,128)}, f32[5,2,32,128]{3,2,1,0:T(8,128)}, f32[5,8,8,128]{3,2,1,0:T(8,128)}, f32[8,1280]{1,0:T(8,128)}, f32[8,1280]{1,0:T(8,128)}) custom-call(f32[5,8,32,128]{3,2,1,0:T(8,128)} %state.5), custom_call_target="tpu_custom_call" | custom-call | tf_op jit(solution)/shard_map/faces/pallas_call | solution.py:70
  9.2 3.4 %collective-permute-start = (f32[5,2,32,128]{3,2,1,0:T(8,128)}, f32[5,2,32,128]{3,2,1,0:T(8,128)S(1)}, u32[]{:S(2)}, u32[]{:S(2)}) collective-permute-start(f32[5,2,32,128]{3,2,1,0:T(8,128)} %get-tuple-element.43), channel_id=1, source_target_pairs={{0,64},{64,128},{128,192},{1,65},{65,129},{129,193},{2,66},{66,130... | collective-permute-start | bytes 491528 | tf_op jit(solution)/shard_map/ppermute | solution.py:425
  12.6 1.3 collective-permute-start.1
  14.0 3.5 %collective-permute-start.3 = (f32[8,1280]{1,0:T(8,128)}, f32[8,1280]{1,0:T(8,128)S(1)}, u32[]{:S(2)}, u32[]{:S(2)}) collective-permute-start(f32[8,1280]{1,0:T(8,128)} %get-tuple-element.48), channel_id=1, source_target_pairs={{0,1},{1,2},{2,3},{3,4},{4,5},{5,6},{6,7},{7,8},{8,9},{9,10},{10,1... | collective-permute-start | bytes 122888 | tf_op jit(solution)/shard_map/ppermute | solution.py:425
  17.6 2.5 %collective-permute-start.4 = (f32[8,1280]{1,0:T(8,128)}, f32[8,1280]{1,0:T(8,128)S(1)}, u32[]{:S(2)}, u32[]{:S(2)}) collective-permute-start(f32[8,1280]{1,0:T(8,128)} %get-tuple-element.49), channel_id=1, source_target_pairs={{1,0},{2,1},{3,2},{4,3},{5,4},{6,5},{7,6},{8,7},{9,8},{10,9},{11,1... | collective-permute-start | bytes 122888 | tf_op jit(solution)/shard_map/ppermute | solution.py:425
  20.1 4.5 %pick.1 = (f32[8,3,64,128]{3,2,1,0:T(8,128)}, f32[8,2,64,128]{3,2,1,0:T(8,128)}, f32[8,5,64,128]{3,2,1,0:T(8,128)}, f32[8,5,64,128]{3,2,1,0:T(8,128)}) custom-call(f32[5,128,4096]{2,1,0:T(8,128)} %inv.2), custom_call_target="tpu_custom_call" | custom-call | tf_op jit(solution)/shard_map/pick/pallas_call | solution.py:276
  24.6 1.3 collective-permute-done.4.znext
  26.0 3.8 %residual.1 = (f32[5,8,32,128]{3,2,1,0:T(8,128)}, f32[5,9,8,128]{3,2,1,0:T(8,128)S(1)}, f32[5,9,8,128]{3,2,1,0:T(8,128)S(1)}, f32[5,9,8,128]{3,2,1,0:T(8,128)S(1)}, f32[5,9,8,128]{3,2,1,0:T(8,128)S(1)}) custom-call(f32[3,5]{1,0:T(4,128)S(1)} %copy-done.13, f32[4,5,5]{2,1,0:T(8,128)S(1)} %copy.14.t_ref, f32[5,8,32,128]{3,2,1,0:T(8,128)S(1)} %copy-done.2, ...), custom_call_target="tpu_custom_call" | custom-call | tf_op jit(solution)/shard_map/residual/pallas_call | solution.py:156
  29.9 2.7 %collective-permute-start.5 = (f32[5,9,8,128]{3,2,1,0:T(8,128)S(1)}, f32[5,9,8,128]{3,2,1,0:T(8,128)S(1)}, u32[]{:S(2)}, u32[]{:S(2)}) collective-permute-start(f32[5,9,8,128]{3,2,1,0:T(8,128)S(1)} %get-tuple-element.52), channel_id=1, source_target_pairs={{0,64},{64,128},{128,192},{192,0},{1,65},{65,129},{129,193},{193,1... | collective-permute-start | bytes 552968 | tf_op jit(solution)/shard_map/ppermute | solution.py:410
  32.6 2.7 %collective-permute-start.6 = (f32[5,9,8,128]{3,2,1,0:T(8,128)S(1)}, f32[5,9,8,128]{3,2,1,0:T(8,128)S(1)}, u32[]{:S(2)}, u32[]{:S(2)}) collective-permute-start(f32[5,9,8,128]{3,2,1,0:T(8,128)S(1)} %get-tuple-element.53), channel_id=1, source_target_pairs={{0,128},{64,192},{128,0},{192,64},{1,129},{65,193},{129,1},{193,65... | collective-permute-start | bytes 552968 | tf_op jit(solution)/shard_map/ppermute | solution.py:410
  35.4 1.4 collective-permute-start.7
  36.8 1.7 %collective-permute-done.5.r1 = f32[5,9,8,128]{3,2,1,0:T(8,128)S(1)} collective-permute-done((f32[5,9,8,128]{3,2,1,0:T(8,128)S(1)}, f32[5,9,8,128]{3,2,1,0:T(8,128)S(1)}, u32[]{:S(2)}, u32[]{:S(2)}) %collective-permute-start.5) | collective-permute-done | bytes 184352 | tf_op jit(solution)/shard_map/ppermute | solution.py:410
  38.5 4.8 %collective-permute-done.6.r2 = f32[5,9,8,128]{3,2,1,0:T(8,128)S(1)} collective-permute-done((f32[5,9,8,128]{3,2,1,0:T(8,128)S(1)}, f32[5,9,8,128]{3,2,1,0:T(8,128)S(1)}, u32[]{:S(2)}, u32[]{:S(2)}) %collective-permute-start.6) | collective-permute-done | bytes 184352 | tf_op jit(solution)/shard_map/ppermute | solution.py:410
  43.3 3.3 %xi_lines.1 = (f32[5,8,8,128]{3,2,1,0:T(8,128)S(1)}, f32[5,8,8,128]{3,2,1,0:T(8,128)S(1)}, f32[5,8,8,128]{3,2,1,0:T(8,128)S(1)}, f32[5,8,8,128]{3,2,1,0:T(8,128)S(1)}) custom-call(f32[4,5,5]{2,1,0:T(8,128)S(1)} %copy.14.t_ref, f32[5,9,8,128]{3,2,1,0:T(8,128)S(1)} %get-tuple-element.51.r0, f32[5,9,8,128]{3,2,1,0:T(8,128)S(1)} %collective-permute-done.5.r1, ...), custom_call_target="tpu_custom_call" | custom-call | tf_op jit(solution)/shard_map/xi_lines/pallas_call | solution.py:209
  46.7 1.2 collective-permute-start.9
  47.9 2.4 %collective-permute-start.10 = (f32[5,8,8,128]{3,2,1,0:T(8,128)S(1)}, f32[5,8,8,128]{3,2,1,0:T(8,128)S(1)}, u32[]{:S(2)}, u32[]{:S(2)}) collective-permute-start(f32[5,8,8,128]{3,2,1,0:T(8,128)S(1)} %get-tuple-element.59), channel_id=1, source_target_pairs={{0,128},{64,192},{128,0},{192,64},{1,129},{65,193},{129,1},{193,65... | collective-permute-start | bytes 491528 | tf_op jit(solution)/shard_map/ppermute | solution.py:410
  50.3 1.8 %collective-permute-start.11 = (f32[5,8,8,128]{3,2,1,0:T(8,128)S(1)}, f32[5,8,8,128]{3,2,1,0:T(8,128)S(1)}, u32[]{:S(2)}, u32[]{:S(2)}) collective-permute-start(f32[5,8,8,128]{3,2,1,0:T(8,128)S(1)} %get-tuple-element.60), channel_id=1, source_target_pairs={{0,192},{64,0},{128,64},{192,128},{1,193},{65,1},{129,65},{193,129... | collective-permute-start | bytes 491528 | tf_op jit(solution)/shard_map/ppermute | solution.py:410
  52.0 2.8 %collective-permute-done.9.p1 = f32[5,8,8,128]{3,2,1,0:T(8,128)S(1)} collective-permute-done((f32[5,8,8,128]{3,2,1,0:T(8,128)S(1)}, f32[5,8,8,128]{3,2,1,0:T(8,128)S(1)}, u32[]{:S(2)}, u32[]{:S(2)}) %collective-permute-start.9) | collective-permute-done | bytes 163872 | tf_op jit(solution)/shard_map/ppermute | solution.py:410
  54.9 2.2 %collective-permute-done.10.p2 = f32[5,8,8,128]{3,2,1,0:T(8,128)S(1)} collective-permute-done((f32[5,8,8,128]{3,2,1,0:T(8,128)S(1)}, f32[5,8,8,128]{3,2,1,0:T(8,128)S(1)}, u32[]{:S(2)}, u32[]{:S(2)}) %collective-permute-start.10) | collective-permute-done | bytes 163872 | tf_op jit(solution)/shard_map/ppermute | solution.py:410
  57.1 0.5 collective-permute-start.15
  57.6 0.9 collective-permute-done.14.q2
  58.5 0.2 collective-permute-done.15.q3
  58.7 2.5 %eta_lines.1 = f32[5,8,32,128]{3,2,1,0:T(8,128)} custom-call(f32[4,5,5]{2,1,0:T(8,128)S(1)} %copy.14.t_ref, f32[5,32,64]{2,1,0:T(8,128)S(1)} %copy-done.11, f32[5,8,8,128]{3,2,1,0:T(8,128)S(1)} %get-tuple-element.57.p0, f32[5,8,8,128]{3,2,1,0:T(8,128)S(1)} %collective-permute-done.9.p1, f32[5,8,8,128]{3,2,1,0:T(8,128)S(1)} %collective-permute-done.10.p2, ...), custom_call_target="tpu_custom_call" | custom-call | tf_op jit(solution)/shard_map/eta_lines/pallas_call | solution.py:246
  61.2 0.7 collective-permute-start.18
  61.9 2.7 %collective-permute-start.17 = (f32[8,5,64,128]{3,2,1,0:T(8,128)S(1)}, f32[8,5,64,128]{3,2,1,0:T(8,128)S(1)}, u32[]{:S(2)}, u32[]{:S(2)}) collective-permute-start(f32[8,5,64,128]{3,2,1,0:T(8,128)S(1)} %copy-done.15), channel_id=1, source_target_pairs={{0,1},{1,2},{2,3},{3,0},{4,5},{5,6},{6,7},{7,4},{8,9},{9,10},{10,1... | collective-permute-start | bytes 3932168 | tf_op jit(solution)/shard_map/ppermute | solution.py:415
  64.6 29.1 %collective-permute-done.18.refs_3_ = f32[8,5,64,128]{3,2,1,0:T(8,128)S(1)} collective-permute-done((f32[8,5,64,128]{3,2,1,0:T(8,128)}, f32[8,5,64,128]{3,2,1,0:T(8,128)S(1)}, u32[]{:S(2)}, u32[]{:S(2)}) %collective-permute-start.18) | collective-permute-done | bytes 1310752 | tf_op jit(solution)/shard_map/ppermute | solution.py:415
  93.7 0.5 collective-permute-start.21
  94.2 1.6 collective-permute-start.16
  96.1 13.6 %collective-permute-done.16.refs_1_ = f32[8,2,64,128]{3,2,1,0:T(8,128)S(1)} collective-permute-done((f32[8,2,64,128]{3,2,1,0:T(8,128)S(1)}, f32[8,2,64,128]{3,2,1,0:T(8,128)S(1)}, u32[]{:S(2)}, u32[]{:S(2)}) %collective-permute-start.16) | collective-permute-done | bytes 524320 | tf_op jit(solution)/shard_map/ppermute | solution.py:415
  109.7 1.9 %collective-permute-done.20.refs_5_ = f32[8,2,64,128]{3,2,1,0:T(8,128)S(1)} collective-permute-done((f32[8,2,64,128]{3,2,1,0:T(8,128)S(1)}, f32[8,2,64,128]{3,2,1,0:T(8,128)S(1)}, u32[]{:S(2)}, u32[]{:S(2)}) %collective-permute-start.20) | collective-permute-done | bytes 524320 | tf_op jit(solution)/shard_map/ppermute | solution.py:419
  111.6 4.8 %prepare.1 = (bf16[5,1024,128]{2,1,0:T(8,128)(2,1)S(1)}, bf16[5,1024,128]{2,1,0:T(8,128)(2,1)S(1)}, bf16[5,1024,256]{2,1,0:T(8,128)(2,1)S(1)}, bf16[5,1024,256]{2,1,0:T(8,128)(2,1)S(1)}) custom-call(f32[8,3,64,128]{3,2,1,0:T(8,128)S(1)} %collective-permute-done.8.refs_0_, f32[8,2,64,128]{3,2,1,0:T(8,128)S(1)} %collective-permute-done.16.refs_1_, ...), custom_call_target="tpu_custom_call" | custom-call | tf_op jit(solution)/shard_map/prepare/pallas_call | solution.py:322
  116.4 1.5 copy-done.3
  117.9 1.6 copy-done.5
  119.5 1.1 copy-done.7
  120.6 1.1 copy-done.8
  121.7 8.7 %all-gather.3.cloned.1.call-done = f32[40,8,32,128]{3,2,1,0:T(8,128)} async-done(((f32[5,8,32,128]{3,2,1,0:T(8,128)}), f32[40,8,32,128]{3,2,1,0:T(8,128)}) %all-gather.3.cloned.1.call-update) | async-done | bytes 5242896 | tf_op jit(solution)/shard_map/all_gather | solution.py:455
  130.4 7.0 %zeta_lines.3 = (f32[5,128,128]{2,1,0:T(8,128)}, f32[5,128,128]{2,1,0:T(8,128)}) custom-call(f32[8,5,8,32,128]{4,3,2,1,0:T(8,128)} %bitcast.1, bf16[5,1024,128]{2,1,0:T(8,128)(2,1)} %copy-done.7, bf16[5,1024,128]{2,1,0:T(8,128)(2,1)} %copy-done.8), custom_call_target="tpu_custom_call" | custom-call | tf_op jit(solution)/shard_map/zeta_lines/pallas_call | solution.py:348
  137.4 0.8 collective-permute-start.27
  138.2 2.4 %collective-permute-start.23 = (f32[5,128,128]{2,1,0:T(8,128)}, f32[5,128,128]{2,1,0:T(8,128)S(1)}, u32[]{:S(2)}, u32[]{:S(2)}) collective-permute-start(f32[5,128,128]{2,1,0:T(8,128)} %get-tuple-element.81), channel_id=1, source_target_pairs={{0,1},{1,2},{2,3},{3,0},{4,5},{5,6},{6,7},{7,4},{8,9},{9,10},{10,1... | collective-permute-start | bytes 983048 | tf_op jit(solution)/shard_map/ppermute | solution.py:415
  140.6 1.7 %copy-done.4 = bf16[5,1024,256]{2,1,0:T(8,128)(2,1)S(1)} copy-done((bf16[5,1024,256]{2,1,0:T(8,128)(2,1)S(1)}, bf16[5,1024,256]{2,1,0:T(8,128)(2,1)}, u32[]{:S(2)}) %copy-start.4) | copy-done | bytes 2621464
  142.4 1.7 %copy-done.6 = bf16[5,1024,256]{2,1,0:T(8,128)(2,1)S(1)} copy-done((bf16[5,1024,256]{2,1,0:T(8,128)(2,1)S(1)}, bf16[5,1024,256]{2,1,0:T(8,128)(2,1)}, u32[]{:S(2)}) %copy-start.6) | copy-done | bytes 2621464
  144.1 3.3 %zeta_lines.2 = (f32[5,128,128]{2,1,0:T(8,128)S(1)}, f32[5,128,128]{2,1,0:T(8,128)S(1)}, f32[5,128,128]{2,1,0:T(8,128)S(1)}, f32[5,128,128]{2,1,0:T(8,128)S(1)}) custom-call(f32[8,5,8,32,128]{4,3,2,1,0:T(8,128)S(1)} %bitcast.2, bf16[5,1024,256]{2,1,0:T(8,128)(2,1)S(1)} %copy-done.4, bf16[5,1024,256]{2,1,0:T(8,128)(2,1)S(1)} %copy-done.6), custom_call_target="tpu_custom_call" | custom-call | tf_op jit(solution)/shard_map/zeta_lines/pallas_call | solution.py:348
  147.5 2.0 %collective-permute-start.26 = (f32[5,128,128]{2,1,0:T(8,128)S(1)}, f32[5,128,128]{2,1,0:T(8,128)S(1)}, u32[]{:S(2)}, u32[]{:S(2)}) collective-permute-start(f32[5,128,128]{2,1,0:T(8,128)S(1)} %get-tuple-element.73), channel_id=1, source_target_pairs={{0,3},{1,0},{2,1},{3,2},{4,7},{5,4},{6,5},{7,6},{8,11},{9,8},{10,9... | collective-permute-start | bytes 983048 | tf_op jit(solution)/shard_map/ppermute | solution.py:415
  149.7 3.3 %collective-permute-start.24 = (f32[5,128,128]{2,1,0:T(8,128)S(1)}, f32[5,128,128]{2,1,0:T(8,128)S(1)}, u32[]{:S(2)}, u32[]{:S(2)}) collective-permute-start(f32[5,128,128]{2,1,0:T(8,128)S(1)} %add.6), channel_id=1, source_target_pairs={{0,1},{1,2},{2,3},{3,0},{4,5},{5,6},{6,7},{7,4},{8,9},{9,10},{10,1... | collective-permute-start | bytes 983048 | tf_op jit(solution)/shard_map/ppermute | solution.py:415
  153.0 4.0 %copy-done.1 = f32[5,128,4096]{2,1,0:T(8,128)S(1)} copy-done((f32[5,128,4096]{2,1,0:T(8,128)S(1)}, f32[5,128,4096]{2,1,0:T(8,128)}, u32[]{:S(2)}) %copy-start.1) | copy-done | bytes 10485784
  157.0 3.4 %own_lines.1 = (f32[5,128,128]{2,1,0:T(8,128)S(1)}, f32[5,128,128]{2,1,0:T(8,128)S(1)}) custom-call(f32[8,5,8,32,128]{4,3,2,1,0:T(8,128)S(1)} %bitcast.3, f32[5,128,4096]{2,1,0:T(8,128)S(1)} %copy-done.1), custom_call_target="tpu_custom_call" | custom-call | tf_op jit(solution)/shard_map/own_lines/pallas_call | solution.py:371
  160.4 4.3 %collective-permute-done.28.high1 = f32[5,128,128]{2,1,0:T(8,128)S(1)} collective-permute-done((f32[5,128,128]{2,1,0:T(8,128)S(1)}, f32[5,128,128]{2,1,0:T(8,128)S(1)}, u32[]{:S(2)}, u32[]{:S(2)}) %collective-permute-start.28) | collective-permute-done | bytes 327712 | tf_op jit(solution)/shard_map/ppermute | solution.py:415
  164.7 2.0 %final.1 = f32[5,8,32,128]{3,2,1,0:T(8,128)} custom-call(f32[4,5,5]{2,1,0:T(8,128)S(1)} %copy.14.t_ref, f32[5,8,32,128]{3,2,1,0:T(8,128)S(1)} %copy-done.2, f32[5,128,128]{2,1,0:T(8,128)S(1)} %get-tuple-element.76.own0, f32[5,128,128]{2,1,0:T(8,128)S(1)} %get-tuple-element.77.own1, f32[5,128,128]{2,1,0:T(8,128)S(1)} %collective-permute-done.24.low0, ...), custom_call_target="tpu_custom_call" | custom-call | tf_op jit(solution)/shard_map/final/pallas_call | solution.py:399
  (62 shorter events, 0.8 us)
Async XLA Ops:
  7.2 123.3 %all-gather.3.cloned.1.call-start = ((), (), s32[]{:S(2)}) async-start(), calls=%async_computation | async-start | bytes 5898240 | tf_op jit(solution)/shard_map/all_gather | solution.py:455
  9.2 15.4 %collective-permute-start = (f32[5,2,32,128]{3,2,1,0:T(8,128)}, f32[5,2,32,128]{3,2,1,0:T(8,128)S(1)}, u32[]{:S(2)}, u32[]{:S(2)}) collective-permute-start(f32[5,2,32,128]{3,2,1,0:T(8,128)} %get-tuple-element.43), channel_id=1, source_target_pairs={{0,64},{64,128},{128,192},{1,65},{65,129},{129,193},{2,66},{66,130... | collective-permute-start | bytes 491528 | tf_op jit(solution)/shard_map/ppermute | solution.py:425
  12.6 13.3 %collective-permute-start.1 = (f32[5,2,32,128]{3,2,1,0:T(8,128)}, f32[5,2,32,128]{3,2,1,0:T(8,128)S(1)}, u32[]{:S(2)}, u32[]{:S(2)}) collective-permute-start(f32[5,2,32,128]{3,2,1,0:T(8,128)} %get-tuple-element.46), channel_id=1, source_target_pairs={{64,0},{128,64},{192,128},{65,1},{129,65},{193,129},{66,2},{130,66... | collective-permute-start | bytes 491528 | tf_op jit(solution)/shard_map/ppermute | solution.py:425
  13.9 12.0 %collective-permute-start.2 = (f32[5,8,8,128]{3,2,1,0:T(8,128)}, f32[5,8,8,128]{3,2,1,0:T(8,128)S(1)}, u32[]{:S(2)}, u32[]{:S(2)}) collective-permute-start(f32[5,8,8,128]{3,2,1,0:T(8,128)} %get-tuple-element.47), channel_id=1, source_target_pairs={{0,32},{32,0},{1,33},{33,1},{2,34},{34,2},{3,35},{35,3},{4,36},{36... | collective-permute-start | bytes 491528 | tf_op jit(solution)/shard_map/ppermute | solution.py:419
  14.0 10.6 %collective-permute-start.3 = (f32[8,1280]{1,0:T(8,128)}, f32[8,1280]{1,0:T(8,128)S(1)}, u32[]{:S(2)}, u32[]{:S(2)}) collective-permute-start(f32[8,1280]{1,0:T(8,128)} %get-tuple-element.48), channel_id=1, source_target_pairs={{0,1},{1,2},{2,3},{3,4},{4,5},{5,6},{6,7},{7,8},{8,9},{9,10},{10,1... | collective-permute-start | bytes 122888 | tf_op jit(solution)/shard_map/ppermute | solution.py:425
  17.5 7.1 %copy-start.14 = (f32[4,5,5]{2,0,1:T(4,128)S(1)}, f32[4,5,5]{2,0,1:T(4,128)}, u32[]{:S(2)}) copy-start(f32[4,5,5]{2,0,1:T(4,128)} %param.12) | copy-start | bytes 1204
  17.5 8.4 %copy-start.2 = (f32[5,8,32,128]{3,2,1,0:T(8,128)S(1)}, f32[5,8,32,128]{3,2,1,0:T(8,128)}, u32[]{:S(2)}) copy-start(f32[5,8,32,128]{3,2,1,0:T(8,128)} %state.5) | copy-start | bytes 1966084
  17.5 8.4 %copy-start.9 = (f32[8,32,128]{2,1,0:T(8,128)S(1)}, f32[8,32,128]{2,1,0:T(8,128)}, u32[]{:S(2)}) copy-start(f32[8,32,128]{2,1,0:T(8,128)} %radius_hbm.1) | copy-start | bytes 393220
  17.5 8.4 %copy-start.10 = (s32[8,32,128]{2,1,0:T(8,128)S(1)}, s32[8,32,128]{2,1,0:T(8,128)}, u32[]{:S(2)}) copy-start(s32[8,32,128]{2,1,0:T(8,128)} %iblank_hbm.1) | copy-start | bytes 393220
  17.5 8.4 %copy-start.12 = (f32[5,8,32]{2,1,0:T(8,128)S(1)}, f32[5,8,32]{2,1,0:T(8,128)}, u32[]{:S(2)}) copy-start(f32[5,8,32]{2,1,0:T(8,128)} %inv_xi_hbm.1) | copy-start | bytes 15364
  17.6 8.4 %copy-start.13 = (f32[3,5]{1,0:T(4,128)S(1)}, f32[3,5]{1,0:T(4,128)}, u32[]{:S(2)}) copy-start(f32[3,5]{1,0:T(4,128)} %speeds.1) | copy-start | bytes 184
  17.6 8.3 %collective-permute-start.4 = (f32[8,1280]{1,0:T(8,128)}, f32[8,1280]{1,0:T(8,128)S(1)}, u32[]{:S(2)}, u32[]{:S(2)}) collective-permute-start(f32[8,1280]{1,0:T(8,128)} %get-tuple-element.49), channel_id=1, source_target_pairs={{1,0},{2,1},{3,2},{4,3},{5,4},{6,5},{7,6},{8,7},{9,8},{10,9},{11,1... | collective-permute-start | bytes 122888 | tf_op jit(solution)/shard_map/ppermute | solution.py:425
  24.6 5.2 %copy-start.16 = (f32[8,3,64,128]{3,2,1,0:T(8,128)S(1)}, f32[8,3,64,128]{3,2,1,0:T(8,128)}, u32[]{:S(2)}) copy-start(f32[8,3,64,128]{3,2,1,0:T(8,128)} %get-tuple-element.56) | copy-start | bytes 2359300
  24.6 34.1 %copy-start.11 = (f32[5,32,64]{2,1,0:T(8,128)S(1)}, f32[5,32,64]{2,1,0:T(8,128)}, u32[]{:S(2)}) copy-start(f32[5,32,64]{2,1,0:T(8,128)} %inv_eta.1) | copy-start | bytes 122884
  29.8 27.8 %collective-permute-start.8 = (f32[8,3,64,128]{3,2,1,0:T(8,128)S(1)}, f32[8,3,64,128]{3,2,1,0:T(8,128)S(1)}, u32[]{:S(2)}, u32[]{:S(2)}) collective-permute-start(f32[8,3,64,128]{3,2,1,0:T(8,128)S(1)} %copy-done.16), channel_id=1, source_target_pairs={{0,2},{1,3},{2,0},{3,1},{4,6},{5,7},{6,4},{7,5},{8,10},{9,11},{10,... | collective-permute-start | bytes 2359304 | tf_op jit(solution)/shard_map/ppermute | solution.py:415
  29.9 8.6 %collective-permute-start.5 = (f32[5,9,8,128]{3,2,1,0:T(8,128)S(1)}, f32[5,9,8,128]{3,2,1,0:T(8,128)S(1)}, u32[]{:S(2)}, u32[]{:S(2)}) collective-permute-start(f32[5,9,8,128]{3,2,1,0:T(8,128)S(1)} %get-tuple-element.52), channel_id=1, source_target_pairs={{0,64},{64,128},{128,192},{192,0},{1,65},{65,129},{129,193},{193,1... | collective-permute-start | bytes 552968 | tf_op jit(solution)/shard_map/ppermute | solution.py:410
  32.6 10.7 %collective-permute-start.6 = (f32[5,9,8,128]{3,2,1,0:T(8,128)S(1)}, f32[5,9,8,128]{3,2,1,0:T(8,128)S(1)}, u32[]{:S(2)}, u32[]{:S(2)}) collective-permute-start(f32[5,9,8,128]{3,2,1,0:T(8,128)S(1)} %get-tuple-element.53), channel_id=1, source_target_pairs={{0,128},{64,192},{128,0},{192,64},{1,129},{65,193},{129,1},{193,65... | collective-permute-start | bytes 552968 | tf_op jit(solution)/shard_map/ppermute | solution.py:410
  35.4 8.0 %collective-permute-start.7 = (f32[5,9,8,128]{3,2,1,0:T(8,128)S(1)}, f32[5,9,8,128]{3,2,1,0:T(8,128)S(1)}, u32[]{:S(2)}, u32[]{:S(2)}) collective-permute-start(f32[5,9,8,128]{3,2,1,0:T(8,128)S(1)} %get-tuple-element.54), channel_id=1, source_target_pairs={{0,192},{64,0},{128,64},{192,128},{1,193},{65,1},{129,65},{193,129... | collective-permute-start | bytes 552968 | tf_op jit(solution)/shard_map/ppermute | solution.py:410
  46.7 8.2 %collective-permute-start.9 = (f32[5,8,8,128]{3,2,1,0:T(8,128)S(1)}, f32[5,8,8,128]{3,2,1,0:T(8,128)S(1)}, u32[]{:S(2)}, u32[]{:S(2)}) collective-permute-start(f32[5,8,8,128]{3,2,1,0:T(8,128)S(1)} %get-tuple-element.58), channel_id=1, source_target_pairs={{0,64},{64,128},{128,192},{192,0},{1,65},{65,129},{129,193},{193,1... | collective-permute-start | bytes 491528 | tf_op jit(solution)/shard_map/ppermute | solution.py:410
  47.9 9.2 %collective-permute-start.10 = (f32[5,8,8,128]{3,2,1,0:T(8,128)S(1)}, f32[5,8,8,128]{3,2,1,0:T(8,128)S(1)}, u32[]{:S(2)}, u32[]{:S(2)}) collective-permute-start(f32[5,8,8,128]{3,2,1,0:T(8,128)S(1)} %get-tuple-element.59), channel_id=1, source_target_pairs={{0,128},{64,192},{128,0},{192,64},{1,129},{65,193},{129,1},{193,65... | collective-permute-start | bytes 491528 | tf_op jit(solution)/shard_map/ppermute | solution.py:410
  50.3 6.8 %collective-permute-start.11 = (f32[5,8,8,128]{3,2,1,0:T(8,128)S(1)}, f32[5,8,8,128]{3,2,1,0:T(8,128)S(1)}, u32[]{:S(2)}, u32[]{:S(2)}) collective-permute-start(f32[5,8,8,128]{3,2,1,0:T(8,128)S(1)} %get-tuple-element.60), channel_id=1, source_target_pairs={{0,192},{64,0},{128,64},{192,128},{1,193},{65,1},{129,65},{193,129... | collective-permute-start | bytes 491528 | tf_op jit(solution)/shard_map/ppermute | solution.py:410
  52.0 9.9 %copy-start.15 = (f32[8,5,64,128]{3,2,1,0:T(8,128)S(1)}, f32[8,5,64,128]{3,2,1,0:T(8,128)}, u32[]{:S(2)}) copy-start(f32[8,5,64,128]{3,2,1,0:T(8,128)} %get-tuple-element.64) | copy-start | bytes 3932164
  52.0 42.2 %copy-start.17 = (f32[8,2,64,128]{3,2,1,0:T(8,128)S(1)}, f32[8,2,64,128]{3,2,1,0:T(8,128)}, u32[]{:S(2)}) copy-start(f32[8,2,64,128]{3,2,1,0:T(8,128)} %get-tuple-element.62) | copy-start | bytes 1572868
  52.0 5.5 %collective-permute-start.12 = (f32[5,8,8,128]{3,2,1,0:T(8,128)S(1)}, f32[5,8,8,128]{3,2,1,0:T(8,128)S(1)}, u32[]{:S(2)}, u32[]{:S(2)}) collective-permute-start(f32[5,8,8,128]{3,2,1,0:T(8,128)S(1)} %get-tuple-element.57.p0), channel_id=1, source_target_pairs={{0,32},{32,0},{1,33},{33,1},{2,34},{34,2},{3,35},{35,3},{4,36},{36... | collective-permute-start | bytes 491528 | tf_op jit(solution)/shard_map/ppermute | solution.py:419
  54.9 2.7 %collective-permute-start.13 = (f32[5,8,8,128]{3,2,1,0:T(8,128)S(1)}, f32[5,8,8,128]{3,2,1,0:T(8,128)S(1)}, u32[]{:S(2)}, u32[]{:S(2)}) collective-permute-start(f32[5,8,8,128]{3,2,1,0:T(8,128)S(1)} %collective-permute-done.9.p1), channel_id=1, source_target_pairs={{0,32},{32,0},{1,33},{33,1},{2,34},{34,2},{3,35},{35,3},{4,36},{36... | collective-permute-start | bytes 491528 | tf_op jit(solution)/shard_map/ppermute | solution.py:419
  57.1 1.4 collective-permute-start.14
  57.1 1.6 collective-permute-start.15
  61.2 32.5 %collective-permute-start.18 = (f32[8,5,64,128]{3,2,1,0:T(8,128)}, f32[8,5,64,128]{3,2,1,0:T(8,128)S(1)}, u32[]{:S(2)}, u32[]{:S(2)}) collective-permute-start(f32[8,5,64,128]{3,2,1,0:T(8,128)} %get-tuple-element.66), channel_id=1, source_target_pairs={{0,3},{1,0},{2,1},{3,2},{4,7},{5,4},{6,5},{7,6},{8,11},{9,8},{10,9... | collective-permute-start | bytes 3932168 | tf_op jit(solution)/shard_map/ppermute | solution.py:415
  61.9 31.8 %collective-permute-start.17 = (f32[8,5,64,128]{3,2,1,0:T(8,128)S(1)}, f32[8,5,64,128]{3,2,1,0:T(8,128)S(1)}, u32[]{:S(2)}, u32[]{:S(2)}) collective-permute-start(f32[8,5,64,128]{3,2,1,0:T(8,128)S(1)} %copy-done.15), channel_id=1, source_target_pairs={{0,1},{1,2},{2,3},{3,0},{4,5},{5,6},{6,7},{7,4},{8,9},{9,10},{10,1... | collective-permute-start | bytes 3932168 | tf_op jit(solution)/shard_map/ppermute | solution.py:415
  93.7 17.9 %collective-permute-start.22 = (f32[8,5,64,128]{3,2,1,0:T(8,128)S(1)}, f32[8,5,64,128]{3,2,1,0:T(8,128)S(1)}, u32[]{:S(2)}, u32[]{:S(2)}) collective-permute-start(f32[8,5,64,128]{3,2,1,0:T(8,128)S(1)} %collective-permute-done.18.refs_3_), channel_id=1, source_target_pairs={{0,32},{32,0},{1,33},{33,1},{2,34},{34,2},{3,35},{35,3},{4,36},{36... | collective-permute-start | bytes 3932168 | tf_op jit(solution)/shard_map/ppermute | solution.py:419
  93.7 17.9 %collective-permute-start.21 = (f32[8,5,64,128]{3,2,1,0:T(8,128)S(1)}, f32[8,5,64,128]{3,2,1,0:T(8,128)S(1)}, u32[]{:S(2)}, u32[]{:S(2)}) collective-permute-start(f32[8,5,64,128]{3,2,1,0:T(8,128)S(1)} %collective-permute-done.17.refs_2_), channel_id=1, source_target_pairs={{0,32},{32,0},{1,33},{33,1},{2,34},{34,2},{3,35},{35,3},{4,36},{36... | collective-permute-start | bytes 3932168 | tf_op jit(solution)/shard_map/ppermute | solution.py:419
  94.2 15.4 %collective-permute-start.16 = (f32[8,2,64,128]{3,2,1,0:T(8,128)S(1)}, f32[8,2,64,128]{3,2,1,0:T(8,128)S(1)}, u32[]{:S(2)}, u32[]{:S(2)}) collective-permute-start(f32[8,2,64,128]{3,2,1,0:T(8,128)S(1)} %copy-done.17), channel_id=1, source_target_pairs={{0,2},{1,3},{2,0},{3,1},{4,6},{5,7},{6,4},{7,5},{8,10},{9,11},{10,... | collective-permute-start | bytes 1572872 | tf_op jit(solution)/shard_map/ppermute | solution.py:415
  95.8 13.8 %collective-permute-start.19 = (f32[8,3,64,128]{3,2,1,0:T(8,128)S(1)}, f32[8,3,64,128]{3,2,1,0:T(8,128)S(1)}, u32[]{:S(2)}, u32[]{:S(2)}) collective-permute-start(f32[8,3,64,128]{3,2,1,0:T(8,128)S(1)} %collective-permute-done.8.refs_0_), channel_id=1, source_target_pairs={{0,32},{32,0},{1,33},{33,1},{2,34},{34,2},{3,35},{35,3},{4,36},{36... | collective-permute-start | bytes 2359304 | tf_op jit(solution)/shard_map/ppermute | solution.py:419
  109.7 1.9 %collective-permute-start.20 = (f32[8,2,64,128]{3,2,1,0:T(8,128)S(1)}, f32[8,2,64,128]{3,2,1,0:T(8,128)S(1)}, u32[]{:S(2)}, u32[]{:S(2)}) collective-permute-start(f32[8,2,64,128]{3,2,1,0:T(8,128)S(1)} %collective-permute-done.16.refs_1_), channel_id=1, source_target_pairs={{0,32},{32,0},{1,33},{33,1},{2,34},{34,2},{3,35},{35,3},{4,36},{36... | collective-permute-start | bytes 1572872 | tf_op jit(solution)/shard_map/ppermute | solution.py:419
  116.4 1.5 copy-start.3
  117.9 1.6 copy-start.5
  119.5 1.1 copy-start.7
  120.6 1.1 copy-start.8
  130.4 10.2 %copy-start = (f32[40,8,32,128]{3,2,1,0:T(8,128)S(1)}, f32[40,8,32,128]{3,2,1,0:T(8,128)}, u32[]{:S(2)}) copy-start(f32[40,8,32,128]{3,2,1,0:T(8,128)} %all-gather.3.cloned.1.call-done) | copy-start | bytes 15728644
  137.4 12.1 %collective-permute-start.27 = (f32[5,128,128]{2,1,0:T(8,128)}, f32[5,128,128]{2,1,0:T(8,128)S(1)}, u32[]{:S(2)}, u32[]{:S(2)}) collective-permute-start(f32[5,128,128]{2,1,0:T(8,128)} %get-tuple-element.83), channel_id=1, source_target_pairs={{0,3},{1,0},{2,1},{3,2},{4,7},{5,4},{6,5},{7,6},{8,11},{9,8},{10,9... | collective-permute-start | bytes 983048 | tf_op jit(solution)/shard_map/ppermute | solution.py:415
  138.2 11.4 %collective-permute-start.23 = (f32[5,128,128]{2,1,0:T(8,128)}, f32[5,128,128]{2,1,0:T(8,128)S(1)}, u32[]{:S(2)}, u32[]{:S(2)}) collective-permute-start(f32[5,128,128]{2,1,0:T(8,128)} %get-tuple-element.81), channel_id=1, source_target_pairs={{0,1},{1,2},{2,3},{3,0},{4,5},{5,6},{6,7},{7,4},{8,9},{9,10},{10,1... | collective-permute-start | bytes 983048 | tf_op jit(solution)/shard_map/ppermute | solution.py:415
  140.6 1.7 %copy-start.4 = (bf16[5,1024,256]{2,1,0:T(8,128)(2,1)S(1)}, bf16[5,1024,256]{2,1,0:T(8,128)(2,1)}, u32[]{:S(2)}) copy-start(bf16[5,1024,256]{2,1,0:T(8,128)(2,1)} %copy-done.3) | copy-start | bytes 7864324
  142.4 1.7 %copy-start.6 = (bf16[5,1024,256]{2,1,0:T(8,128)(2,1)S(1)}, bf16[5,1024,256]{2,1,0:T(8,128)(2,1)}, u32[]{:S(2)}) copy-start(bf16[5,1024,256]{2,1,0:T(8,128)(2,1)} %copy-done.5) | copy-start | bytes 7864324
  147.4 13.0 %collective-permute-start.25 = (f32[5,128,128]{2,1,0:T(8,128)S(1)}, f32[5,128,128]{2,1,0:T(8,128)S(1)}, u32[]{:S(2)}, u32[]{:S(2)}) collective-permute-start(f32[5,128,128]{2,1,0:T(8,128)S(1)} %get-tuple-element.74), channel_id=1, source_target_pairs={{0,1},{1,2},{2,3},{3,0},{4,5},{5,6},{6,7},{7,4},{8,9},{9,10},{10,1... | collective-permute-start | bytes 983048 | tf_op jit(solution)/shard_map/ppermute | solution.py:415
  147.5 12.9 %collective-permute-start.26 = (f32[5,128,128]{2,1,0:T(8,128)S(1)}, f32[5,128,128]{2,1,0:T(8,128)S(1)}, u32[]{:S(2)}, u32[]{:S(2)}) collective-permute-start(f32[5,128,128]{2,1,0:T(8,128)S(1)} %get-tuple-element.73), channel_id=1, source_target_pairs={{0,3},{1,0},{2,1},{3,2},{4,7},{5,4},{6,5},{7,6},{8,11},{9,8},{10,9... | collective-permute-start | bytes 983048 | tf_op jit(solution)/shard_map/ppermute | solution.py:415
  149.6 15.1 %collective-permute-start.28 = (f32[5,128,128]{2,1,0:T(8,128)S(1)}, f32[5,128,128]{2,1,0:T(8,128)S(1)}, u32[]{:S(2)}, u32[]{:S(2)}) collective-permute-start(f32[5,128,128]{2,1,0:T(8,128)S(1)} %add.7), channel_id=1, source_target_pairs={{0,3},{1,0},{2,1},{3,2},{4,7},{5,4},{6,5},{7,6},{8,11},{9,8},{10,9... | collective-permute-start | bytes 983048 | tf_op jit(solution)/shard_map/ppermute | solution.py:415
  149.7 15.0 %collective-permute-start.24 = (f32[5,128,128]{2,1,0:T(8,128)S(1)}, f32[5,128,128]{2,1,0:T(8,128)S(1)}, u32[]{:S(2)}, u32[]{:S(2)}) collective-permute-start(f32[5,128,128]{2,1,0:T(8,128)S(1)} %add.6), channel_id=1, source_target_pairs={{0,1},{1,2},{2,3},{3,0},{4,5},{5,6},{6,7},{7,4},{8,9},{9,10},{10,1... | collective-permute-start | bytes 983048 | tf_op jit(solution)/shard_map/ppermute | solution.py:415
  153.0 4.0 %copy-start.1 = (f32[5,128,4096]{2,1,0:T(8,128)S(1)}, f32[5,128,4096]{2,1,0:T(8,128)}, u32[]{:S(2)}) copy-start(f32[5,128,4096]{2,1,0:T(8,128)} %inv.2) | copy-start | bytes 31457284
Sparse Core Ops, SparseCore 0:
  61.4 69.0 all-gather.2

commit v3 on v1

--- a/solution.py
+++ b/solution.py
@@ -331,30 +331,46 @@
     )(*own_parts, *other_parts)
 
 
-def zeta_kernel(count, b_ref, *refs):
-    b = split(jnp.concatenate([b_ref[z, 0].reshape(256, 128) for z in range(NZC)], axis=1))
-    outs = list(refs[2 * count :])
-    for high, low in zip(refs[0 : 2 * count : 2], refs[1 : 2 * count : 2]):
-        value = dot3(b, (high[0], low[0]))
-        for place in range(high.shape[2] // 128):
-            lanes = slice(128 * place, 128 * (place + 1))
-            outs.pop(0)[0] = value[:128, lanes]
-            outs.pop(0)[0] = value[128:, lanes]
-
-
-def zeta_step(gathered, *lines):
-    widths = [array.shape[2] for array in lines]
-    count = sum(widths) // 128
-    return pl.pallas_call(
-        functools.partial(zeta_kernel, len(lines) // 2),
-        grid=(5,),
-        in_specs=[pl.BlockSpec((NZC, 1, 8, 32, 128), lambda v: (0, v, 0, 0, 0))]
-        + [pl.BlockSpec((1, 1024, w), lambda v: (v, 0, 0)) for w in widths],
-        out_specs=[pl.BlockSpec((1, 128, 128), lambda v: (v, 0, 0))] * count,
+def zeta_kernel(gathered, high_hbm, low_hbm, *refs):
+    *outs, field, high, low, sems = refs
+    copies = []
+    for v in range(5):
+        pairs = (
+            (gathered.at[:, v], field.at[:, v]),
+            (high_hbm.at[v], high.at[v]),
+            (low_hbm.at[v], low.at[v]),
+        )
+        copies.append([
+            pltpu.make_async_copy(*pair, sems.at[v, n]) for n, pair in enumerate(pairs)
+        ])
+        for copy in copies[-1]:
+            copy.start()
+    for v in range(5):
+        for copy in copies[v]:
+            copy.wait()
+        lines = [field[z, v].reshape(256, 128) for z in range(NZC)]
+        value = dot3(split(jnp.concatenate(lines, axis=1)), (high[v], low[v]))
+        for n, out in enumerate(outs):
+            half, place = n % 2, n // 2
+            out[v] = value[128 * half : 128 * (half + 1), 128 * place : 128 * (place + 1)]
+
+
+def zeta_step(gathered, high, low):
+    count = 2 * (high.shape[2] // 128)
+    return pl.pallas_call(
+        zeta_kernel,
+        in_specs=[HBM] * 3,
+        out_specs=[VMEM] * count,
         out_shape=[shape(5, 128, 128)] * count,
+        scratch_shapes=[
+            pltpu.VMEM(gathered.shape, F32),
+            pltpu.VMEM(high.shape, BF16),
+            pltpu.VMEM(low.shape, BF16),
+            pltpu.SemaphoreType.DMA((5, 3)),
+        ],
         compiler_params=pltpu.CompilerParams(vmem_limit_bytes=56 << 20),
         name="zeta_lines",
-    )(gathered, *lines)
+    )(gathered, high, low)
 
 
 def own_kernel(b_ref, inv, out0, out1):

time: 175 us -> 173 us (0.989)
  Pallas kernels: 40.9 us -> 38.8 us
    pallas_call x2, Pallas kernels: 14.5 us -> 12.4 us  [zeta_step(): pl.pallas_call(zeta_kernel, in_specs=[HBM] * 3, out_specs=[VMEM] * count,...]
  transfers between devices with their start and end apart: 30 -> 30, of which waited for: 12 -> 12; matrix products, arithmetic and copies ran while one was open for 1% -> 1% of each run, Pallas kernels for 14% -> 13%
where the time goes in v3:
time: 173 us
  waiting for transfers between devices  70.1 us (41%)
  Pallas kernels  38.8 us (22%)
  starting transfers between devices  38.1 us (22%)
  between operations  14.4 us (8%)
  local copies, waits for them, and re-layouts  9.38 us (5%)
  other arithmetic  2.02 us (1%)
    ppermute x10, waiting for transfers between devices, over_y(): return lax.ppermute(array, 'zeta', pairs)  45.5 us
    ppermute x10, starting transfers between devices, over_y(): return lax.ppermute(array, 'zeta', pairs)  13.8 us
    pallas_call x2, Pallas kernels, zeta_step(): pl.pallas_call(zeta_kernel, in_specs=[HBM] * 3, out_specs=[VMEM] * count,...  12.4 us
    ppermute x6, starting transfers between devices, over_x(): return lax.ppermute(array, 'xi', [(i, (i + s) % 4) for i in range(4)])  12.2 us
    ppermute x6, waiting for transfers between devices, over_x(): return lax.ppermute(array, 'xi', [(i, (i + s) % 4) for i in range(4)])  11.6 us
    ppermute x4, starting transfers between devices, shift_line(): return lax.ppermute(array, axis, pairs)  10.7 us
    unnamed x35, local copies, waits for them, and re-layouts  9.38 us
    all_gather x1, waiting for transfers between devices, local(): gathered = lax.all_gather(work, 'zeta', axis_index_groups=columns)  8.69 us
  transfers between devices with their start and end apart: 30, of which 12 were waited for; matrix products, arithmetic and copies ran while one was open for 1% of the time, Pallas kernels for 13%

profile of v3, /device:TPU:24, one launch (start us, length us, event | category | flops | bytes accessed | tf_op | source)
XLA Modules:
  0.0 172.8 jit_solution(12889787510466651731)
XLA Ops:
  7.2 2.0 %faces.1 = (f32[5,2,32,128]{3,2,1,0:T(8,128)}, f32[5,2,32,128]{3,2,1,0:T(8,128)}, f32[5,8,8,128]{3,2,1,0:T(8,128)}, f32[8,1280]{1,0:T(8,128)}, f32[8,1280]{1,0:T(8,128)}) custom-call(f32[5,8,32,128]{3,2,1,0:T(8,128)} %state.5), custom_call_target="tpu_custom_call" | custom-call | tf_op jit(solution)/shard_map/faces/pallas_call | solution.py:70
  9.2 3.4 %collective-permute-start = (f32[5,2,32,128]{3,2,1,0:T(8,128)}, f32[5,2,32,128]{3,2,1,0:T(8,128)S(1)}, u32[]{:S(2)}, u32[]{:S(2)}) collective-permute-start(f32[5,2,32,128]{3,2,1,0:T(8,128)} %get-tuple-element.43), channel_id=1, source_target_pairs={{0,64},{64,128},{128,192},{1,65},{65,129},{129,193},{2,66},{66,130... | collective-permute-start | bytes 491528 | tf_op jit(solution)/shard_map/ppermute | solution.py:441
  12.6 1.3 collective-permute-start.1
  14.0 3.5 %collective-permute-start.3 = (f32[8,1280]{1,0:T(8,128)}, f32[8,1280]{1,0:T(8,128)S(1)}, u32[]{:S(2)}, u32[]{:S(2)}) collective-permute-start(f32[8,1280]{1,0:T(8,128)} %get-tuple-element.48), channel_id=1, source_target_pairs={{0,1},{1,2},{2,3},{3,4},{4,5},{5,6},{6,7},{7,8},{8,9},{9,10},{10,1... | collective-permute-start | bytes 122888 | tf_op jit(solution)/shard_map/ppermute | solution.py:441
  17.6 2.5 %collective-permute-start.4 = (f32[8,1280]{1,0:T(8,128)}, f32[8,1280]{1,0:T(8,128)S(1)}, u32[]{:S(2)}, u32[]{:S(2)}) collective-permute-start(f32[8,1280]{1,0:T(8,128)} %get-tuple-element.49), channel_id=1, source_target_pairs={{1,0},{2,1},{3,2},{4,3},{5,4},{6,5},{7,6},{8,7},{9,8},{10,9},{11,1... | collective-permute-start | bytes 122888 | tf_op jit(solution)/shard_map/ppermute | solution.py:441
  20.1 4.5 %pick.1 = (f32[8,3,64,128]{3,2,1,0:T(8,128)}, f32[8,2,64,128]{3,2,1,0:T(8,128)}, f32[8,5,64,128]{3,2,1,0:T(8,128)}, f32[8,5,64,128]{3,2,1,0:T(8,128)}) custom-call(f32[5,128,4096]{2,1,0:T(8,128)} %inv.2), custom_call_target="tpu_custom_call" | custom-call | tf_op jit(solution)/shard_map/pick/pallas_call | solution.py:276
  24.6 1.3 collective-permute-done.4.znext
  26.0 3.8 %residual.1 = (f32[5,8,32,128]{3,2,1,0:T(8,128)}, f32[5,9,8,128]{3,2,1,0:T(8,128)S(1)}, f32[5,9,8,128]{3,2,1,0:T(8,128)S(1)}, f32[5,9,8,128]{3,2,1,0:T(8,128)S(1)}, f32[5,9,8,128]{3,2,1,0:T(8,128)S(1)}) custom-call(f32[3,5]{1,0:T(4,128)S(1)} %copy-done.10, f32[4,5,5]{2,1,0:T(8,128)S(1)} %copy.14.t_ref, f32[5,8,32,128]{3,2,1,0:T(8,128)S(1)} %copy-done.1, ...), custom_call_target="tpu_custom_call" | custom-call | tf_op jit(solution)/shard_map/residual/pallas_call | solution.py:156
  29.9 2.7 %collective-permute-start.5 = (f32[5,9,8,128]{3,2,1,0:T(8,128)S(1)}, f32[5,9,8,128]{3,2,1,0:T(8,128)S(1)}, u32[]{:S(2)}, u32[]{:S(2)}) collective-permute-start(f32[5,9,8,128]{3,2,1,0:T(8,128)S(1)} %get-tuple-element.52), channel_id=1, source_target_pairs={{0,64},{64,128},{128,192},{192,0},{1,65},{65,129},{129,193},{193,1... | collective-permute-start | bytes 552968 | tf_op jit(solution)/shard_map/ppermute | solution.py:426
  32.6 2.7 %collective-permute-start.6 = (f32[5,9,8,128]{3,2,1,0:T(8,128)S(1)}, f32[5,9,8,128]{3,2,1,0:T(8,128)S(1)}, u32[]{:S(2)}, u32[]{:S(2)}) collective-permute-start(f32[5,9,8,128]{3,2,1,0:T(8,128)S(1)} %get-tuple-element.53), channel_id=1, source_target_pairs={{0,128},{64,192},{128,0},{192,64},{1,129},{65,193},{129,1},{193,65... | collective-permute-start | bytes 552968 | tf_op jit(solution)/shard_map/ppermute | solution.py:426
  35.4 1.4 collective-permute-start.7
  36.8 1.8 %collective-permute-done.5.r1 = f32[5,9,8,128]{3,2,1,0:T(8,128)S(1)} collective-permute-done((f32[5,9,8,128]{3,2,1,0:T(8,128)S(1)}, f32[5,9,8,128]{3,2,1,0:T(8,128)S(1)}, u32[]{:S(2)}, u32[]{:S(2)}) %collective-permute-start.5) | collective-permute-done | bytes 184352 | tf_op jit(solution)/shard_map/ppermute | solution.py:426
  38.5 4.8 %collective-permute-done.6.r2 = f32[5,9,8,128]{3,2,1,0:T(8,128)S(1)} collective-permute-done((f32[5,9,8,128]{3,2,1,0:T(8,128)S(1)}, f32[5,9,8,128]{3,2,1,0:T(8,128)S(1)}, u32[]{:S(2)}, u32[]{:S(2)}) %collective-permute-start.6) | collective-permute-done | bytes 184352 | tf_op jit(solution)/shard_map/ppermute | solution.py:426
  43.4 3.3 %xi_lines.1 = (f32[5,8,8,128]{3,2,1,0:T(8,128)S(1)}, f32[5,8,8,128]{3,2,1,0:T(8,128)S(1)}, f32[5,8,8,128]{3,2,1,0:T(8,128)S(1)}, f32[5,8,8,128]{3,2,1,0:T(8,128)S(1)}) custom-call(f32[4,5,5]{2,1,0:T(8,128)S(1)} %copy.14.t_ref, f32[5,9,8,128]{3,2,1,0:T(8,128)S(1)} %get-tuple-element.51.r0, f32[5,9,8,128]{3,2,1,0:T(8,128)S(1)} %collective-permute-done.5.r1, ...), custom_call_target="tpu_custom_call" | custom-call | tf_op jit(solution)/shard_map/xi_lines/pallas_call | solution.py:209
  46.7 1.2 collective-permute-start.9
  47.9 2.4 %collective-permute-start.10 = (f32[5,8,8,128]{3,2,1,0:T(8,128)S(1)}, f32[5,8,8,128]{3,2,1,0:T(8,128)S(1)}, u32[]{:S(2)}, u32[]{:S(2)}) collective-permute-start(f32[5,8,8,128]{3,2,1,0:T(8,128)S(1)} %get-tuple-element.59), channel_id=1, source_target_pairs={{0,128},{64,192},{128,0},{192,64},{1,129},{65,193},{129,1},{193,65... | collective-permute-start | bytes 491528 | tf_op jit(solution)/shard_map/ppermute | solution.py:426
  50.3 1.8 %collective-permute-start.11 = (f32[5,8,8,128]{3,2,1,0:T(8,128)S(1)}, f32[5,8,8,128]{3,2,1,0:T(8,128)S(1)}, u32[]{:S(2)}, u32[]{:S(2)}) collective-permute-start(f32[5,8,8,128]{3,2,1,0:T(8,128)S(1)} %get-tuple-element.60), channel_id=1, source_target_pairs={{0,192},{64,0},{128,64},{192,128},{1,193},{65,1},{129,65},{193,129... | collective-permute-start | bytes 491528 | tf_op jit(solution)/shard_map/ppermute | solution.py:426
  52.1 2.8 %collective-permute-done.9.p1 = f32[5,8,8,128]{3,2,1,0:T(8,128)S(1)} collective-permute-done((f32[5,8,8,128]{3,2,1,0:T(8,128)S(1)}, f32[5,8,8,128]{3,2,1,0:T(8,128)S(1)}, u32[]{:S(2)}, u32[]{:S(2)}) %collective-permute-start.9) | collective-permute-done | bytes 163872 | tf_op jit(solution)/shard_map/ppermute | solution.py:426
  54.8 2.3 %collective-permute-done.10.p2 = f32[5,8,8,128]{3,2,1,0:T(8,128)S(1)} collective-permute-done((f32[5,8,8,128]{3,2,1,0:T(8,128)S(1)}, f32[5,8,8,128]{3,2,1,0:T(8,128)S(1)}, u32[]{:S(2)}, u32[]{:S(2)}) %collective-permute-start.10) | collective-permute-done | bytes 163872 | tf_op jit(solution)/shard_map/ppermute | solution.py:426
  57.1 0.5 collective-permute-start.15
  57.6 0.9 collective-permute-done.14.q2
  58.5 0.2 collective-permute-done.15.q3
  58.7 2.5 %eta_lines.1 = f32[5,8,32,128]{3,2,1,0:T(8,128)} custom-call(f32[4,5,5]{2,1,0:T(8,128)S(1)} %copy.14.t_ref, f32[5,32,64]{2,1,0:T(8,128)S(1)} %copy-done.8, f32[5,8,8,128]{3,2,1,0:T(8,128)S(1)} %get-tuple-element.57.p0, f32[5,8,8,128]{3,2,1,0:T(8,128)S(1)} %collective-permute-done.9.p1, f32[5,8,8,128]{3,2,1,0:T(8,128)S(1)} %collective-permute-done.10.p2, ...), custom_call_target="tpu_custom_call" | custom-call | tf_op jit(solution)/shard_map/eta_lines/pallas_call | solution.py:246
  61.3 0.6 collective-permute-start.18
  61.9 2.7 %collective-permute-start.17 = (f32[8,5,64,128]{3,2,1,0:T(8,128)S(1)}, f32[8,5,64,128]{3,2,1,0:T(8,128)S(1)}, u32[]{:S(2)}, u32[]{:S(2)}) collective-permute-start(f32[8,5,64,128]{3,2,1,0:T(8,128)S(1)} %copy-done.12), channel_id=1, source_target_pairs={{0,1},{1,2},{2,3},{3,0},{4,5},{5,6},{6,7},{7,4},{8,9},{9,10},{10,1... | collective-permute-start | bytes 3932168 | tf_op jit(solution)/shard_map/ppermute | solution.py:431
  64.6 29.1 %collective-permute-done.18.refs_3_ = f32[8,5,64,128]{3,2,1,0:T(8,128)S(1)} collective-permute-done((f32[8,5,64,128]{3,2,1,0:T(8,128)}, f32[8,5,64,128]{3,2,1,0:T(8,128)S(1)}, u32[]{:S(2)}, u32[]{:S(2)}) %collective-permute-start.18) | collective-permute-done | bytes 1310752 | tf_op jit(solution)/shard_map/ppermute | solution.py:431
  93.8 0.5 collective-permute-start.21
  94.3 1.6 collective-permute-start.16
  96.1 13.6 %collective-permute-done.16.refs_1_ = f32[8,2,64,128]{3,2,1,0:T(8,128)S(1)} collective-permute-done((f32[8,2,64,128]{3,2,1,0:T(8,128)S(1)}, f32[8,2,64,128]{3,2,1,0:T(8,128)S(1)}, u32[]{:S(2)}, u32[]{:S(2)}) %collective-permute-start.16) | collective-permute-done | bytes 524320 | tf_op jit(solution)/shard_map/ppermute | solution.py:431
  109.7 1.9 %collective-permute-done.20.refs_5_ = f32[8,2,64,128]{3,2,1,0:T(8,128)S(1)} collective-permute-done((f32[8,2,64,128]{3,2,1,0:T(8,128)S(1)}, f32[8,2,64,128]{3,2,1,0:T(8,128)S(1)}, u32[]{:S(2)}, u32[]{:S(2)}) %collective-permute-start.20) | collective-permute-done | bytes 524320 | tf_op jit(solution)/shard_map/ppermute | solution.py:435
  111.6 4.8 %prepare.1 = (bf16[5,1024,128]{2,1,0:T(8,128)(2,1)S(1)}, bf16[5,1024,128]{2,1,0:T(8,128)(2,1)S(1)}, bf16[5,1024,256]{2,1,0:T(8,128)(2,1)S(1)}, bf16[5,1024,256]{2,1,0:T(8,128)(2,1)S(1)}) custom-call(f32[8,3,64,128]{3,2,1,0:T(8,128)S(1)} %collective-permute-done.8.refs_0_, f32[8,2,64,128]{3,2,1,0:T(8,128)S(1)} %collective-permute-done.16.refs_1_, ...), custom_call_target="tpu_custom_call" | custom-call | tf_op jit(solution)/shard_map/prepare/pallas_call | solution.py:322
  116.4 1.5 copy-done.2
  118.0 1.6 copy-done.3
  119.6 1.1 copy-done.4
  120.6 1.1 copy-done.5
  121.8 8.7 %all-gather.3.cloned.1.call-done = f32[40,8,32,128]{3,2,1,0:T(8,128)} async-done(((f32[5,8,32,128]{3,2,1,0:T(8,128)}), f32[40,8,32,128]{3,2,1,0:T(8,128)}) %all-gather.3.cloned.1.call-update) | async-done | bytes 5242896 | tf_op jit(solution)/shard_map/all_gather | solution.py:471
  130.5 5.2 %zeta_lines.3 = (f32[5,128,128]{2,1,0:T(8,128)}, f32[5,128,128]{2,1,0:T(8,128)}) custom-call(f32[8,5,8,32,128]{4,3,2,1,0:T(8,128)} %bitcast.1, bf16[5,1024,128]{2,1,0:T(8,128)(2,1)} %copy-done.4, bf16[5,1024,128]{2,1,0:T(8,128)(2,1)} %copy-done.5), custom_call_target="tpu_custom_call" | custom-call | tf_op jit(solution)/shard_map/zeta_lines/pallas_call | solution.py:360
  135.6 0.9 collective-permute-start.27
  136.5 2.4 %collective-permute-start.23 = (f32[5,128,128]{2,1,0:T(8,128)}, f32[5,128,128]{2,1,0:T(8,128)S(1)}, u32[]{:S(2)}, u32[]{:S(2)}) collective-permute-start(f32[5,128,128]{2,1,0:T(8,128)} %get-tuple-element.81), channel_id=1, source_target_pairs={{0,1},{1,2},{2,3},{3,0},{4,5},{5,6},{6,7},{7,4},{8,9},{9,10},{10,1... | collective-permute-start | bytes 983048 | tf_op jit(solution)/shard_map/ppermute | solution.py:431
  138.9 7.3 %zeta_lines.2 = (f32[5,128,128]{2,1,0:T(8,128)}, f32[5,128,128]{2,1,0:T(8,128)}, f32[5,128,128]{2,1,0:T(8,128)}, f32[5,128,128]{2,1,0:T(8,128)}) custom-call(f32[8,5,8,32,128]{4,3,2,1,0:T(8,128)} %bitcast.2, bf16[5,1024,256]{2,1,0:T(8,128)(2,1)} %copy-done.2, bf16[5,1024,256]{2,1,0:T(8,128)(2,1)} %copy-done.3), custom_call_target="tpu_custom_call" | custom-call | tf_op jit(solution)/shard_map/zeta_lines/pallas_call | solution.py:360
  146.3 2.0 %collective-permute-start.26 = (f32[5,128,128]{2,1,0:T(8,128)}, f32[5,128,128]{2,1,0:T(8,128)S(1)}, u32[]{:S(2)}, u32[]{:S(2)}) collective-permute-start(f32[5,128,128]{2,1,0:T(8,128)} %get-tuple-element.73), channel_id=1, source_target_pairs={{0,3},{1,0},{2,1},{3,2},{4,7},{5,4},{6,5},{7,6},{8,11},{9,8},{10,9... | collective-permute-start | bytes 983048 | tf_op jit(solution)/shard_map/ppermute | solution.py:431
  148.3 1.0 add.7
  149.4 1.0 add.6
  150.5 3.3 %collective-permute-start.24 = (f32[5,128,128]{2,1,0:T(8,128)S(1)}, f32[5,128,128]{2,1,0:T(8,128)S(1)}, u32[]{:S(2)}, u32[]{:S(2)}) collective-permute-start(f32[5,128,128]{2,1,0:T(8,128)S(1)} %add.6), channel_id=1, source_target_pairs={{0,1},{1,2},{2,3},{3,0},{4,5},{5,6},{6,7},{7,4},{8,9},{9,10},{10,1... | collective-permute-start | bytes 983048 | tf_op jit(solution)/shard_map/ppermute | solution.py:431
  153.8 4.0 %copy-done = f32[5,128,4096]{2,1,0:T(8,128)S(1)} copy-done((f32[5,128,4096]{2,1,0:T(8,128)S(1)}, f32[5,128,4096]{2,1,0:T(8,128)}, u32[]{:S(2)}) %copy-start) | copy-done | bytes 10485784
  157.7 3.4 %own_lines.1 = (f32[5,128,128]{2,1,0:T(8,128)S(1)}, f32[5,128,128]{2,1,0:T(8,128)S(1)}) custom-call(f32[8,5,8,32,128]{4,3,2,1,0:T(8,128)S(1)} %bitcast.5, f32[5,128,4096]{2,1,0:T(8,128)S(1)} %copy-done), custom_call_target="tpu_custom_call" | custom-call | tf_op jit(solution)/shard_map/own_lines/pallas_call | solution.py:387
  161.2 2.8 %collective-permute-done.28.high1 = f32[5,128,128]{2,1,0:T(8,128)S(1)} collective-permute-done((f32[5,128,128]{2,1,0:T(8,128)S(1)}, f32[5,128,128]{2,1,0:T(8,128)S(1)}, u32[]{:S(2)}, u32[]{:S(2)}) %collective-permute-start.28) | collective-permute-done | bytes 327712 | tf_op jit(solution)/shard_map/ppermute | solution.py:431
  164.0 2.0 %final.1 = f32[5,8,32,128]{3,2,1,0:T(8,128)} custom-call(f32[4,5,5]{2,1,0:T(8,128)S(1)} %copy.14.t_ref, f32[5,8,32,128]{3,2,1,0:T(8,128)S(1)} %copy-done.1, f32[5,128,128]{2,1,0:T(8,128)S(1)} %get-tuple-element.76.own0, f32[5,128,128]{2,1,0:T(8,128)S(1)} %get-tuple-element.77.own1, f32[5,128,128]{2,1,0:T(8,128)S(1)} %collective-permute-done.24.low0, ...), custom_call_target="tpu_custom_call" | custom-call | tf_op jit(solution)/shard_map/final/pallas_call | solution.py:415
  (61 shorter events, 0.8 us)
Async XLA Ops:
  7.2 123.3 %all-gather.3.cloned.1.call-start = ((), (), s32[]{:S(2)}) async-start(), calls=%async_computation | async-start | bytes 5898240 | tf_op jit(solution)/shard_map/all_gather | solution.py:471
  9.2 15.4 %collective-permute-start = (f32[5,2,32,128]{3,2,1,0:T(8,128)}, f32[5,2,32,128]{3,2,1,0:T(8,128)S(1)}, u32[]{:S(2)}, u32[]{:S(2)}) collective-permute-start(f32[5,2,32,128]{3,2,1,0:T(8,128)} %get-tuple-element.43), channel_id=1, source_target_pairs={{0,64},{64,128},{128,192},{1,65},{65,129},{129,193},{2,66},{66,130... | collective-permute-start | bytes 491528 | tf_op jit(solution)/shard_map/ppermute | solution.py:441
  12.6 13.3 %collective-permute-start.1 = (f32[5,2,32,128]{3,2,1,0:T(8,128)}, f32[5,2,32,128]{3,2,1,0:T(8,128)S(1)}, u32[]{:S(2)}, u32[]{:S(2)}) collective-permute-start(f32[5,2,32,128]{3,2,1,0:T(8,128)} %get-tuple-element.46), channel_id=1, source_target_pairs={{64,0},{128,64},{192,128},{65,1},{129,65},{193,129},{66,2},{130,66... | collective-permute-start | bytes 491528 | tf_op jit(solution)/shard_map/ppermute | solution.py:441
  13.9 12.0 %collective-permute-start.2 = (f32[5,8,8,128]{3,2,1,0:T(8,128)}, f32[5,8,8,128]{3,2,1,0:T(8,128)S(1)}, u32[]{:S(2)}, u32[]{:S(2)}) collective-permute-start(f32[5,8,8,128]{3,2,1,0:T(8,128)} %get-tuple-element.47), channel_id=1, source_target_pairs={{0,32},{32,0},{1,33},{33,1},{2,34},{34,2},{3,35},{35,3},{4,36},{36... | collective-permute-start | bytes 491528 | tf_op jit(solution)/shard_map/ppermute | solution.py:435
  14.0 10.6 %collective-permute-start.3 = (f32[8,1280]{1,0:T(8,128)}, f32[8,1280]{1,0:T(8,128)S(1)}, u32[]{:S(2)}, u32[]{:S(2)}) collective-permute-start(f32[8,1280]{1,0:T(8,128)} %get-tuple-element.48), channel_id=1, source_target_pairs={{0,1},{1,2},{2,3},{3,4},{4,5},{5,6},{6,7},{7,8},{8,9},{9,10},{10,1... | collective-permute-start | bytes 122888 | tf_op jit(solution)/shard_map/ppermute | solution.py:441
  17.5 7.1 %copy-start.11 = (f32[4,5,5]{2,0,1:T(4,128)S(1)}, f32[4,5,5]{2,0,1:T(4,128)}, u32[]{:S(2)}) copy-start(f32[4,5,5]{2,0,1:T(4,128)} %param.12) | copy-start | bytes 1204
  17.5 8.4 %copy-start.1 = (f32[5,8,32,128]{3,2,1,0:T(8,128)S(1)}, f32[5,8,32,128]{3,2,1,0:T(8,128)}, u32[]{:S(2)}) copy-start(f32[5,8,32,128]{3,2,1,0:T(8,128)} %state.5) | copy-start | bytes 1966084
  17.5 8.4 %copy-start.6 = (f32[8,32,128]{2,1,0:T(8,128)S(1)}, f32[8,32,128]{2,1,0:T(8,128)}, u32[]{:S(2)}) copy-start(f32[8,32,128]{2,1,0:T(8,128)} %radius_hbm.1) | copy-start | bytes 393220
  17.5 8.4 %copy-start.7 = (s32[8,32,128]{2,1,0:T(8,128)S(1)}, s32[8,32,128]{2,1,0:T(8,128)}, u32[]{:S(2)}) copy-start(s32[8,32,128]{2,1,0:T(8,128)} %iblank_hbm.1) | copy-start | bytes 393220
  17.5 8.4 %copy-start.9 = (f32[5,8,32]{2,1,0:T(8,128)S(1)}, f32[5,8,32]{2,1,0:T(8,128)}, u32[]{:S(2)}) copy-start(f32[5,8,32]{2,1,0:T(8,128)} %inv_xi_hbm.1) | copy-start | bytes 15364
  17.6 8.4 %copy-start.10 = (f32[3,5]{1,0:T(4,128)S(1)}, f32[3,5]{1,0:T(4,128)}, u32[]{:S(2)}) copy-start(f32[3,5]{1,0:T(4,128)} %speeds.1) | copy-start | bytes 184
  17.6 8.3 %collective-permute-start.4 = (f32[8,1280]{1,0:T(8,128)}, f32[8,1280]{1,0:T(8,128)S(1)}, u32[]{:S(2)}, u32[]{:S(2)}) collective-permute-start(f32[8,1280]{1,0:T(8,128)} %get-tuple-element.49), channel_id=1, source_target_pairs={{1,0},{2,1},{3,2},{4,3},{5,4},{6,5},{7,6},{8,7},{9,8},{10,9},{11,1... | collective-permute-start | bytes 122888 | tf_op jit(solution)/shard_map/ppermute | solution.py:441
  24.6 5.2 %copy-start.13 = (f32[8,3,64,128]{3,2,1,0:T(8,128)S(1)}, f32[8,3,64,128]{3,2,1,0:T(8,128)}, u32[]{:S(2)}) copy-start(f32[8,3,64,128]{3,2,1,0:T(8,128)} %get-tuple-element.56) | copy-start | bytes 2359300
  24.6 34.1 %copy-start.8 = (f32[5,32,64]{2,1,0:T(8,128)S(1)}, f32[5,32,64]{2,1,0:T(8,128)}, u32[]{:S(2)}) copy-start(f32[5,32,64]{2,1,0:T(8,128)} %inv_eta.1) | copy-start | bytes 122884
  29.8 27.8 %collective-permute-start.8 = (f32[8,3,64,128]{3,2,1,0:T(8,128)S(1)}, f32[8,3,64,128]{3,2,1,0:T(8,128)S(1)}, u32[]{:S(2)}, u32[]{:S(2)}) collective-permute-start(f32[8,3,64,128]{3,2,1,0:T(8,128)S(1)} %copy-done.13), channel_id=1, source_target_pairs={{0,2},{1,3},{2,0},{3,1},{4,6},{5,7},{6,4},{7,5},{8,10},{9,11},{10,... | collective-permute-start | bytes 2359304 | tf_op jit(solution)/shard_map/ppermute | solution.py:431
  29.9 8.6 %collective-permute-start.5 = (f32[5,9,8,128]{3,2,1,0:T(8,128)S(1)}, f32[5,9,8,128]{3,2,1,0:T(8,128)S(1)}, u32[]{:S(2)}, u32[]{:S(2)}) collective-permute-start(f32[5,9,8,128]{3,2,1,0:T(8,128)S(1)} %get-tuple-element.52), channel_id=1, source_target_pairs={{0,64},{64,128},{128,192},{192,0},{1,65},{65,129},{129,193},{193,1... | collective-permute-start | bytes 552968 | tf_op jit(solution)/shard_map/ppermute | solution.py:426
  32.6 10.7 %collective-permute-start.6 = (f32[5,9,8,128]{3,2,1,0:T(8,128)S(1)}, f32[5,9,8,128]{3,2,1,0:T(8,128)S(1)}, u32[]{:S(2)}, u32[]{:S(2)}) collective-permute-start(f32[5,9,8,128]{3,2,1,0:T(8,128)S(1)} %get-tuple-element.53), channel_id=1, source_target_pairs={{0,128},{64,192},{128,0},{192,64},{1,129},{65,193},{129,1},{193,65... | collective-permute-start | bytes 552968 | tf_op jit(solution)/shard_map/ppermute | solution.py:426
  35.4 8.0 %collective-permute-start.7 = (f32[5,9,8,128]{3,2,1,0:T(8,128)S(1)}, f32[5,9,8,128]{3,2,1,0:T(8,128)S(1)}, u32[]{:S(2)}, u32[]{:S(2)}) collective-permute-start(f32[5,9,8,128]{3,2,1,0:T(8,128)S(1)} %get-tuple-element.54), channel_id=1, source_target_pairs={{0,192},{64,0},{128,64},{192,128},{1,193},{65,1},{129,65},{193,129... | collective-permute-start | bytes 552968 | tf_op jit(solution)/shard_map/ppermute | solution.py:426
  46.7 8.1 %collective-permute-start.9 = (f32[5,8,8,128]{3,2,1,0:T(8,128)S(1)}, f32[5,8,8,128]{3,2,1,0:T(8,128)S(1)}, u32[]{:S(2)}, u32[]{:S(2)}) collective-permute-start(f32[5,8,8,128]{3,2,1,0:T(8,128)S(1)} %get-tuple-element.58), channel_id=1, source_target_pairs={{0,64},{64,128},{128,192},{192,0},{1,65},{65,129},{129,193},{193,1... | collective-permute-start | bytes 491528 | tf_op jit(solution)/shard_map/ppermute | solution.py:426
  47.9 9.2 %collective-permute-start.10 = (f32[5,8,8,128]{3,2,1,0:T(8,128)S(1)}, f32[5,8,8,128]{3,2,1,0:T(8,128)S(1)}, u32[]{:S(2)}, u32[]{:S(2)}) collective-permute-start(f32[5,8,8,128]{3,2,1,0:T(8,128)S(1)} %get-tuple-element.59), channel_id=1, source_target_pairs={{0,128},{64,192},{128,0},{192,64},{1,129},{65,193},{129,1},{193,65... | collective-permute-start | bytes 491528 | tf_op jit(solution)/shard_map/ppermute | solution.py:426
  50.3 6.8 %collective-permute-start.11 = (f32[5,8,8,128]{3,2,1,0:T(8,128)S(1)}, f32[5,8,8,128]{3,2,1,0:T(8,128)S(1)}, u32[]{:S(2)}, u32[]{:S(2)}) collective-permute-start(f32[5,8,8,128]{3,2,1,0:T(8,128)S(1)} %get-tuple-element.60), channel_id=1, source_target_pairs={{0,192},{64,0},{128,64},{192,128},{1,193},{65,1},{129,65},{193,129... | collective-permute-start | bytes 491528 | tf_op jit(solution)/shard_map/ppermute | solution.py:426
  52.1 9.9 %copy-start.12 = (f32[8,5,64,128]{3,2,1,0:T(8,128)S(1)}, f32[8,5,64,128]{3,2,1,0:T(8,128)}, u32[]{:S(2)}) copy-start(f32[8,5,64,128]{3,2,1,0:T(8,128)} %get-tuple-element.64) | copy-start | bytes 3932164
  52.1 42.2 %copy-start.14 = (f32[8,2,64,128]{3,2,1,0:T(8,128)S(1)}, f32[8,2,64,128]{3,2,1,0:T(8,128)}, u32[]{:S(2)}) copy-start(f32[8,2,64,128]{3,2,1,0:T(8,128)} %get-tuple-element.62) | copy-start | bytes 1572868
  52.1 5.6 %collective-permute-start.12 = (f32[5,8,8,128]{3,2,1,0:T(8,128)S(1)}, f32[5,8,8,128]{3,2,1,0:T(8,128)S(1)}, u32[]{:S(2)}, u32[]{:S(2)}) collective-permute-start(f32[5,8,8,128]{3,2,1,0:T(8,128)S(1)} %get-tuple-element.57.p0), channel_id=1, source_target_pairs={{0,32},{32,0},{1,33},{33,1},{2,34},{34,2},{3,35},{35,3},{4,36},{36... | collective-permute-start | bytes 491528 | tf_op jit(solution)/shard_map/ppermute | solution.py:435
  54.8 2.8 %collective-permute-start.13 = (f32[5,8,8,128]{3,2,1,0:T(8,128)S(1)}, f32[5,8,8,128]{3,2,1,0:T(8,128)S(1)}, u32[]{:S(2)}, u32[]{:S(2)}) collective-permute-start(f32[5,8,8,128]{3,2,1,0:T(8,128)S(1)} %collective-permute-done.9.p1), channel_id=1, source_target_pairs={{0,32},{32,0},{1,33},{33,1},{2,34},{34,2},{3,35},{35,3},{4,36},{36... | collective-permute-start | bytes 491528 | tf_op jit(solution)/shard_map/ppermute | solution.py:435
  57.1 1.4 collective-permute-start.14
  57.1 1.6 collective-permute-start.15
  61.3 32.5 %collective-permute-start.18 = (f32[8,5,64,128]{3,2,1,0:T(8,128)}, f32[8,5,64,128]{3,2,1,0:T(8,128)S(1)}, u32[]{:S(2)}, u32[]{:S(2)}) collective-permute-start(f32[8,5,64,128]{3,2,1,0:T(8,128)} %get-tuple-element.66), channel_id=1, source_target_pairs={{0,3},{1,0},{2,1},{3,2},{4,7},{5,4},{6,5},{7,6},{8,11},{9,8},{10,9... | collective-permute-start | bytes 3932168 | tf_op jit(solution)/shard_map/ppermute | solution.py:431
  61.9 31.8 %collective-permute-start.17 = (f32[8,5,64,128]{3,2,1,0:T(8,128)S(1)}, f32[8,5,64,128]{3,2,1,0:T(8,128)S(1)}, u32[]{:S(2)}, u32[]{:S(2)}) collective-permute-start(f32[8,5,64,128]{3,2,1,0:T(8,128)S(1)} %copy-done.12), channel_id=1, source_target_pairs={{0,1},{1,2},{2,3},{3,0},{4,5},{5,6},{6,7},{7,4},{8,9},{9,10},{10,1... | collective-permute-start | bytes 3932168 | tf_op jit(solution)/shard_map/ppermute | solution.py:431
  93.7 17.9 %collective-permute-start.22 = (f32[8,5,64,128]{3,2,1,0:T(8,128)S(1)}, f32[8,5,64,128]{3,2,1,0:T(8,128)S(1)}, u32[]{:S(2)}, u32[]{:S(2)}) collective-permute-start(f32[8,5,64,128]{3,2,1,0:T(8,128)S(1)} %collective-permute-done.18.refs_3_), channel_id=1, source_target_pairs={{0,32},{32,0},{1,33},{33,1},{2,34},{34,2},{3,35},{35,3},{4,36},{36... | collective-permute-start | bytes 3932168 | tf_op jit(solution)/shard_map/ppermute | solution.py:435
  93.8 17.9 %collective-permute-start.21 = (f32[8,5,64,128]{3,2,1,0:T(8,128)S(1)}, f32[8,5,64,128]{3,2,1,0:T(8,128)S(1)}, u32[]{:S(2)}, u32[]{:S(2)}) collective-permute-start(f32[8,5,64,128]{3,2,1,0:T(8,128)S(1)} %collective-permute-done.17.refs_2_), channel_id=1, source_target_pairs={{0,32},{32,0},{1,33},{33,1},{2,34},{34,2},{3,35},{35,3},{4,36},{36... | collective-permute-start | bytes 3932168 | tf_op jit(solution)/shard_map/ppermute | solution.py:435
  94.3 15.4 %collective-permute-start.16 = (f32[8,2,64,128]{3,2,1,0:T(8,128)S(1)}, f32[8,2,64,128]{3,2,1,0:T(8,128)S(1)}, u32[]{:S(2)}, u32[]{:S(2)}) collective-permute-start(f32[8,2,64,128]{3,2,1,0:T(8,128)S(1)} %copy-done.14), channel_id=1, source_target_pairs={{0,2},{1,3},{2,0},{3,1},{4,6},{5,7},{6,4},{7,5},{8,10},{9,11},{10,... | collective-permute-start | bytes 1572872 | tf_op jit(solution)/shard_map/ppermute | solution.py:431
  95.9 13.8 %collective-permute-start.19 = (f32[8,3,64,128]{3,2,1,0:T(8,128)S(1)}, f32[8,3,64,128]{3,2,1,0:T(8,128)S(1)}, u32[]{:S(2)}, u32[]{:S(2)}) collective-permute-start(f32[8,3,64,128]{3,2,1,0:T(8,128)S(1)} %collective-permute-done.8.refs_0_), channel_id=1, source_target_pairs={{0,32},{32,0},{1,33},{33,1},{2,34},{34,2},{3,35},{35,3},{4,36},{36... | collective-permute-start | bytes 2359304 | tf_op jit(solution)/shard_map/ppermute | solution.py:435
  109.7 1.9 %collective-permute-start.20 = (f32[8,2,64,128]{3,2,1,0:T(8,128)S(1)}, f32[8,2,64,128]{3,2,1,0:T(8,128)S(1)}, u32[]{:S(2)}, u32[]{:S(2)}) collective-permute-start(f32[8,2,64,128]{3,2,1,0:T(8,128)S(1)} %collective-permute-done.16.refs_1_), channel_id=1, source_target_pairs={{0,32},{32,0},{1,33},{33,1},{2,34},{34,2},{3,35},{35,3},{4,36},{36... | collective-permute-start | bytes 1572872 | tf_op jit(solution)/shard_map/ppermute | solution.py:435
  116.4 1.6 copy-start.2
  118.0 1.6 copy-start.3
  119.6 1.1 copy-start.4
  120.6 1.1 copy-start.5
  135.6 12.7 %collective-permute-start.27 = (f32[5,128,128]{2,1,0:T(8,128)}, f32[5,128,128]{2,1,0:T(8,128)S(1)}, u32[]{:S(2)}, u32[]{:S(2)}) collective-permute-start(f32[5,128,128]{2,1,0:T(8,128)} %get-tuple-element.83), channel_id=1, source_target_pairs={{0,3},{1,0},{2,1},{3,2},{4,7},{5,4},{6,5},{7,6},{8,11},{9,8},{10,9... | collective-permute-start | bytes 983048 | tf_op jit(solution)/shard_map/ppermute | solution.py:431
  136.5 12.9 %collective-permute-start.23 = (f32[5,128,128]{2,1,0:T(8,128)}, f32[5,128,128]{2,1,0:T(8,128)S(1)}, u32[]{:S(2)}, u32[]{:S(2)}) collective-permute-start(f32[5,128,128]{2,1,0:T(8,128)} %get-tuple-element.81), channel_id=1, source_target_pairs={{0,1},{1,2},{2,3},{3,0},{4,5},{5,6},{6,7},{7,4},{8,9},{9,10},{10,1... | collective-permute-start | bytes 983048 | tf_op jit(solution)/shard_map/ppermute | solution.py:431
  138.9 14.8 %slice-start = ((s8[5242880]{0:T(1024)(128)(4,1)}), s8[4194304]{0:T(1024)(128)(4,1)S(1)}, s32[]{:S(2)}) async-start(s8[5242880]{0:T(1024)(128)(4,1)} %bitcast.3), calls=%async_computation.1 | async-start | bytes 8388608
  138.9 14.8 %slice-start.1 = ((s8[5242880]{0:T(1024)(128)(4,1)}), s8[1048576]{0:T(1024)(128)(4,1)S(1)}, s32[]{:S(2)}) async-start(s8[5242880]{0:T(1024)(128)(4,1)} %bitcast.3), calls=%async_computation.2 | async-start | bytes 2097152
  146.2 14.9 %collective-permute-start.25 = (f32[5,128,128]{2,1,0:T(8,128)}, f32[5,128,128]{2,1,0:T(8,128)S(1)}, u32[]{:S(2)}, u32[]{:S(2)}) collective-permute-start(f32[5,128,128]{2,1,0:T(8,128)} %get-tuple-element.74), channel_id=1, source_target_pairs={{0,1},{1,2},{2,3},{3,0},{4,5},{5,6},{6,7},{7,4},{8,9},{9,10},{10,1... | collective-permute-start | bytes 983048 | tf_op jit(solution)/shard_map/ppermute | solution.py:431
  146.3 14.9 %collective-permute-start.26 = (f32[5,128,128]{2,1,0:T(8,128)}, f32[5,128,128]{2,1,0:T(8,128)S(1)}, u32[]{:S(2)}, u32[]{:S(2)}) collective-permute-start(f32[5,128,128]{2,1,0:T(8,128)} %get-tuple-element.73), channel_id=1, source_target_pairs={{0,3},{1,0},{2,1},{3,2},{4,7},{5,4},{6,5},{7,6},{8,11},{9,8},{10,9... | collective-permute-start | bytes 983048 | tf_op jit(solution)/shard_map/ppermute | solution.py:431
  149.3 14.6 %collective-permute-start.28 = (f32[5,128,128]{2,1,0:T(8,128)S(1)}, f32[5,128,128]{2,1,0:T(8,128)S(1)}, u32[]{:S(2)}, u32[]{:S(2)}) collective-permute-start(f32[5,128,128]{2,1,0:T(8,128)S(1)} %add.7), channel_id=1, source_target_pairs={{0,3},{1,0},{2,1},{3,2},{4,7},{5,4},{6,5},{7,6},{8,11},{9,8},{10,9... | collective-permute-start | bytes 983048 | tf_op jit(solution)/shard_map/ppermute | solution.py:431
  150.5 13.5 %collective-permute-start.24 = (f32[5,128,128]{2,1,0:T(8,128)S(1)}, f32[5,128,128]{2,1,0:T(8,128)S(1)}, u32[]{:S(2)}, u32[]{:S(2)}) collective-permute-start(f32[5,128,128]{2,1,0:T(8,128)S(1)} %add.6), channel_id=1, source_target_pairs={{0,1},{1,2},{2,3},{3,0},{4,5},{5,6},{6,7},{7,4},{8,9},{9,10},{10,1... | collective-permute-start | bytes 983048 | tf_op jit(solution)/shard_map/ppermute | solution.py:431
  153.8 4.0 %copy-start = (f32[5,128,4096]{2,1,0:T(8,128)S(1)}, f32[5,128,4096]{2,1,0:T(8,128)}, u32[]{:S(2)}) copy-start(f32[5,128,4096]{2,1,0:T(8,128)} %inv.2) | copy-start | bytes 31457284
Sparse Core Ops, SparseCore 0:
  61.4 69.0 all-gather.2

commit v4 on v3

--- a/solution.py
+++ b/solution.py
@@ -13,6 +13,7 @@
 HBM = pl.BlockSpec(memory_space=pltpu.HBM)
 VMEM = pl.BlockSpec()
 NZC, NYC = 8, 4
+SHIFTS = (0, 2, 1, 3)
 PICKED_STEP = (2, 2, 1, 3)
 PICKED_FIRST = (0, 3, 0, 0)
 PICKED_COUNT = (3, 2, 5, 5)
@@ -146,7 +147,7 @@
         return carry
 
     lax.fori_loop(0, 8, body, 0)
-    for s, m in enumerate((m0, m1, m2, m3)):
+    for s, m in zip(SHIFTS, (m0, m1, m2, m3)):
         start = pl.multiple_of(8 * lax.rem(xi + s, 4), 8)
         m[:, 0:8] = w0[:, :, pl.ds(start, 8), :]
         m[:, 8] = jnp.concatenate([inv_xi[...], jnp.zeros((5, 8, 96), F32)], axis=2)
@@ -174,7 +175,7 @@
 
 def xi_kernel(t_ref, r0, r1, r2, r3, b0, b1, b2, b3, field, inverse, work):
     xi, _, _, _ = position()
-    for s, r in enumerate((r0, r1, r2, r3)):
+    for s, r in zip(SHIFTS, (r0, r1, r2, r3)):
         start = pl.multiple_of(8 * lax.rem(xi + 4 - s, 4), 8)
         field[:, pl.ds(start, 8)] = r[:, 0:8]
         inverse[:, pl.ds(start, 8), :] = r[:, 8]
@@ -201,7 +202,7 @@
         return carry
 
     lax.fori_loop(0, 32, body, 0)
-    for s, b in enumerate((b0, b1, b2, b3)):
+    for s, b in zip(SHIFTS, (b0, b1, b2, b3)):
         b[...] = field[:, pl.ds(8 * lax.rem(xi + s, 4), 8)]
 
 
@@ -223,7 +224,7 @@
 
 def eta_kernel(t_ref, inv_eta, p0, p1, p2, p3, q0, q1, q2, q3, out, field, work):
     xi, eta, _, _ = position()
-    for s, (p, q) in enumerate(zip((p0, p1, p2, p3), (q0, q1, q2, q3))):
+    for s, p, q in zip(SHIFTS, (p0, p1, p2, p3), (q0, q1, q2, q3)):
         rows = 8 * lax.rem(xi + 4 - s, 4)
         field[:, :, pl.ds(pl.multiple_of(32 * eta + rows, 8), 8), :] = p[...]
         field[:, :, pl.ds(pl.multiple_of(32 * (1 - eta) + rows, 8), 8), :] = q[...]
@@ -456,13 +457,15 @@
     ]
     picked = pick(inv_zeta)
     halos[0] = after(halos[0], picked[0])
-    residual, m0, m1, m2, m3 = residual_step(
+    residual, m0, m2, m1, m3 = residual_step(
         speeds, transforms, state, radius, iblank, inv_xi, *halos
     )
-    parts = [m0] + [over_x(m, s + 1) for s, m in enumerate((m1, m2, m3))]
+    r2, r1, r3 = over_x(m2, 2), over_x(m1, 1), over_x(m3, 3)
+    parts = [m0, r2, r1, r3]
     sent = [over_y(after(picked[0], m0), PICKED_STEP[0])]
-    b0, b1, b2, b3 = xi_step(transforms, parts)
-    own = [b0] + [over_x(b, s + 1) for s, b in enumerate((b1, b2, b3))]
+    b0, b2, b1, b3 = xi_step(transforms, parts)
+    p2, p1, p3 = over_x(b2, 2), over_x(b1, 1), over_x(b3, 3)
+    own = [b0, p2, p1, p3]
     other = [over_core(p) for p in own]
     own[0] = after(own[0], *sent)
     work = eta_step(transforms, inv_eta, own, other)

time: 173 us -> 173 us (level)
  transfers between devices with their start and end apart: 30 -> 30, of which waited for: 12 -> 14; matrix products, arithmetic and copies ran while one was open for 1% -> 1% of each run, Pallas kernels for 13% -> 14%
where the time goes in v4:
time: 173 us
  waiting for transfers between devices  69.5 us (40%)
  Pallas kernels  38.8 us (22%)
  starting transfers between devices  38.5 us (22%)
  between operations  14.4 us (8%)
  local copies, waits for them, and re-layouts  9.38 us (5%)
  other arithmetic  2.02 us (1%)
    ppermute x10, waiting for transfers between devices, over_y(): return lax.ppermute(array, 'zeta', pairs)  45.5 us
    ppermute x10, starting transfers between devices, over_y(): return lax.ppermute(array, 'zeta', pairs)  13.8 us
    ppermute x6, starting transfers between devices, over_x(): return lax.ppermute(array, 'xi', [(i, (i + s) % 4) for i in range(4)])  12.9 us
    pallas_call x2, Pallas kernels, zeta_step(): pl.pallas_call(zeta_kernel, in_specs=[HBM] * 3, out_specs=[VMEM] * count,...  12.4 us
    ppermute x4, starting transfers between devices, shift_line(): return lax.ppermute(array, axis, pairs)  10.7 us
    ppermute x6, waiting for transfers between devices, over_x(): return lax.ppermute(array, 'xi', [(i, (i + s) % 4) for i in range(4)])  10.3 us
    unnamed x35, local copies, waits for them, and re-layouts  9.38 us
    all_gather x1, waiting for transfers between devices, local(): gathered = lax.all_gather(work, 'zeta', axis_index_groups=columns)  9.34 us
  transfers between devices with their start and end apart: 30, of which 14 were waited for; matrix products, arithmetic and copies ran while one was open for 1% of the time, Pallas kernels for 14%

profile of v4, /device:TPU:24, one launch (start us, length us, event | category | flops | bytes accessed | tf_op | source)
XLA Modules:
  0.0 172.6 jit_solution(608575583481694520)
XLA Ops:
  7.2 2.0 %faces.1 = (f32[5,2,32,128]{3,2,1,0:T(8,128)}, f32[5,2,32,128]{3,2,1,0:T(8,128)}, f32[5,8,8,128]{3,2,1,0:T(8,128)}, f32[8,1280]{1,0:T(8,128)}, f32[8,1280]{1,0:T(8,128)}) custom-call(f32[5,8,32,128]{3,2,1,0:T(8,128)} %state.5), custom_call_target="tpu_custom_call" | custom-call | tf_op jit(solution)/shard_map/faces/pallas_call | solution.py:71
  9.2 3.4 %collective-permute-start = (f32[5,2,32,128]{3,2,1,0:T(8,128)}, f32[5,2,32,128]{3,2,1,0:T(8,128)S(1)}, u32[]{:S(2)}, u32[]{:S(2)}) collective-permute-start(f32[5,2,32,128]{3,2,1,0:T(8,128)} %get-tuple-element.43), channel_id=1, source_target_pairs={{0,64},{64,128},{128,192},{1,65},{65,129},{129,193},{2,66},{66,130... | collective-permute-start | bytes 491528 | tf_op jit(solution)/shard_map/ppermute | solution.py:442
  12.6 1.3 collective-permute-start.1
  14.0 3.5 %collective-permute-start.3 = (f32[8,1280]{1,0:T(8,128)}, f32[8,1280]{1,0:T(8,128)S(1)}, u32[]{:S(2)}, u32[]{:S(2)}) collective-permute-start(f32[8,1280]{1,0:T(8,128)} %get-tuple-element.48), channel_id=1, source_target_pairs={{0,1},{1,2},{2,3},{3,4},{4,5},{5,6},{6,7},{7,8},{8,9},{9,10},{10,1... | collective-permute-start | bytes 122888 | tf_op jit(solution)/shard_map/ppermute | solution.py:442
  17.6 2.5 %collective-permute-start.4 = (f32[8,1280]{1,0:T(8,128)}, f32[8,1280]{1,0:T(8,128)S(1)}, u32[]{:S(2)}, u32[]{:S(2)}) collective-permute-start(f32[8,1280]{1,0:T(8,128)} %get-tuple-element.49), channel_id=1, source_target_pairs={{1,0},{2,1},{3,2},{4,3},{5,4},{6,5},{7,6},{8,7},{9,8},{10,9},{11,1... | collective-permute-start | bytes 122888 | tf_op jit(solution)/shard_map/ppermute | solution.py:442
  20.1 4.5 %pick.1 = (f32[8,3,64,128]{3,2,1,0:T(8,128)}, f32[8,2,64,128]{3,2,1,0:T(8,128)}, f32[8,5,64,128]{3,2,1,0:T(8,128)}, f32[8,5,64,128]{3,2,1,0:T(8,128)}) custom-call(f32[5,128,4096]{2,1,0:T(8,128)} %inv.2), custom_call_target="tpu_custom_call" | custom-call | tf_op jit(solution)/shard_map/pick/pallas_call | solution.py:277
  24.6 1.3 collective-permute-done.4.znext
  26.0 3.8 %residual.1 = (f32[5,8,32,128]{3,2,1,0:T(8,128)}, f32[5,9,8,128]{3,2,1,0:T(8,128)S(1)}, f32[5,9,8,128]{3,2,1,0:T(8,128)S(1)}, f32[5,9,8,128]{3,2,1,0:T(8,128)S(1)}, f32[5,9,8,128]{3,2,1,0:T(8,128)S(1)}) custom-call(f32[3,5]{1,0:T(4,128)S(1)} %copy-done.10, f32[4,5,5]{2,1,0:T(8,128)S(1)} %copy.14.t_ref, f32[5,8,32,128]{3,2,1,0:T(8,128)S(1)} %copy-done.1, ...), custom_call_target="tpu_custom_call" | custom-call | tf_op jit(solution)/shard_map/residual/pallas_call | solution.py:157
  29.9 4.3 %collective-permute-start.5 = (f32[5,9,8,128]{3,2,1,0:T(8,128)S(1)}, f32[5,9,8,128]{3,2,1,0:T(8,128)S(1)}, u32[]{:S(2)}, u32[]{:S(2)}) collective-permute-start(f32[5,9,8,128]{3,2,1,0:T(8,128)S(1)} %get-tuple-element.52), channel_id=1, source_target_pairs={{0,128},{64,192},{128,0},{192,64},{1,129},{65,193},{129,1},{193,65... | collective-permute-start | bytes 552968 | tf_op jit(solution)/shard_map/ppermute | solution.py:427
  34.2 0.6 collective-permute-start.6
  34.8 2.6 %collective-permute-start.7 = (f32[5,9,8,128]{3,2,1,0:T(8,128)S(1)}, f32[5,9,8,128]{3,2,1,0:T(8,128)S(1)}, u32[]{:S(2)}, u32[]{:S(2)}) collective-permute-start(f32[5,9,8,128]{3,2,1,0:T(8,128)S(1)} %get-tuple-element.54), channel_id=1, source_target_pairs={{0,192},{64,0},{128,64},{192,128},{1,193},{65,1},{129,65},{193,129... | collective-permute-start | bytes 552968 | tf_op jit(solution)/shard_map/ppermute | solution.py:427
  37.4 2.3 %collective-permute-done.5.r1 = f32[5,9,8,128]{3,2,1,0:T(8,128)S(1)} collective-permute-done((f32[5,9,8,128]{3,2,1,0:T(8,128)S(1)}, f32[5,9,8,128]{3,2,1,0:T(8,128)S(1)}, u32[]{:S(2)}, u32[]{:S(2)}) %collective-permute-start.5) | collective-permute-done | bytes 184352 | tf_op jit(solution)/shard_map/ppermute | solution.py:427
  39.7 2.8 %collective-permute-done.6.r2 = f32[5,9,8,128]{3,2,1,0:T(8,128)S(1)} collective-permute-done((f32[5,9,8,128]{3,2,1,0:T(8,128)S(1)}, f32[5,9,8,128]{3,2,1,0:T(8,128)S(1)}, u32[]{:S(2)}, u32[]{:S(2)}) %collective-permute-start.6) | collective-permute-done | bytes 184352 | tf_op jit(solution)/shard_map/ppermute | solution.py:427
  42.4 0.3 collective-permute-done.7.r3
  42.8 3.3 %xi_lines.1 = (f32[5,8,8,128]{3,2,1,0:T(8,128)S(1)}, f32[5,8,8,128]{3,2,1,0:T(8,128)S(1)}, f32[5,8,8,128]{3,2,1,0:T(8,128)S(1)}, f32[5,8,8,128]{3,2,1,0:T(8,128)S(1)}) custom-call(f32[4,5,5]{2,1,0:T(8,128)S(1)} %copy.14.t_ref, f32[5,9,8,128]{3,2,1,0:T(8,128)S(1)} %get-tuple-element.51.r0, f32[5,9,8,128]{3,2,1,0:T(8,128)S(1)} %collective-permute-done.5.r1, ...), custom_call_target="tpu_custom_call" | custom-call | tf_op jit(solution)/shard_map/xi_lines/pallas_call | solution.py:210
  46.1 2.2 %collective-permute-start.9 = (f32[5,8,8,128]{3,2,1,0:T(8,128)S(1)}, f32[5,8,8,128]{3,2,1,0:T(8,128)S(1)}, u32[]{:S(2)}, u32[]{:S(2)}) collective-permute-start(f32[5,8,8,128]{3,2,1,0:T(8,128)S(1)} %get-tuple-element.58), channel_id=1, source_target_pairs={{0,128},{64,192},{128,0},{192,64},{1,129},{65,193},{129,1},{193,65... | collective-permute-start | bytes 491528 | tf_op jit(solution)/shard_map/ppermute | solution.py:427
  48.2 1.6 collective-permute-start.10
  49.8 1.7 collective-permute-start.11
  51.5 2.5 %collective-permute-done.9.p1 = f32[5,8,8,128]{3,2,1,0:T(8,128)S(1)} collective-permute-done((f32[5,8,8,128]{3,2,1,0:T(8,128)S(1)}, f32[5,8,8,128]{3,2,1,0:T(8,128)S(1)}, u32[]{:S(2)}, u32[]{:S(2)}) %collective-permute-start.9) | collective-permute-done | bytes 163872 | tf_op jit(solution)/shard_map/ppermute | solution.py:427
  54.0 2.2 %collective-permute-done.10.p2 = f32[5,8,8,128]{3,2,1,0:T(8,128)S(1)} collective-permute-done((f32[5,8,8,128]{3,2,1,0:T(8,128)S(1)}, f32[5,8,8,128]{3,2,1,0:T(8,128)S(1)}, u32[]{:S(2)}, u32[]{:S(2)}) %collective-permute-start.10) | collective-permute-done | bytes 163872 | tf_op jit(solution)/shard_map/ppermute | solution.py:427
  56.4 0.3 collective-permute-start.15
  56.7 0.9 collective-permute-done.14.q2
  57.8 2.5 %eta_lines.1 = f32[5,8,32,128]{3,2,1,0:T(8,128)} custom-call(f32[4,5,5]{2,1,0:T(8,128)S(1)} %copy.14.t_ref, f32[5,32,64]{2,1,0:T(8,128)S(1)} %copy-done.8, f32[5,8,8,128]{3,2,1,0:T(8,128)S(1)} %get-tuple-element.57.p0, f32[5,8,8,128]{3,2,1,0:T(8,128)S(1)} %collective-permute-done.9.p1, f32[5,8,8,128]{3,2,1,0:T(8,128)S(1)} %collective-permute-done.10.p2, ...), custom_call_target="tpu_custom_call" | custom-call | tf_op jit(solution)/shard_map/eta_lines/pallas_call | solution.py:247
  60.4 0.4 collective-permute-start.18
  60.8 2.9 %collective-permute-start.17 = (f32[8,5,64,128]{3,2,1,0:T(8,128)S(1)}, f32[8,5,64,128]{3,2,1,0:T(8,128)S(1)}, u32[]{:S(2)}, u32[]{:S(2)}) collective-permute-start(f32[8,5,64,128]{3,2,1,0:T(8,128)S(1)} %copy-done.12), channel_id=1, source_target_pairs={{0,1},{1,2},{2,3},{3,0},{4,5},{5,6},{6,7},{7,4},{8,9},{9,10},{10,1... | collective-permute-start | bytes 3932168 | tf_op jit(solution)/shard_map/ppermute | solution.py:432
  63.7 29.1 %collective-permute-done.18.refs_3_ = f32[8,5,64,128]{3,2,1,0:T(8,128)S(1)} collective-permute-done((f32[8,5,64,128]{3,2,1,0:T(8,128)}, f32[8,5,64,128]{3,2,1,0:T(8,128)S(1)}, u32[]{:S(2)}, u32[]{:S(2)}) %collective-permute-start.18) | collective-permute-done | bytes 1310752 | tf_op jit(solution)/shard_map/ppermute | solution.py:432
  92.9 0.5 collective-permute-start.21
  93.4 1.6 collective-permute-start.16
  95.2 13.6 %collective-permute-done.16.refs_1_ = f32[8,2,64,128]{3,2,1,0:T(8,128)S(1)} collective-permute-done((f32[8,2,64,128]{3,2,1,0:T(8,128)S(1)}, f32[8,2,64,128]{3,2,1,0:T(8,128)S(1)}, u32[]{:S(2)}, u32[]{:S(2)}) %collective-permute-start.16) | collective-permute-done | bytes 524320 | tf_op jit(solution)/shard_map/ppermute | solution.py:432
  108.8 1.9 %collective-permute-done.20.refs_5_ = f32[8,2,64,128]{3,2,1,0:T(8,128)S(1)} collective-permute-done((f32[8,2,64,128]{3,2,1,0:T(8,128)S(1)}, f32[8,2,64,128]{3,2,1,0:T(8,128)S(1)}, u32[]{:S(2)}, u32[]{:S(2)}) %collective-permute-start.20) | collective-permute-done | bytes 524320 | tf_op jit(solution)/shard_map/ppermute | solution.py:436
  110.7 4.8 %prepare.1 = (bf16[5,1024,128]{2,1,0:T(8,128)(2,1)S(1)}, bf16[5,1024,128]{2,1,0:T(8,128)(2,1)S(1)}, bf16[5,1024,256]{2,1,0:T(8,128)(2,1)S(1)}, bf16[5,1024,256]{2,1,0:T(8,128)(2,1)S(1)}) custom-call(f32[8,3,64,128]{3,2,1,0:T(8,128)S(1)} %collective-permute-done.8.refs_0_, f32[8,2,64,128]{3,2,1,0:T(8,128)S(1)} %collective-permute-done.16.refs_1_, ...), custom_call_target="tpu_custom_call" | custom-call | tf_op jit(solution)/shard_map/prepare/pallas_call | solution.py:323
  115.5 1.5 copy-done.2
  117.1 1.6 copy-done.3
  118.7 1.1 copy-done.4
  119.8 1.1 copy-done.5
  120.9 9.3 %all-gather.3.cloned.1.call-done = f32[40,8,32,128]{3,2,1,0:T(8,128)} async-done(((f32[5,8,32,128]{3,2,1,0:T(8,128)}), f32[40,8,32,128]{3,2,1,0:T(8,128)}) %all-gather.3.cloned.1.call-update) | async-done | bytes 5242896 | tf_op jit(solution)/shard_map/all_gather | solution.py:474
  130.2 5.2 %zeta_lines.3 = (f32[5,128,128]{2,1,0:T(8,128)}, f32[5,128,128]{2,1,0:T(8,128)}) custom-call(f32[8,5,8,32,128]{4,3,2,1,0:T(8,128)} %bitcast.1, bf16[5,1024,128]{2,1,0:T(8,128)(2,1)} %copy-done.4, bf16[5,1024,128]{2,1,0:T(8,128)(2,1)} %copy-done.5), custom_call_target="tpu_custom_call" | custom-call | tf_op jit(solution)/shard_map/zeta_lines/pallas_call | solution.py:361
  135.4 0.9 collective-permute-start.27
  136.3 2.4 %collective-permute-start.23 = (f32[5,128,128]{2,1,0:T(8,128)}, f32[5,128,128]{2,1,0:T(8,128)S(1)}, u32[]{:S(2)}, u32[]{:S(2)}) collective-permute-start(f32[5,128,128]{2,1,0:T(8,128)} %get-tuple-element.81), channel_id=1, source_target_pairs={{0,1},{1,2},{2,3},{3,0},{4,5},{5,6},{6,7},{7,4},{8,9},{9,10},{10,1... | collective-permute-start | bytes 983048 | tf_op jit(solution)/shard_map/ppermute | solution.py:432
  138.7 7.3 %zeta_lines.2 = (f32[5,128,128]{2,1,0:T(8,128)}, f32[5,128,128]{2,1,0:T(8,128)}, f32[5,128,128]{2,1,0:T(8,128)}, f32[5,128,128]{2,1,0:T(8,128)}) custom-call(f32[8,5,8,32,128]{4,3,2,1,0:T(8,128)} %bitcast.2, bf16[5,1024,256]{2,1,0:T(8,128)(2,1)} %copy-done.2, bf16[5,1024,256]{2,1,0:T(8,128)(2,1)} %copy-done.3), custom_call_target="tpu_custom_call" | custom-call | tf_op jit(solution)/shard_map/zeta_lines/pallas_call | solution.py:361
  146.1 2.0 %collective-permute-start.26 = (f32[5,128,128]{2,1,0:T(8,128)}, f32[5,128,128]{2,1,0:T(8,128)S(1)}, u32[]{:S(2)}, u32[]{:S(2)}) collective-permute-start(f32[5,128,128]{2,1,0:T(8,128)} %get-tuple-element.73), channel_id=1, source_target_pairs={{0,3},{1,0},{2,1},{3,2},{4,7},{5,4},{6,5},{7,6},{8,11},{9,8},{10,9... | collective-permute-start | bytes 983048 | tf_op jit(solution)/shard_map/ppermute | solution.py:432
  148.1 1.0 add.7
  149.2 1.0 add.6
  150.2 3.3 %collective-permute-start.24 = (f32[5,128,128]{2,1,0:T(8,128)S(1)}, f32[5,128,128]{2,1,0:T(8,128)S(1)}, u32[]{:S(2)}, u32[]{:S(2)}) collective-permute-start(f32[5,128,128]{2,1,0:T(8,128)S(1)} %add.6), channel_id=1, source_target_pairs={{0,1},{1,2},{2,3},{3,0},{4,5},{5,6},{6,7},{7,4},{8,9},{9,10},{10,1... | collective-permute-start | bytes 983048 | tf_op jit(solution)/shard_map/ppermute | solution.py:432
  153.5 4.0 %copy-done = f32[5,128,4096]{2,1,0:T(8,128)S(1)} copy-done((f32[5,128,4096]{2,1,0:T(8,128)S(1)}, f32[5,128,4096]{2,1,0:T(8,128)}, u32[]{:S(2)}) %copy-start) | copy-done | bytes 10485784
  157.5 3.4 %own_lines.1 = (f32[5,128,128]{2,1,0:T(8,128)S(1)}, f32[5,128,128]{2,1,0:T(8,128)S(1)}) custom-call(f32[8,5,8,32,128]{4,3,2,1,0:T(8,128)S(1)} %bitcast.5, f32[5,128,4096]{2,1,0:T(8,128)S(1)} %copy-done), custom_call_target="tpu_custom_call" | custom-call | tf_op jit(solution)/shard_map/own_lines/pallas_call | solution.py:388
  161.0 2.8 %collective-permute-done.28.high1 = f32[5,128,128]{2,1,0:T(8,128)S(1)} collective-permute-done((f32[5,128,128]{2,1,0:T(8,128)S(1)}, f32[5,128,128]{2,1,0:T(8,128)S(1)}, u32[]{:S(2)}, u32[]{:S(2)}) %collective-permute-start.28) | collective-permute-done | bytes 327712 | tf_op jit(solution)/shard_map/ppermute | solution.py:432
  163.7 2.0 %final.1 = f32[5,8,32,128]{3,2,1,0:T(8,128)} custom-call(f32[4,5,5]{2,1,0:T(8,128)S(1)} %copy.14.t_ref, f32[5,8,32,128]{3,2,1,0:T(8,128)S(1)} %copy-done.1, f32[5,128,128]{2,1,0:T(8,128)S(1)} %get-tuple-element.76.own0, f32[5,128,128]{2,1,0:T(8,128)S(1)} %get-tuple-element.77.own1, f32[5,128,128]{2,1,0:T(8,128)S(1)} %collective-permute-done.24.low0, ...), custom_call_target="tpu_custom_call" | custom-call | tf_op jit(solution)/shard_map/final/pallas_call | solution.py:416
  (61 shorter events, 1.2 us)
Async XLA Ops:
  7.2 123.1 %all-gather.3.cloned.1.call-start = ((), (), s32[]{:S(2)}) async-start(), calls=%async_computation | async-start | bytes 5898240 | tf_op jit(solution)/shard_map/all_gather | solution.py:474
  9.2 15.4 %collective-permute-start = (f32[5,2,32,128]{3,2,1,0:T(8,128)}, f32[5,2,32,128]{3,2,1,0:T(8,128)S(1)}, u32[]{:S(2)}, u32[]{:S(2)}) collective-permute-start(f32[5,2,32,128]{3,2,1,0:T(8,128)} %get-tuple-element.43), channel_id=1, source_target_pairs={{0,64},{64,128},{128,192},{1,65},{65,129},{129,193},{2,66},{66,130... | collective-permute-start | bytes 491528 | tf_op jit(solution)/shard_map/ppermute | solution.py:442
  12.6 13.3 %collective-permute-start.1 = (f32[5,2,32,128]{3,2,1,0:T(8,128)}, f32[5,2,32,128]{3,2,1,0:T(8,128)S(1)}, u32[]{:S(2)}, u32[]{:S(2)}) collective-permute-start(f32[5,2,32,128]{3,2,1,0:T(8,128)} %get-tuple-element.46), channel_id=1, source_target_pairs={{64,0},{128,64},{192,128},{65,1},{129,65},{193,129},{66,2},{130,66... | collective-permute-start | bytes 491528 | tf_op jit(solution)/shard_map/ppermute | solution.py:442
  13.9 12.0 %collective-permute-start.2 = (f32[5,8,8,128]{3,2,1,0:T(8,128)}, f32[5,8,8,128]{3,2,1,0:T(8,128)S(1)}, u32[]{:S(2)}, u32[]{:S(2)}) collective-permute-start(f32[5,8,8,128]{3,2,1,0:T(8,128)} %get-tuple-element.47), channel_id=1, source_target_pairs={{0,32},{32,0},{1,33},{33,1},{2,34},{34,2},{3,35},{35,3},{4,36},{36... | collective-permute-start | bytes 491528 | tf_op jit(solution)/shard_map/ppermute | solution.py:436
  14.0 10.6 %collective-permute-start.3 = (f32[8,1280]{1,0:T(8,128)}, f32[8,1280]{1,0:T(8,128)S(1)}, u32[]{:S(2)}, u32[]{:S(2)}) collective-permute-start(f32[8,1280]{1,0:T(8,128)} %get-tuple-element.48), channel_id=1, source_target_pairs={{0,1},{1,2},{2,3},{3,4},{4,5},{5,6},{6,7},{7,8},{8,9},{9,10},{10,1... | collective-permute-start | bytes 122888 | tf_op jit(solution)/shard_map/ppermute | solution.py:442
  17.5 7.1 %copy-start.11 = (f32[4,5,5]{2,0,1:T(4,128)S(1)}, f32[4,5,5]{2,0,1:T(4,128)}, u32[]{:S(2)}) copy-start(f32[4,5,5]{2,0,1:T(4,128)} %param.12) | copy-start | bytes 1204
  17.5 8.4 %copy-start.1 = (f32[5,8,32,128]{3,2,1,0:T(8,128)S(1)}, f32[5,8,32,128]{3,2,1,0:T(8,128)}, u32[]{:S(2)}) copy-start(f32[5,8,32,128]{3,2,1,0:T(8,128)} %state.5) | copy-start | bytes 1966084
  17.5 8.4 %copy-start.6 = (f32[8,32,128]{2,1,0:T(8,128)S(1)}, f32[8,32,128]{2,1,0:T(8,128)}, u32[]{:S(2)}) copy-start(f32[8,32,128]{2,1,0:T(8,128)} %radius_hbm.1) | copy-start | bytes 393220
  17.5 8.4 %copy-start.7 = (s32[8,32,128]{2,1,0:T(8,128)S(1)}, s32[8,32,128]{2,1,0:T(8,128)}, u32[]{:S(2)}) copy-start(s32[8,32,128]{2,1,0:T(8,128)} %iblank_hbm.1) | copy-start | bytes 393220
  17.5 8.4 %copy-start.9 = (f32[5,8,32]{2,1,0:T(8,128)S(1)}, f32[5,8,32]{2,1,0:T(8,128)}, u32[]{:S(2)}) copy-start(f32[5,8,32]{2,1,0:T(8,128)} %inv_xi_hbm.1) | copy-start | bytes 15364
  17.6 8.4 %copy-start.10 = (f32[3,5]{1,0:T(4,128)S(1)}, f32[3,5]{1,0:T(4,128)}, u32[]{:S(2)}) copy-start(f32[3,5]{1,0:T(4,128)} %speeds.1) | copy-start | bytes 184
  17.6 8.3 %collective-permute-start.4 = (f32[8,1280]{1,0:T(8,128)}, f32[8,1280]{1,0:T(8,128)S(1)}, u32[]{:S(2)}, u32[]{:S(2)}) collective-permute-start(f32[8,1280]{1,0:T(8,128)} %get-tuple-element.49), channel_id=1, source_target_pairs={{1,0},{2,1},{3,2},{4,3},{5,4},{6,5},{7,6},{8,7},{9,8},{10,9},{11,1... | collective-permute-start | bytes 122888 | tf_op jit(solution)/shard_map/ppermute | solution.py:442
  24.6 5.2 %copy-start.13 = (f32[8,3,64,128]{3,2,1,0:T(8,128)S(1)}, f32[8,3,64,128]{3,2,1,0:T(8,128)}, u32[]{:S(2)}) copy-start(f32[8,3,64,128]{3,2,1,0:T(8,128)} %get-tuple-element.56) | copy-start | bytes 2359300
  24.6 33.2 %copy-start.8 = (f32[5,32,64]{2,1,0:T(8,128)S(1)}, f32[5,32,64]{2,1,0:T(8,128)}, u32[]{:S(2)}) copy-start(f32[5,32,64]{2,1,0:T(8,128)} %inv_eta.1) | copy-start | bytes 122884
  29.8 26.9 %collective-permute-start.8 = (f32[8,3,64,128]{3,2,1,0:T(8,128)S(1)}, f32[8,3,64,128]{3,2,1,0:T(8,128)S(1)}, u32[]{:S(2)}, u32[]{:S(2)}) collective-permute-start(f32[8,3,64,128]{3,2,1,0:T(8,128)S(1)} %copy-done.13), channel_id=1, source_target_pairs={{0,2},{1,3},{2,0},{3,1},{4,6},{5,7},{6,4},{7,5},{8,10},{9,11},{10,... | collective-permute-start | bytes 2359304 | tf_op jit(solution)/shard_map/ppermute | solution.py:432
  29.9 9.8 %collective-permute-start.5 = (f32[5,9,8,128]{3,2,1,0:T(8,128)S(1)}, f32[5,9,8,128]{3,2,1,0:T(8,128)S(1)}, u32[]{:S(2)}, u32[]{:S(2)}) collective-permute-start(f32[5,9,8,128]{3,2,1,0:T(8,128)S(1)} %get-tuple-element.52), channel_id=1, source_target_pairs={{0,128},{64,192},{128,0},{192,64},{1,129},{65,193},{129,1},{193,65... | collective-permute-start | bytes 552968 | tf_op jit(solution)/shard_map/ppermute | solution.py:427
  34.2 8.3 %collective-permute-start.6 = (f32[5,9,8,128]{3,2,1,0:T(8,128)S(1)}, f32[5,9,8,128]{3,2,1,0:T(8,128)S(1)}, u32[]{:S(2)}, u32[]{:S(2)}) collective-permute-start(f32[5,9,8,128]{3,2,1,0:T(8,128)S(1)} %get-tuple-element.53), channel_id=1, source_target_pairs={{0,64},{64,128},{128,192},{192,0},{1,65},{65,129},{129,193},{193,1... | collective-permute-start | bytes 552968 | tf_op jit(solution)/shard_map/ppermute | solution.py:427
  34.8 8.0 %collective-permute-start.7 = (f32[5,9,8,128]{3,2,1,0:T(8,128)S(1)}, f32[5,9,8,128]{3,2,1,0:T(8,128)S(1)}, u32[]{:S(2)}, u32[]{:S(2)}) collective-permute-start(f32[5,9,8,128]{3,2,1,0:T(8,128)S(1)} %get-tuple-element.54), channel_id=1, source_target_pairs={{0,192},{64,0},{128,64},{192,128},{1,193},{65,1},{129,65},{193,129... | collective-permute-start | bytes 552968 | tf_op jit(solution)/shard_map/ppermute | solution.py:427
  46.1 7.9 %collective-permute-start.9 = (f32[5,8,8,128]{3,2,1,0:T(8,128)S(1)}, f32[5,8,8,128]{3,2,1,0:T(8,128)S(1)}, u32[]{:S(2)}, u32[]{:S(2)}) collective-permute-start(f32[5,8,8,128]{3,2,1,0:T(8,128)S(1)} %get-tuple-element.58), channel_id=1, source_target_pairs={{0,128},{64,192},{128,0},{192,64},{1,129},{65,193},{129,1},{193,65... | collective-permute-start | bytes 491528 | tf_op jit(solution)/shard_map/ppermute | solution.py:427
  48.2 8.0 %collective-permute-start.10 = (f32[5,8,8,128]{3,2,1,0:T(8,128)S(1)}, f32[5,8,8,128]{3,2,1,0:T(8,128)S(1)}, u32[]{:S(2)}, u32[]{:S(2)}) collective-permute-start(f32[5,8,8,128]{3,2,1,0:T(8,128)S(1)} %get-tuple-element.59), channel_id=1, source_target_pairs={{0,64},{64,128},{128,192},{192,0},{1,65},{65,129},{129,193},{193,1... | collective-permute-start | bytes 491528 | tf_op jit(solution)/shard_map/ppermute | solution.py:427
  49.8 6.6 %collective-permute-start.11 = (f32[5,8,8,128]{3,2,1,0:T(8,128)S(1)}, f32[5,8,8,128]{3,2,1,0:T(8,128)S(1)}, u32[]{:S(2)}, u32[]{:S(2)}) collective-permute-start(f32[5,8,8,128]{3,2,1,0:T(8,128)S(1)} %get-tuple-element.60), channel_id=1, source_target_pairs={{0,192},{64,0},{128,64},{192,128},{1,193},{65,1},{129,65},{193,129... | collective-permute-start | bytes 491528 | tf_op jit(solution)/shard_map/ppermute | solution.py:427
  51.5 9.3 %copy-start.12 = (f32[8,5,64,128]{3,2,1,0:T(8,128)S(1)}, f32[8,5,64,128]{3,2,1,0:T(8,128)}, u32[]{:S(2)}) copy-start(f32[8,5,64,128]{3,2,1,0:T(8,128)} %get-tuple-element.64) | copy-start | bytes 3932164
  51.5 41.9 %copy-start.14 = (f32[8,2,64,128]{3,2,1,0:T(8,128)S(1)}, f32[8,2,64,128]{3,2,1,0:T(8,128)}, u32[]{:S(2)}) copy-start(f32[8,2,64,128]{3,2,1,0:T(8,128)} %get-tuple-element.62) | copy-start | bytes 1572868
  51.5 5.2 %collective-permute-start.12 = (f32[5,8,8,128]{3,2,1,0:T(8,128)S(1)}, f32[5,8,8,128]{3,2,1,0:T(8,128)S(1)}, u32[]{:S(2)}, u32[]{:S(2)}) collective-permute-start(f32[5,8,8,128]{3,2,1,0:T(8,128)S(1)} %get-tuple-element.57.p0), channel_id=1, source_target_pairs={{0,32},{32,0},{1,33},{33,1},{2,34},{34,2},{3,35},{35,3},{4,36},{36... | collective-permute-start | bytes 491528 | tf_op jit(solution)/shard_map/ppermute | solution.py:436
  54.0 2.7 %collective-permute-start.13 = (f32[5,8,8,128]{3,2,1,0:T(8,128)S(1)}, f32[5,8,8,128]{3,2,1,0:T(8,128)S(1)}, u32[]{:S(2)}, u32[]{:S(2)}) collective-permute-start(f32[5,8,8,128]{3,2,1,0:T(8,128)S(1)} %collective-permute-done.9.p1), channel_id=1, source_target_pairs={{0,32},{32,0},{1,33},{33,1},{2,34},{34,2},{3,35},{35,3},{4,36},{36... | collective-permute-start | bytes 491528 | tf_op jit(solution)/shard_map/ppermute | solution.py:436
  56.2 1.4 collective-permute-start.14
  56.4 1.4 collective-permute-start.15
  60.4 32.5 %collective-permute-start.18 = (f32[8,5,64,128]{3,2,1,0:T(8,128)}, f32[8,5,64,128]{3,2,1,0:T(8,128)S(1)}, u32[]{:S(2)}, u32[]{:S(2)}) collective-permute-start(f32[8,5,64,128]{3,2,1,0:T(8,128)} %get-tuple-element.66), channel_id=1, source_target_pairs={{0,3},{1,0},{2,1},{3,2},{4,7},{5,4},{6,5},{7,6},{8,11},{9,8},{10,9... | collective-permute-start | bytes 3932168 | tf_op jit(solution)/shard_map/ppermute | solution.py:432
  60.8 32.0 %collective-permute-start.17 = (f32[8,5,64,128]{3,2,1,0:T(8,128)S(1)}, f32[8,5,64,128]{3,2,1,0:T(8,128)S(1)}, u32[]{:S(2)}, u32[]{:S(2)}) collective-permute-start(f32[8,5,64,128]{3,2,1,0:T(8,128)S(1)} %copy-done.12), channel_id=1, source_target_pairs={{0,1},{1,2},{2,3},{3,0},{4,5},{5,6},{6,7},{7,4},{8,9},{9,10},{10,1... | collective-permute-start | bytes 3932168 | tf_op jit(solution)/shard_map/ppermute | solution.py:432
  92.9 17.9 %collective-permute-start.22 = (f32[8,5,64,128]{3,2,1,0:T(8,128)S(1)}, f32[8,5,64,128]{3,2,1,0:T(8,128)S(1)}, u32[]{:S(2)}, u32[]{:S(2)}) collective-permute-start(f32[8,5,64,128]{3,2,1,0:T(8,128)S(1)} %collective-permute-done.18.refs_3_), channel_id=1, source_target_pairs={{0,32},{32,0},{1,33},{33,1},{2,34},{34,2},{3,35},{35,3},{4,36},{36... | collective-permute-start | bytes 3932168 | tf_op jit(solution)/shard_map/ppermute | solution.py:436
  92.9 17.9 %collective-permute-start.21 = (f32[8,5,64,128]{3,2,1,0:T(8,128)S(1)}, f32[8,5,64,128]{3,2,1,0:T(8,128)S(1)}, u32[]{:S(2)}, u32[]{:S(2)}) collective-permute-start(f32[8,5,64,128]{3,2,1,0:T(8,128)S(1)} %collective-permute-done.17.refs_2_), channel_id=1, source_target_pairs={{0,32},{32,0},{1,33},{33,1},{2,34},{34,2},{3,35},{35,3},{4,36},{36... | collective-permute-start | bytes 3932168 | tf_op jit(solution)/shard_map/ppermute | solution.py:436
  93.4 15.4 %collective-permute-start.16 = (f32[8,2,64,128]{3,2,1,0:T(8,128)S(1)}, f32[8,2,64,128]{3,2,1,0:T(8,128)S(1)}, u32[]{:S(2)}, u32[]{:S(2)}) collective-permute-start(f32[8,2,64,128]{3,2,1,0:T(8,128)S(1)} %copy-done.14), channel_id=1, source_target_pairs={{0,2},{1,3},{2,0},{3,1},{4,6},{5,7},{6,4},{7,5},{8,10},{9,11},{10,... | collective-permute-start | bytes 1572872 | tf_op jit(solution)/shard_map/ppermute | solution.py:432
  94.9 13.9 %collective-permute-start.19 = (f32[8,3,64,128]{3,2,1,0:T(8,128)S(1)}, f32[8,3,64,128]{3,2,1,0:T(8,128)S(1)}, u32[]{:S(2)}, u32[]{:S(2)}) collective-permute-start(f32[8,3,64,128]{3,2,1,0:T(8,128)S(1)} %collective-permute-done.8.refs_0_), channel_id=1, source_target_pairs={{0,32},{32,0},{1,33},{33,1},{2,34},{34,2},{3,35},{35,3},{4,36},{36... | collective-permute-start | bytes 2359304 | tf_op jit(solution)/shard_map/ppermute | solution.py:436
  108.8 1.9 %collective-permute-start.20 = (f32[8,2,64,128]{3,2,1,0:T(8,128)S(1)}, f32[8,2,64,128]{3,2,1,0:T(8,128)S(1)}, u32[]{:S(2)}, u32[]{:S(2)}) collective-permute-start(f32[8,2,64,128]{3,2,1,0:T(8,128)S(1)} %collective-permute-done.16.refs_1_), channel_id=1, source_target_pairs={{0,32},{32,0},{1,33},{33,1},{2,34},{34,2},{3,35},{35,3},{4,36},{36... | collective-permute-start | bytes 1572872 | tf_op jit(solution)/shard_map/ppermute | solution.py:436
  115.5 1.6 copy-start.2
  117.1 1.6 copy-start.3
  118.7 1.1 copy-start.4
  119.8 1.1 copy-start.5
  135.4 12.7 %collective-permute-start.27 = (f32[5,128,128]{2,1,0:T(8,128)}, f32[5,128,128]{2,1,0:T(8,128)S(1)}, u32[]{:S(2)}, u32[]{:S(2)}) collective-permute-start(f32[5,128,128]{2,1,0:T(8,128)} %get-tuple-element.83), channel_id=1, source_target_pairs={{0,3},{1,0},{2,1},{3,2},{4,7},{5,4},{6,5},{7,6},{8,11},{9,8},{10,9... | collective-permute-start | bytes 983048 | tf_op jit(solution)/shard_map/ppermute | solution.py:432
  136.3 12.9 %collective-permute-start.23 = (f32[5,128,128]{2,1,0:T(8,128)}, f32[5,128,128]{2,1,0:T(8,128)S(1)}, u32[]{:S(2)}, u32[]{:S(2)}) collective-permute-start(f32[5,128,128]{2,1,0:T(8,128)} %get-tuple-element.81), channel_id=1, source_target_pairs={{0,1},{1,2},{2,3},{3,0},{4,5},{5,6},{6,7},{7,4},{8,9},{9,10},{10,1... | collective-permute-start | bytes 983048 | tf_op jit(solution)/shard_map/ppermute | solution.py:432
  138.7 14.8 %slice-start = ((s8[5242880]{0:T(1024)(128)(4,1)}), s8[4194304]{0:T(1024)(128)(4,1)S(1)}, s32[]{:S(2)}) async-start(s8[5242880]{0:T(1024)(128)(4,1)} %bitcast.3), calls=%async_computation.1 | async-start | bytes 8388608
  138.7 14.8 %slice-start.1 = ((s8[5242880]{0:T(1024)(128)(4,1)}), s8[1048576]{0:T(1024)(128)(4,1)S(1)}, s32[]{:S(2)}) async-start(s8[5242880]{0:T(1024)(128)(4,1)} %bitcast.3), calls=%async_computation.2 | async-start | bytes 2097152
  146.0 14.9 %collective-permute-start.25 = (f32[5,128,128]{2,1,0:T(8,128)}, f32[5,128,128]{2,1,0:T(8,128)S(1)}, u32[]{:S(2)}, u32[]{:S(2)}) collective-permute-start(f32[5,128,128]{2,1,0:T(8,128)} %get-tuple-element.74), channel_id=1, source_target_pairs={{0,1},{1,2},{2,3},{3,0},{4,5},{5,6},{6,7},{7,4},{8,9},{9,10},{10,1... | collective-permute-start | bytes 983048 | tf_op jit(solution)/shard_map/ppermute | solution.py:432
  146.1 14.9 %collective-permute-start.26 = (f32[5,128,128]{2,1,0:T(8,128)}, f32[5,128,128]{2,1,0:T(8,128)S(1)}, u32[]{:S(2)}, u32[]{:S(2)}) collective-permute-start(f32[5,128,128]{2,1,0:T(8,128)} %get-tuple-element.73), channel_id=1, source_target_pairs={{0,3},{1,0},{2,1},{3,2},{4,7},{5,4},{6,5},{7,6},{8,11},{9,8},{10,9... | collective-permute-start | bytes 983048 | tf_op jit(solution)/shard_map/ppermute | solution.py:432
  149.1 14.6 %collective-permute-start.28 = (f32[5,128,128]{2,1,0:T(8,128)S(1)}, f32[5,128,128]{2,1,0:T(8,128)S(1)}, u32[]{:S(2)}, u32[]{:S(2)}) collective-permute-start(f32[5,128,128]{2,1,0:T(8,128)S(1)} %add.7), channel_id=1, source_target_pairs={{0,3},{1,0},{2,1},{3,2},{4,7},{5,4},{6,5},{7,6},{8,11},{9,8},{10,9... | collective-permute-start | bytes 983048 | tf_op jit(solution)/shard_map/ppermute | solution.py:432
  150.2 13.5 %collective-permute-start.24 = (f32[5,128,128]{2,1,0:T(8,128)S(1)}, f32[5,128,128]{2,1,0:T(8,128)S(1)}, u32[]{:S(2)}, u32[]{:S(2)}) collective-permute-start(f32[5,128,128]{2,1,0:T(8,128)S(1)} %add.6), channel_id=1, source_target_pairs={{0,1},{1,2},{2,3},{3,0},{4,5},{5,6},{6,7},{7,4},{8,9},{9,10},{10,1... | collective-permute-start | bytes 983048 | tf_op jit(solution)/shard_map/ppermute | solution.py:432
  153.5 4.0 %copy-start = (f32[5,128,4096]{2,1,0:T(8,128)S(1)}, f32[5,128,4096]{2,1,0:T(8,128)}, u32[]{:S(2)}) copy-start(f32[5,128,4096]{2,1,0:T(8,128)} %inv.2) | copy-start | bytes 31457284
Sparse Core Ops, SparseCore 0:
  60.5 69.6 all-gather.2
